TPU v7x, 32 devices: a whole 2x2x4 slice. The times are simulated.
32 devices in a mesh: line: 16 (over z, y, core), centroid: 2 (over x).
Axes of the slice: x: 2, y: 2, z: 4, core: 2. Of those that a mesh axis runs over, the one named last changes fastest.
Arguments:
- line_blocks: bfloat16 [256, 128, 768], P('line', 'centroid'), may hold values from -6 to 6
- line_counts: int32 [16], P('line'), may hold values from 0 to 2048, as said below
- destinations: int32 [256], P('line'), may hold values from 0 to 127, as said below
- centroids: bfloat16 [2048, 768], P(('centroid', 'line')), may hold values from -6 to 6
Outputs:
- nearest: float32 [128, 128], P('line', 'centroid')
- runner_up: float32 [128, 128], P('line', 'centroid')
Inputs may be any that keep to these rules, and one draw needn't show every extreme that they name: `line_counts`: each count is a multiple of 128; the counts add up to 16384. `destinations`: among usable slots each balanced position is named exactly once, and position p is named by a slot of host p // 8 or of the host before it (host 16 - 1 before host 0). At most 8 usable slots of one host name positions of one host. Slots that are not usable hold arbitrary positions.
All inputs are finite; a program needn't handle non-finite values.
Results may differ from a plain program's by a relative error of at most 0.0003.
Values may be sent and summed in bfloat16 or wider, within the bound.
No kernel may reach another device: no remote copies, remote signals or barrier semaphores. Data moves between devices by JAX's collectives and lax.ppermute only.
A program may use at most 64 MiB of HBM per device.

v0:
```python
import jax
import jax.numpy as jnp
from jax import lax
from jax.sharding import PartitionSpec as P

BLK = 128


HUGE_DISTANCE = 3e38


def swapped(block, axis, distance):
    count = lax.axis_size(axis)
    route = []
    for low in range(count):
        high = low | 1 << distance
        if high != low and high < count:
            route += [(low, high), (high, low)]
    return lax.ppermute(block, axis, route)


def combined_all(value, axis, join):
    pieces = jax.tree.map(lambda part: lax.all_gather(part, axis), value)
    head = jax.tree.map(lambda part: part[0], pieces)
    tail = jax.tree.map(lambda part: part[1:], pieces)
    subtotal, _ = lax.scan(lambda subtotal, piece: (join(subtotal, piece), None), head, tail)
    return subtotal


def shifted(value, axis, by):
    length = lax.axis_size(axis)
    return lax.ppermute(value, axis, [(i, (i + by) % length) for i in range(length)])


def second_smallest(values, along):
    lowest = jnp.min(values, axis=along, keepdims=True)
    tie_count = jnp.sum((values == lowest).astype(jnp.int32), axis=along)
    others = jnp.min(jnp.where(values > lowest, values, HUGE_DISTANCE), axis=along)
    return jnp.where(tie_count >= 2, jnp.squeeze(lowest, along), others)


def combine(earlier, later):
    lowest = jnp.minimum(earlier[0], later[0])
    runner = jnp.minimum(jnp.minimum(jnp.maximum(earlier[0], later[0]), earlier[1]), later[1])
    return (lowest, runner)


def nearest_two(gathered):
    features = gathered.shape[2]
    line_rows = gathered.reshape(-1, features)
    wide_rows = line_rows.astype(jnp.float32)
    line_norms = jnp.sum(wide_rows * wide_rows, axis=1)

    def absorb(running, bank_piece, offset):
        products = jnp.einsum(
            "nd,kd->nk", line_rows, bank_piece, preferred_element_type=jnp.float32
        )
        wide_bank = bank_piece.astype(jnp.float32)
        bank_norms = jnp.sum(wide_bank * wide_bank, axis=1)
        distance = (line_norms[:, None] + bank_norms[None, :] - 2.0 * products) / features
        return combine(running, (jnp.min(distance, axis=1), second_smallest(distance, 1)))

    line_total = line_rows.shape[0]
    starting = (
        jnp.full((line_total,), HUGE_DISTANCE, jnp.float32),
        jnp.full((line_total,), HUGE_DISTANCE, jnp.float32),
    )
    return (starting, absorb)


def score_blocks(gathered, centroids):
    partner_lines = swapped(gathered, "line", 0)
    both_lines = jnp.concatenate([gathered, partner_lines], axis=0)
    starting, absorb = nearest_two(both_lines)
    running = absorb(starting, centroids, 0)
    held = centroids
    bit_total = lax.axis_size("line").bit_length() - 1
    for bit in range(1, bit_total):
        received = swapped(held, "line", bit)
        running = absorb(running, received, 0)
        held = jnp.concatenate([held, received], axis=0)
    own_count = gathered.shape[0] * gathered.shape[1]
    mine = (running[0][:own_count], running[1][:own_count])
    returned = swapped((running[0][own_count:], running[1][own_count:]), "line", 0)
    return combine(mine, returned)


def finish(lowest_all, runner_all):
    block_total, block_rows = lowest_all.shape
    part_count = lax.axis_size("centroid")
    sub_rows = block_rows // part_count
    merged = combined_all((lowest_all, runner_all), "centroid", combine)
    offset = lax.axis_index("centroid") * sub_rows
    lowest = lax.dynamic_slice_in_dim(merged[0], offset, sub_rows, 1)
    runner = lax.dynamic_slice_in_dim(merged[1], offset, sub_rows, 1)
    return (lowest, runner)


def shards(line_blocks, line_counts, destinations, centroids):
    host_count = lax.axis_size("line")
    host_index = lax.axis_index("line")
    slot_total, sub_rows, features = line_blocks.shape
    balanced_count = slot_total // 2
    block_rows = sub_rows * lax.axis_size("centroid")
    slot_ids = jnp.arange(slot_total, dtype=jnp.int32)
    usable = slot_ids * BLK < line_counts[0]
    place_ids = jnp.arange(balanced_count, dtype=jnp.int32)
    own_positions = host_index * balanced_count + place_ids
    next_positions = (host_index + 1) % host_count * balanced_count + place_ids
    keep_selector = (destinations[None, :] == own_positions[:, None]) & usable[None, :]
    send_selector = (destinations[None, :] == next_positions[:, None]) & usable[None, :]
    staying = jnp.einsum(
        "bs,srd->brd",
        keep_selector.astype(jnp.bfloat16),
        line_blocks,
        preferred_element_type=jnp.float32,
    ).astype(jnp.bfloat16)
    outgoing = jnp.einsum(
        "bs,srd->brd",
        send_selector.astype(jnp.bfloat16),
        line_blocks,
        preferred_element_type=jnp.float32,
    ).astype(jnp.bfloat16)
    arriving = shifted(outgoing, "line", 1)
    resident = staying + arriving
    gathered = lax.all_gather(resident, "centroid", axis=1, tiled=True)
    scored = score_blocks(gathered, centroids)
    nearest, runner_up = finish(
        scored[0].reshape(balanced_count, block_rows), scored[1].reshape(balanced_count, block_rows)
    )
    return (nearest, runner_up)


def solution(mesh):
    in_specs = (P("line", "centroid", None), P("line"), P("line"), P(("centroid", "line"), None))
    out_specs = (P("line", "centroid"), P("line", "centroid"))
    return jax.shard_map(shards, mesh=mesh, in_specs=in_specs, out_specs=out_specs, check_vma=False)
```

profile of v0, /device:TPU:0, one launch (start us, length us, event | category | flops | bytes accessed | tf_op | source)
XLA Modules:
  0.0 111.6 jit_solution(11393455755910047002)
XLA Ops:
  8.0 0.6 copy-done
  8.6 1.6 %convolution_convert_fusion = bf16[8,64,768]{2,0,1:T(8,128)(2,1)S(1)} fusion(bf16[16,64,768]{2,1,0:T(8,128)(2,1)S(1)} %copy-done, s32[16]{0:T(128)} %param.6, s32[8]{0:T(128)S(1)} %iota_add_fusion, pred[16]{0:T(512)(128)(4,1)S(1)} %multiply_compare_fusion), kind=kOutput, calls=%fused_computation.12 | convolution fusion | flops 12976384 | bytes 2359408 | tf_op jit(solution)/shard_map/bs,srd->brd/dot_general | solution.py:118
  10.2 0.5 collective-permute-start
  10.7 14.7 %collective-permute-done = bf16[8,64,768]{2,0,1:T(8,128)(2,1)S(1)} collective-permute-done((bf16[8,64,768]{2,0,1:T(8,128)(2,1)S(1)}, bf16[8,64,768]{2,0,1:T(8,128)(2,1)S(1)}, u32[]{:S(2)}, u32[]{:S(2)}) %collective-permute-start) | collective-permute-done | bytes 786464 | tf_op jit(solution)/shard_map/ppermute | solution.py:32
  25.4 1.9 %fusion.4 = bf16[8,64,768]{2,0,1:T(8,128)(2,1)} fusion(bf16[8,64,768]{2,0,1:T(8,128)(2,1)S(1)} %collective-permute-done, bf16[16,64,768]{2,1,0:T(8,128)(2,1)S(1)} %copy-done, s32[16]{0:T(128)S(1)} %copy-done.2, s32[8]{0:T(128)S(1)} %iota_add_fusion.1, pred[16]{0:T(512)(128)(4,1)S(1)} %multiply_compare_fusion), kind=kOutput, calls=%fused_computation.17 | convolution fusion | flops 13369600 | bytes 3145840 | tf_op jit(solution)/shard_map/bs,srd->brd/dot_general | solution.py:112
  27.3 26.3 %all-gather.2.cloned.1.call-done = bf16[8,128,768]{2,0,1:T(8,128)(2,1)} async-done(((bf16[8,64,768]{2,0,1:T(8,128)(2,1)}), bf16[8,128,768]{2,0,1:T(8,128)(2,1)}) %all-gather.2.cloned.1.call-update) | async-done | bytes 1572880 | tf_op jit(solution)/shard_map/all_gather | solution.py:126
  53.6 1.7 %fusion.29 = (bf16[8,128,768]{2,1,0:T(8,128)(2,1)S(1)}, bf16[16,128,768]{2,1,0:T(8,128)(2,1)S(1)}) fusion(bf16[8,128,768]{2,0,1:T(8,128)(2,1)} %all-gather.2.cloned.1.call-done), kind=kLoop, calls=%fused_computation.66 | loop fusion | bytes 4718592 | tf_op jit(solution)/shard_map/all_gather | solution.py:126
  55.5 1.5 %collective-permute-start.2 = (bf16[64,768]{1,0:T(8,128)(2,1)S(1)}, bf16[64,768]{1,0:T(8,128)(2,1)S(1)}, u32[]{:S(2)}, u32[]{:S(2)}) collective-permute-start(bf16[64,768]{1,0:T(8,128)(2,1)S(1)} %copy-done.1), channel_id=1, source_target_pairs={{0,4},{4,0},{2,6},{6,2},{8,12},{12,8},{10,14},{14,10},{16,20},{20,... | collective-permute-start | bytes 294920 | tf_op jit(solution)/shard_map/ppermute | solution.py:19
  57.0 3.7 %collective-permute-done.2 = bf16[64,768]{1,0:T(8,128)(2,1)S(1)} collective-permute-done((bf16[64,768]{1,0:T(8,128)(2,1)S(1)}, bf16[64,768]{1,0:T(8,128)(2,1)S(1)}, u32[]{:S(2)}, u32[]{:S(2)}) %collective-permute-start.2) | collective-permute-done | bytes 98336 | tf_op jit(solution)/shard_map/ppermute | solution.py:19
  60.7 1.6 %collective-permute-start.3 = (bf16[128,768]{1,0:T(8,128)(2,1)S(1)}, bf16[128,768]{1,0:T(8,128)(2,1)S(1)}, u32[]{:S(2)}, u32[]{:S(2)}) collective-permute-start(bf16[128,768]{1,0:T(8,128)(2,1)S(1)} %pad_maximum_fusion.1), channel_id=1, source_target_pairs={{0,8},{8,0},{2,10},{10,2},{4,12},{12,4},{6,14},{14,6},{16,24},{24,... | collective-permute-start | bytes 589832 | tf_op jit(solution)/shard_map/ppermute | solution.py:19
  62.3 5.0 %collective-permute-done.3 = bf16[128,768]{1,0:T(8,128)(2,1)S(1)} collective-permute-done((bf16[128,768]{1,0:T(8,128)(2,1)S(1)}, bf16[128,768]{1,0:T(8,128)(2,1)S(1)}, u32[]{:S(2)}, u32[]{:S(2)}) %collective-permute-start.3) | collective-permute-done | bytes 196640 | tf_op jit(solution)/shard_map/ppermute | solution.py:19
  67.3 2.5 %collective-permute-start.4 = (bf16[256,768]{1,0:T(8,128)(2,1)S(1)}, bf16[256,768]{1,0:T(8,128)(2,1)S(1)}, u32[]{:S(2)}, u32[]{:S(2)}) collective-permute-start(bf16[256,768]{1,0:T(8,128)(2,1)S(1)} %pad_maximum_fusion), channel_id=1, source_target_pairs={{0,16},{16,0},{2,18},{18,2},{4,20},{20,4},{6,22},{22,6},{8,24},{24... | collective-permute-start | bytes 1179656 | tf_op jit(solution)/shard_map/ppermute | solution.py:19
  70.0 0.1 multiply_reduce_fusion.2
  70.1 16.3 %collective-permute-done.4 = bf16[256,768]{1,0:T(8,128)(2,1)S(1)} collective-permute-done((bf16[256,768]{1,0:T(8,128)(2,1)S(1)}, bf16[256,768]{1,0:T(8,128)(2,1)S(1)}, u32[]{:S(2)}, u32[]{:S(2)}) %collective-permute-start.4) | collective-permute-done | bytes 393248 | tf_op jit(solution)/shard_map/ppermute | solution.py:19
  86.4 0.2 multiply_reduce_fusion.1
  86.7 0.7 multiply_reduce_fusion
  87.4 1.1 fusion.11
  88.5 1.1 fusion.9
  89.6 0.3 convert_reduce_fusion.3
  89.9 0.2 fusion.10
  90.1 1.2 %fusion.8 = (f32[2048]{0:T(1024)S(1)}, f32[2048,128]{0,1:T(8,128)S(1)}) fusion(f32[128]{0:T(128)S(1)} %multiply_reduce_fusion.2, f32[2048]{0:T(1024)S(1)} %bitcast.34, bf16[2048,768]{1,0:T(8,128)(2,1)S(1)} %bitcast.28, bf16[128,768]{1,0:T(8,128)(2,1)S(1)} %collective-permute-done.3), kind=kOutput, calls=%fused_computation.22 | convolution fusion | flops 403961856 | bytes 4407808 | tf_op jit(solution)/shard_map/nd,kd->nk/dot_general | solution.py:55
  91.2 0.3 convert_reduce_fusion.1
  91.5 0.3 fusion.7
  91.8 1.1 %fusion.3 = (f32[2048]{0:T(1024)S(1)}, f32[2048,256]{0,1:T(8,128)S(1)}) fusion(f32[256]{0:T(256)S(1)} %multiply_reduce_fusion.1, f32[2048]{0:T(1024)S(1)} %bitcast.37, bf16[2048,768]{1,0:T(8,128)(2,1)S(1)} %bitcast.29, bf16[256,768]{1,0:T(8,128)(2,1)S(1)} %collective-permute-done.4), kind=kOutput, calls=%fused_computation.16 | convolution fusion | flops 807925760 | bytes 5653504 | tf_op jit(solution)/shard_map/nd,kd->nk/dot_general | solution.py:55
  93.0 0.5 convert_reduce_fusion
  93.5 0.5 fusion
  94.1 0.5 collective-permute-start.6
  94.6 0.7 collective-permute-done.5
  95.3 0.2 collective-permute-done.6
  95.5 4.3 %all_gather.10 = f32[2,8,128]{2,1,0:T(8,128)S(1)} all-gather(f32[1,8,128]{2,1,0:T(8,128)S(1)} %get-tuple-element.26), channel_id=1, replica_groups=mesh['line'=16,'centroid'=2] {'centroid'}, dimensions={0}, use_global_device_ids=true | all-gather | bytes 12288 | tf_op jit(solution)/shard_map/all_gather | solution.py:23
  99.8 4.3 %all_gather.11 = f32[2,8,128]{2,1,0:T(8,128)S(1)} all-gather(f32[1,8,128]{2,1,0:T(8,128)S(1)} %get-tuple-element.25), channel_id=1, replica_groups=mesh['line'=16,'centroid'=2] {'centroid'}, dimensions={0}, use_global_device_ids=true | all-gather | bytes 12288 | tf_op jit(solution)/shard_map/all_gather | solution.py:23
  104.1 0.7 dynamic-slice_bitcast_fusion
  (23 shorter events, 0.7 us)
Async XLA Ops:
  7.2 1.4 %copy-start = (bf16[16,64,768]{2,1,0:T(8,128)(2,1)S(1)}, bf16[16,64,768]{2,1,0:T(8,128)(2,1)}, u32[]{:S(2)}) copy-start(bf16[16,64,768]{2,1,0:T(8,128)(2,1)} %param.4) | copy-start | bytes 4718596
  7.2 18.2 %copy-start.2 = (s32[16]{0:T(128)S(1)}, s32[16]{0:T(128)}, u32[]{:S(2)}) copy-start(s32[16]{0:T(128)} %param.6) | copy-start | bytes 196
  7.2 46.5 %all-gather.2.cloned.1.call-start = ((), (), s32[]{:S(2)}) async-start(), calls=%async_computation | async-start | bytes 2359296 | tf_op jit(solution)/shard_map/all_gather | solution.py:126
  10.2 15.2 %collective-permute-start = (bf16[8,64,768]{2,0,1:T(8,128)(2,1)S(1)}, bf16[8,64,768]{2,0,1:T(8,128)(2,1)S(1)}, u32[]{:S(2)}, u32[]{:S(2)}) collective-permute-start(bf16[8,64,768]{2,0,1:T(8,128)(2,1)S(1)} %convolution_convert_fusion), channel_id=1, source_target_pairs={{0,2},{2,4},{4,6},{6,8},{8,10},{10,12},{12,14},{14,16},{16,18},{18... | collective-permute-start | bytes 2359304 | tf_op jit(solution)/shard_map/ppermute | solution.py:32
  27.3 28.2 %copy-start.1 = (bf16[64,768]{1,0:T(8,128)(2,1)S(1)}, bf16[64,768]{1,0:T(8,128)(2,1)}, u32[]{:S(2)}) copy-start(bf16[64,768]{1,0:T(8,128)(2,1)} %param.7) | copy-start | bytes 294916
  55.4 31.2 %collective-permute-start.1 = (bf16[8,128,768]{2,1,0:T(8,128)(2,1)S(1)}, bf16[8,128,768]{2,1,0:T(8,128)(2,1)S(1)}, u32[]{:S(2)}, u32[]{:S(2)}) collective-permute-start(bf16[8,128,768]{2,1,0:T(8,128)(2,1)S(1)} %get-tuple-element.21), channel_id=1, source_target_pairs={{0,2},{2,0},{4,6},{6,4},{8,10},{10,8},{12,14},{14,12},{16,18},{18,... | collective-permute-start | bytes 4718600 | tf_op jit(solution)/shard_map/ppermute | solution.py:19
  55.5 5.2 %collective-permute-start.2 = (bf16[64,768]{1,0:T(8,128)(2,1)S(1)}, bf16[64,768]{1,0:T(8,128)(2,1)S(1)}, u32[]{:S(2)}, u32[]{:S(2)}) collective-permute-start(bf16[64,768]{1,0:T(8,128)(2,1)S(1)} %copy-done.1), channel_id=1, source_target_pairs={{0,4},{4,0},{2,6},{6,2},{8,12},{12,8},{10,14},{14,10},{16,20},{20,... | collective-permute-start | bytes 294920 | tf_op jit(solution)/shard_map/ppermute | solution.py:19
  60.7 6.5 %collective-permute-start.3 = (bf16[128,768]{1,0:T(8,128)(2,1)S(1)}, bf16[128,768]{1,0:T(8,128)(2,1)S(1)}, u32[]{:S(2)}, u32[]{:S(2)}) collective-permute-start(bf16[128,768]{1,0:T(8,128)(2,1)S(1)} %pad_maximum_fusion.1), channel_id=1, source_target_pairs={{0,8},{8,0},{2,10},{10,2},{4,12},{12,4},{6,14},{14,6},{16,24},{24,... | collective-permute-start | bytes 589832 | tf_op jit(solution)/shard_map/ppermute | solution.py:19
  67.3 19.2 %collective-permute-start.4 = (bf16[256,768]{1,0:T(8,128)(2,1)S(1)}, bf16[256,768]{1,0:T(8,128)(2,1)S(1)}, u32[]{:S(2)}, u32[]{:S(2)}) collective-permute-start(bf16[256,768]{1,0:T(8,128)(2,1)S(1)} %pad_maximum_fusion), channel_id=1, source_target_pairs={{0,16},{16,0},{2,18},{18,2},{4,20},{20,4},{6,22},{22,6},{8,24},{24... | collective-permute-start | bytes 1179656 | tf_op jit(solution)/shard_map/ppermute | solution.py:19
  94.1 1.2 %collective-permute-start.5 = (f32[1024]{0:T(1024)S(1)}, f32[1024]{0:T(1024)S(1)}, u32[]{:S(2)}, u32[]{:S(2)}) collective-permute-start(f32[1024]{0:T(1024)S(1)} %slice.33), channel_id=1, source_target_pairs={{0,2},{2,0},{4,6},{6,4},{8,10},{10,8},{12,14},{14,12},{16,18},{18,... | collective-permute-start | bytes 12296 | tf_op jit(solution)/shard_map/ppermute | solution.py:19
  94.1 1.3 %collective-permute-start.6 = (f32[1024]{0:T(1024)S(1)}, f32[1024]{0:T(1024)S(1)}, u32[]{:S(2)}, u32[]{:S(2)}) collective-permute-start(f32[1024]{0:T(1024)S(1)} %slice.37), channel_id=1, source_target_pairs={{0,2},{2,0},{4,6},{6,4},{8,10},{10,8},{12,14},{14,12},{16,18},{18,... | collective-permute-start | bytes 12296 | tf_op jit(solution)/shard_map/ppermute | solution.py:19
Sparse Core Ops, SparseCore 0:
  27.4 26.1 all-gather.1
where the time goes:
time: 112 us
  waiting for transfers between devices  66.8 us (60%)
  between operations  15 us (13%)
  blocking collectives  8.65 us (8%)
  matrix products  7.97 us (7%)
  starting transfers between devices  6.74 us (6%)
  other arithmetic  3.36 us (3%)
  local copies, waits for them, and re-layouts  3.11 us (3%)
    all_gather x1, waiting for transfers between devices, shards(): gathered = lax.all_gather(resident, 'centroid', axis=1, tiled=True)  26.3 us
    ppermute x6, waiting for transfers between devices, swapped(): return lax.ppermute(block, axis, route)  25.8 us
    ppermute x1, waiting for transfers between devices, shifted(): lax.ppermute(value, axis, [(i, (i + by) % length) for i in range(length)])  14.7 us
    all_gather x2, blocking collectives, combined_all(): pieces = jax.tree.map(lambda part: lax.all_gather(part, axis), value)  8.65 us
    ppermute x6, starting transfers between devices, swapped(): return lax.ppermute(block, axis, route)  6.19 us
    dot_general x4, matrix products, absorb(): jnp.einsum('nd,kd->nk', line_rows, bank_piece, preferred_element_type=jnp...  4.48 us
  transfers between devices with their start and end apart: 8, of which 7 were waited for; matrix products, arithmetic and copies ran while one was open for 1% of the time, Pallas kernels for 0%

commit v1 on v0

v1 whole, which is shorter than its diff:
```python
import functools

import jax
import jax.numpy as jnp
from jax import lax
from jax.experimental import pallas as pl
from jax.experimental.pallas import tpu as pltpu
from jax.sharding import PartitionSpec as P

HUGE_DISTANCE = 3e38
AXES = ("line", "centroid")
GROUP_LINES = 256
BANK_TILE = 512
SUBLANES = 8
VMEM_LIMIT = 24 * 2**20


def moved(value, target):
    hosts, columns = (lax.axis_size(axis) for axis in AXES)
    route = []
    for host in range(hosts):
        for column in range(columns):
            to = target(host, column)
            if to is not None:
                route.append((host * columns + column, to[0] % hosts * columns + to[1]))
    return lax.ppermute(value, AXES, route)


def across(axis, bit):
    if axis == "line":
        return lambda host, column: (host ^ 1 << bit, column)
    return lambda host, column: (host, column ^ 1 << bit)


def by_parity(even, odd):
    return lambda host, column: (odd if host & 1 else even)(host, column)


def fold(first, second, value):
    second = jnp.minimum(second, jnp.maximum(first, value))
    return jnp.minimum(first, value), second


def line_groups(lines, slots):
    per_slot = lines // slots
    return max(1, min(slots, GROUP_LINES // per_slot))


def norm_kernel(own_ref, partner_ref, norms_ref):
    lines, features = own_ref.shape
    ones = jnp.ones((SUBLANES, features), jnp.bfloat16)
    step = min(lines, GROUP_LINES)
    for part, ref in enumerate((own_ref, partner_ref)):
        for at in range(0, lines, step):
            wide = ref[at : at + step, :].astype(jnp.float32)
            square = wide * wide
            high = square.astype(jnp.bfloat16)
            low = (square - high.astype(jnp.float32)).astype(jnp.bfloat16)
            total = sum(
                lax.dot_general(
                    ones, half, (((1,), (1,)), ((), ())), preferred_element_type=jnp.float32
                )
                for half in (high, low)
            )
            norms_ref[:, part * lines + at : part * lines + at + step] = total


def line_norms(own, partner):
    lines, features = own.shape
    return pl.pallas_call(
        norm_kernel,
        out_shape=jax.ShapeDtypeStruct((SUBLANES, 2 * lines), jnp.float32),
        compiler_params=pltpu.CompilerParams(vmem_limit_bytes=VMEM_LIMIT),
        cost_estimate=pl.CostEstimate(
            flops=4 * SUBLANES * lines * features,
            bytes_accessed=4 * lines * features,
            transcendentals=0,
        ),
        name="line_norms",
    )(own, partner)


def absorb_kernel(slots, block_rows, counts_ref, bank_ref, own_ref, partner_ref, *rest):
    first_in, second_in, first_ref, second_ref = rest
    lines = own_ref.shape[0]
    per_slot = lines // slots
    group = line_groups(lines, slots)
    step = group * per_slot

    @pl.when(pl.program_id(0) == 0)
    def start():
        first_ref[...] = first_in[...]
        second_ref[...] = second_in[...]

    wide = bank_ref[...].astype(jnp.float32)
    bank_norms = jnp.sum(wide * wide, axis=1, keepdims=True)
    scaled = bank_ref[...] * jnp.array(-2, jnp.bfloat16)
    for part, ref in enumerate((own_ref, partner_ref)):
        for index in range(slots // group):

            @pl.when(index * group * block_rows < counts_ref[part])
            def work(part=part, ref=ref, index=index):
                products = lax.dot_general(
                    scaled,
                    ref[index * step : (index + 1) * step, :],
                    (((1,), (1,)), ((), ())),
                    preferred_element_type=jnp.float32,
                )
                distance = products + bank_norms
                at = slice(part * lines + index * step, part * lines + (index + 1) * step)
                first, second = first_ref[:, at], second_ref[:, at]
                for row in range(0, distance.shape[0], SUBLANES):
                    first, second = fold(first, second, distance[row : row + SUBLANES])
                first_ref[:, at] = first
                second_ref[:, at] = second


def absorb(running, bank, counts, own, partner, slots, block_rows):
    lines, features = own.shape
    centroids = bank.shape[0]
    tile = min(centroids, BANK_TILE)
    whole = lambda index: (0, 0)
    lines_spec = pl.BlockSpec((lines, features), whole)
    state_spec = pl.BlockSpec((SUBLANES, 2 * lines), whole)
    state = jax.ShapeDtypeStruct((SUBLANES, 2 * lines), jnp.float32)
    return pl.pallas_call(
        functools.partial(absorb_kernel, slots, block_rows),
        grid=(centroids // tile,),
        in_specs=[
            pl.BlockSpec(memory_space=pltpu.SMEM),
            pl.BlockSpec((tile, features), lambda index: (index, 0)),
            lines_spec,
            lines_spec,
            state_spec,
            state_spec,
        ],
        out_specs=(state_spec, state_spec),
        out_shape=(state, state),
        input_output_aliases={4: 0, 5: 1},
        compiler_params=pltpu.CompilerParams(vmem_limit_bytes=VMEM_LIMIT),
        cost_estimate=pl.CostEstimate(
            flops=4 * lines * centroids * features,
            bytes_accessed=4 * lines * features + 2 * centroids * features,
            transcendentals=0,
        ),
        name="absorb",
    )(counts, bank, own, partner, *running)


def reduce_kernel(features, first_in, second_in, norms_ref, own_ref, partner_ref):
    first, second = first_in[...], second_in[...]
    lowest, runner = first[:1], second[:1]
    for row in range(1, SUBLANES):
        low, high = first[row : row + 1], second[row : row + 1]
        runner = jnp.minimum(jnp.minimum(runner, high), jnp.maximum(lowest, low))
        lowest = jnp.minimum(lowest, low)
    norms = norms_ref[:1]
    lines = norms.shape[1] // 2
    both = [(value + norms) / features for value in (lowest, runner)]
    for row, value in enumerate(both):
        own_ref[row : row + 1, :] = value[:, :lines]
        partner_ref[row : row + 1, :] = value[:, lines:]


def reduced(running, norms, features):
    lines = norms.shape[1] // 2
    part = jax.ShapeDtypeStruct((2, lines), jnp.float32)
    return pl.pallas_call(
        functools.partial(reduce_kernel, features),
        out_shape=(part, part),
        name="reduced",
    )(*running, norms)


def scatter_kernel(block_rows, base_ref, count_ref, to_ref, mine_ref, returned_ref, keep_ref, send_ref):
    slots = to_ref.shape[0]
    places, per_slot = keep_ref.shape[1:]
    mine, returned = mine_ref[...], returned_ref[...]
    lowest = jnp.minimum(mine[:1], returned[:1])
    runner = jnp.minimum(
        jnp.minimum(mine[1:], returned[1:]), jnp.maximum(mine[:1], returned[:1])
    )
    keep_ref[...] = jnp.full(keep_ref.shape, HUGE_DISTANCE, jnp.float32)
    send_ref[...] = jnp.full(send_ref.shape, HUGE_DISTANCE, jnp.float32)
    for slot in range(slots):
        usable = slot * block_rows < count_ref[0]
        for ref, base in ((keep_ref, base_ref[0]), (send_ref, base_ref[1])):
            place = to_ref[slot] - base
            inside = jnp.logical_and(place >= 0, place < places)

            @pl.when(jnp.logical_and(usable, inside))
            def put(ref=ref, place=place, slot=slot):
                for row, value in enumerate((lowest, runner)):
                    ref[row, pl.ds(place, 1), :] = value[
                        :, slot * per_slot : (slot + 1) * per_slot
                    ]


def scattered(mine, returned, bases, line_counts, destinations, places, block_rows):
    slots = destinations.shape[0]
    per_slot = mine.shape[1] // slots
    placed = jax.ShapeDtypeStruct((2, places, per_slot), jnp.float32)
    smem = pl.BlockSpec(memory_space=pltpu.SMEM)
    vmem = pl.BlockSpec(memory_space=pltpu.VMEM)
    return pl.pallas_call(
        functools.partial(scatter_kernel, block_rows),
        in_specs=[smem, smem, smem, vmem, vmem],
        out_shape=(placed, placed),
        name="scattered",
    )(bases, line_counts, destinations, mine, returned)


def doubled(piece, bits):
    for axis, bit in bits:
        piece = jnp.concatenate([piece, moved(piece, across(axis, bit))], axis=0)
    return piece


def shards(line_blocks, line_counts, destinations, centroids):
    hosts, columns = (lax.axis_size(axis) for axis in AXES)
    host = lax.axis_index("line")
    slots, sub_rows, features = line_blocks.shape
    block_rows = sub_rows * columns
    places = slots // 2
    own = line_blocks.reshape(slots * sub_rows, features)
    partner_of = across("line", 0)
    partner = moved(own, partner_of)
    counts = jnp.concatenate([line_counts, moved(line_counts, partner_of)])

    far = [("line", bit) for bit in range(2, hosts.bit_length() - 1)]
    far += [("centroid", bit) for bit in range(1, columns.bit_length() - 1)]
    sets = [
        doubled(centroids, far[:-1]),
        doubled(moved(centroids, across(*far[-1])), far[:-1]),
    ]
    by_line, by_column = across("line", 1), across("centroid", 0)
    norms = line_norms(own, partner)
    running = (jnp.full((SUBLANES, norms.shape[1]), HUGE_DISTANCE, jnp.float32),) * 2
    for held in sets:
        near = moved(held, by_parity(by_column, by_line))
        side = moved(held, by_parity(by_line, by_column))
        corner = moved(near, by_parity(by_line, by_column))
        for bank in (held, near, side, corner):
            running = absorb(running, bank, counts, own, partner, slots, block_rows)

    mine, theirs = reduced(running, norms, features)
    returned = moved(theirs, partner_of)
    bases = jnp.stack([host, (host + 1) % hosts]).astype(jnp.int32) * places
    keep, send = scattered(
        mine, returned, bases, line_counts, destinations, places, block_rows
    )
    arrived = moved(send, lambda at, column: (at + 1, column))
    final = jnp.minimum(keep, arrived)
    return (final[0], final[1])


def solution(mesh):
    in_specs = (P("line", "centroid", None), P("line"), P("line"), P(("centroid", "line"), None))
    out_specs = (P("line", "centroid"), P("line", "centroid"))
    return jax.shard_map(shards, mesh=mesh, in_specs=in_specs, out_specs=out_specs, check_vma=False)
```

time: 112 us -> 57.3 us (0.51)
  waiting for transfers between devices: 66.8 us -> 14.7 us
  Pallas kernels: 0 us -> 19.6 us
  between operations: 15 us -> 1.45 us
  blocking collectives: 8.65 us -> 0 us
  matrix products: 7.97 us -> 0 us
  starting transfers between devices: 6.74 us -> 13.9 us
  local copies, waits for them, and re-layouts: 3.11 us -> 5.42 us
  other arithmetic: 3.36 us -> 1.98 us
    all_gather x1 -> x0, waiting for transfers between devices: 26.3 us -> none  [shards(): gathered = lax.all_gather(resident, 'centroid', axis=1, tiled=True)]
    ppermute x7 -> x13, waiting for transfers between devices: 40.4 us -> 14.7 us  [moved(): return lax.ppermute(value, AXES, route)]
    pallas_call x0 -> x11, Pallas kernels: none -> 19.6 us  [the longest x8 14.4 us: absorb(): pl.pallas_call(functools.partial(absorb_kernel, slots, block_rows), grid=...]
    all_gather x2 -> x0, blocking collectives: 8.65 us -> none  [combined_all(): pieces = jax.tree.map(lambda part: lax.all_gather(part, axis), value)]
    dot_general x6 -> x0, matrix products: 7.97 us -> none  [the longest x4 4.48 us: absorb(): jnp.einsum('nd,kd->nk', line_rows, bank_piece, preferred_element_type=jnp...]
    ppermute x7 -> x13, starting transfers between devices: 6.7 us -> 13.9 us  [moved(): return lax.ppermute(value, AXES, route)]
    unnamed x6 -> x14, local copies, waits for them, and re-layouts: 0.59 us -> 4.8 us
    reduce_sum x8 -> x0, other arithmetic: 2.29 us -> none  [the longest x3 1.09 us: second_smallest(): tie_count = jnp.sum((values == lowest).astype(jnp.int32), axis=along)]
  transfers between devices with their start and end apart: 8 -> 13, of which waited for: 7 -> 6; matrix products, arithmetic and copies ran while one was open for 1% -> 4% of each run, Pallas kernels for 0% -> 25%
where the time goes in v1:
time: 57.3 us; the launch traced here: 57 us
  Pallas kernels  19.6 us (34%)
  waiting for transfers between devices  14.7 us (26%)
  starting transfers between devices  13.9 us (24%)
  local copies, waits for them, and re-layouts  5.42 us (9%)
  other arithmetic  1.98 us (3%)
  between operations  1.45 us (3%)
    ppermute x13, waiting for transfers between devices, moved(): return lax.ppermute(value, AXES, route)  14.7 us
    pallas_call x8, Pallas kernels, absorb(): pl.pallas_call(functools.partial(absorb_kernel, slots, block_rows), grid=...  14.4 us
    ppermute x13, starting transfers between devices, moved(): return lax.ppermute(value, AXES, route)  13.9 us
    unnamed x14, local copies, waits for them, and re-layouts  4.8 us
    pallas_call x1, Pallas kernels, line_norms(): pl.pallas_call(norm_kernel, out_shape=jax.ShapeDtypeStruct((SUBLANES, 2 *...  1.8 us
    pallas_call x1, Pallas kernels, scattered(): pl.pallas_call(functools.partial(scatter_kernel, block_rows), in_specs=[s...  1.7 us
    pallas_call x1, Pallas kernels, reduced(): pl.pallas_call(functools.partial(reduce_kernel, features), out_shape=(par...  1.63 us
  transfers between devices with their start and end apart: 13, of which 6 were waited for; matrix products, arithmetic and copies ran while one was open for 4% of the time, Pallas kernels for 25%

profile of v1, /device:TPU:0, one launch (start us, length us, event | category | flops | bytes accessed | tf_op | source)
XLA Modules:
  0.0 57.0 jit_solution(8477991180526508979)
XLA Ops:
  1.1 2.7 %collective-permute-start.7 = (bf16[64,768]{1,0:T(8,128)(2,1)}, bf16[64,768]{1,0:T(8,128)(2,1)S(1)}, u32[]{:S(2)}, u32[]{:S(2)}) collective-permute-start(bf16[64,768]{1,0:T(8,128)(2,1)} %param.7), channel_id=1, source_target_pairs={{0,8},{1,9},{2,10},{3,11},{4,12},{5,13},{6,14},{7,15},{8,0},{9,1},... | collective-permute-start | bytes 294920 | tf_op jit(solution)/shard_map/ppermute | solution.py:26
  3.8 2.6 %collective-permute-start.1 = (bf16[64,768]{1,0:T(8,128)(2,1)}, bf16[64,768]{1,0:T(8,128)(2,1)S(1)}, u32[]{:S(2)}, u32[]{:S(2)}) collective-permute-start(bf16[64,768]{1,0:T(8,128)(2,1)} %param.7), channel_id=1, source_target_pairs={{0,16},{1,17},{2,18},{3,19},{4,20},{5,21},{6,22},{7,23},{8,24},{9,... | collective-permute-start | bytes 294920 | tf_op jit(solution)/shard_map/ppermute | solution.py:26
  6.4 0.9 %constant_dynamic-update-slice_fusion.3 = bf16[128,768]{1,0:T(8,128)(2,1)S(1)} fusion(bf16[64,768]{1,0:T(8,128)(2,1)} %param.7), kind=kLoop, calls=%fused_computation.3 | loop fusion | bytes 196608
  7.4 1.7 %collective-permute-start.8 = (bf16[128,768]{1,0:T(8,128)(2,1)S(1)}, bf16[128,768]{1,0:T(8,128)(2,1)S(1)}, u32[]{:S(2)}, u32[]{:S(2)}) collective-permute-start(bf16[128,768]{1,0:T(8,128)(2,1)S(1)} %constant_dynamic-update-slice_fusion.2.bank_ref), channel_id=1, source_target_pairs={{0,1},{1,0},{2,6},{3,7},{4,5},{5,4},{6,2},{7,3},{8,9},{9,8},{10,14... | collective-permute-start | bytes 589832 | tf_op jit(solution)/shard_map/ppermute | solution.py:26
  9.1 2.8 %collective-permute-done.1 = bf16[64,768]{1,0:T(8,128)(2,1)S(1)} collective-permute-done((bf16[64,768]{1,0:T(8,128)(2,1)}, bf16[64,768]{1,0:T(8,128)(2,1)S(1)}, u32[]{:S(2)}, u32[]{:S(2)}) %collective-permute-start.1) | collective-permute-done | bytes 98336 | tf_op jit(solution)/shard_map/ppermute | solution.py:26
  12.4 4.1 %collective-permute-done.2 = bf16[64,768]{1,0:T(8,128)(2,1)S(1)} collective-permute-done((bf16[64,768]{1,0:T(8,128)(2,1)S(1)}, bf16[64,768]{1,0:T(8,128)(2,1)S(1)}, u32[]{:S(2)}, u32[]{:S(2)}) %collective-permute-start.2) | collective-permute-done | bytes 98336 | tf_op jit(solution)/shard_map/ppermute | solution.py:26
  16.5 1.6 %collective-permute-start.3 = (bf16[128,768]{1,0:T(8,128)(2,1)S(1)}, bf16[128,768]{1,0:T(8,128)(2,1)S(1)}, u32[]{:S(2)}, u32[]{:S(2)}) collective-permute-start(bf16[128,768]{1,0:T(8,128)(2,1)S(1)} %constant_dynamic-update-slice_fusion.bank_ref), channel_id=1, source_target_pairs={{0,1},{1,0},{2,6},{3,7},{4,5},{5,4},{6,2},{7,3},{8,9},{9,8},{10,14... | collective-permute-start | bytes 589832 | tf_op jit(solution)/shard_map/ppermute | solution.py:26
  18.1 1.5 %collective-permute-start.10 = (bf16[128,768]{1,0:T(8,128)(2,1)S(1)}, bf16[128,768]{1,0:T(8,128)(2,1)S(1)}, u32[]{:S(2)}, u32[]{:S(2)}) collective-permute-start(bf16[128,768]{1,0:T(8,128)(2,1)S(1)} %constant_dynamic-update-slice_fusion.2.bank_ref), channel_id=1, source_target_pairs={{0,4},{1,5},{2,3},{3,2},{4,0},{5,1},{6,7},{7,6},{8,12},{9,13},{10,... | collective-permute-start | bytes 589832 | tf_op jit(solution)/shard_map/ppermute | solution.py:26
  21.0 0.7 %pad_add_fusion.counts_ref = s32[2]{0:T(128)S(1)} fusion(s32[1]{0:T(128)} %collective-permute-done, s32[1]{0:T(128)S(6)} %copy.40.count_ref), kind=kLoop, calls=%fused_computation.7 | loop fusion | flops 2 | bytes 16 | tf_op jit(solution)/shard_map/concatenate | solution.py:228
  21.7 1.4 %collective-permute-start.6 = (bf16[128,768]{1,0:T(8,128)(2,1)S(1)}, bf16[128,768]{1,0:T(8,128)(2,1)S(1)}, u32[]{:S(2)}, u32[]{:S(2)}) collective-permute-start(bf16[128,768]{1,0:T(8,128)(2,1)S(1)} %constant_dynamic-update-slice_fusion.bank_ref), channel_id=1, source_target_pairs={{0,4},{1,5},{2,3},{3,2},{4,0},{5,1},{6,7},{7,6},{8,12},{9,13},{10,... | collective-permute-start | bytes 589832 | tf_op jit(solution)/shard_map/ppermute | solution.py:26
  23.1 0.7 %collective-permute-start.4 = (bf16[128,768]{1,0:T(8,128)(2,1)S(1)}, bf16[128,768]{1,0:T(8,128)(2,1)S(1)}, u32[]{:S(2)}, u32[]{:S(2)}) collective-permute-start(bf16[128,768]{1,0:T(8,128)(2,1)S(1)} %collective-permute-done.3.bank_ref), channel_id=1, source_target_pairs={{0,4},{1,5},{2,3},{3,2},{4,0},{5,1},{6,7},{7,6},{8,12},{9,13},{10,... | collective-permute-start | bytes 589832 | tf_op jit(solution)/shard_map/ppermute | solution.py:26
  23.8 1.4 %copy-done = bf16[16,64,768]{2,1,0:T(8,128)(2,1)S(1)} copy-done((bf16[16,64,768]{2,1,0:T(8,128)(2,1)S(1)}, bf16[16,64,768]{2,1,0:T(8,128)(2,1)}, u32[]{:S(2)}) %copy-start) | copy-done | bytes 1572888
  25.2 1.8 %absorb.8 = (f32[8,2048]{1,0:T(8,128)S(1)}, f32[8,2048]{1,0:T(8,128)S(1)}) custom-call(s32[2]{0:T(128)S(1)} %pad_add_fusion.counts_ref, bf16[128,768]{1,0:T(8,128)(2,1)S(1)} %constant_dynamic-update-slice_fusion.2.bank_ref, bf16[1024,768]{1,0:T(8,128)(2,1)S(1)} %bitcast.8, ...), custom_call_target="tpu_custom_call", output_to_operand_aliasing={{0}: (4, {}), {1}: (5, {})} | custom-call | flops 402653184 | bytes 3342336 | tf_op jit(solution)/shard_map/absorb/pallas_call | solution.py:126
  27.0 1.8 %absorb.9 = (f32[8,2048]{1,0:T(8,128)S(1)}, f32[8,2048]{1,0:T(8,128)S(1)}) custom-call(s32[2]{0:T(128)S(1)} %pad_add_fusion.counts_ref, bf16[128,768]{1,0:T(8,128)(2,1)S(1)} %collective-permute-done.8.bank_ref, bf16[1024,768]{1,0:T(8,128)(2,1)S(1)} %bitcast.9, ...), custom_call_target="tpu_custom_call", output_to_operand_aliasing={{0}: (4, {}), {1}: (5, {})} | custom-call | flops 402653184 | bytes 3342336 | tf_op jit(solution)/shard_map/absorb/pallas_call | solution.py:126
  28.8 1.8 %line_norms.1.norms_ref = f32[8,2048]{1,0:T(8,128)S(1)} custom-call(bf16[1024,768]{1,0:T(8,128)(2,1)S(1)} %bitcast.10, bf16[1024,768]{1,0:T(8,128)(2,1)S(1)} %collective-permute-done.5.partner_ref), custom_call_target="tpu_custom_call" | custom-call | flops 25165824 | bytes 3145728 | tf_op jit(solution)/shard_map/line_norms/pallas_call | solution.py:70
  30.6 0.6 %copy-done.4 = f32[8,2048]{1,0:T(8,128)} copy-done((f32[8,2048]{1,0:T(8,128)}, f32[8,2048]{1,0:T(8,128)S(1)}, u32[]{:S(2)}) %copy-start.4) | copy-done | bytes 65560
  31.3 1.8 %absorb.10 = (f32[8,2048]{1,0:T(8,128)S(1)}, f32[8,2048]{1,0:T(8,128)S(1)}) custom-call(s32[2]{0:T(128)S(1)} %pad_add_fusion.counts_ref, bf16[128,768]{1,0:T(8,128)(2,1)S(1)} %collective-permute-done.10.bank_ref, bf16[1024,768]{1,0:T(8,128)(2,1)S(1)} %bitcast.11, ...), custom_call_target="tpu_custom_call", output_to_operand_aliasing={{0}: (4, {}), {1}: (5, {})} | custom-call | flops 402653184 | bytes 3342336 | tf_op jit(solution)/shard_map/absorb/pallas_call | solution.py:126
  33.1 1.8 %absorb.11 = (f32[8,2048]{1,0:T(8,128)S(1)}, f32[8,2048]{1,0:T(8,128)S(1)}) custom-call(s32[2]{0:T(128)S(1)} %pad_add_fusion.counts_ref, bf16[128,768]{1,0:T(8,128)(2,1)S(1)} %collective-permute-done.9.bank_ref, bf16[1024,768]{1,0:T(8,128)(2,1)S(1)} %bitcast.12, ...), custom_call_target="tpu_custom_call", output_to_operand_aliasing={{0}: (4, {}), {1}: (5, {})} | custom-call | flops 402653184 | bytes 3342336 | tf_op jit(solution)/shard_map/absorb/pallas_call | solution.py:126
  34.9 1.8 %absorb.12 = (f32[8,2048]{1,0:T(8,128)S(1)}, f32[8,2048]{1,0:T(8,128)S(1)}) custom-call(s32[2]{0:T(128)S(1)} %pad_add_fusion.counts_ref, bf16[128,768]{1,0:T(8,128)(2,1)S(1)} %constant_dynamic-update-slice_fusion.bank_ref, bf16[1024,768]{1,0:T(8,128)(2,1)S(1)} %bitcast.13, ...), custom_call_target="tpu_custom_call", output_to_operand_aliasing={{0}: (4, {}), {1}: (5, {})} | custom-call | flops 402653184 | bytes 3342336 | tf_op jit(solution)/shard_map/absorb/pallas_call | solution.py:126
  36.7 1.8 %absorb.13 = (f32[8,2048]{1,0:T(8,128)S(1)}, f32[8,2048]{1,0:T(8,128)S(1)}) custom-call(s32[2]{0:T(128)S(1)} %pad_add_fusion.counts_ref, bf16[128,768]{1,0:T(8,128)(2,1)S(1)} %collective-permute-done.3.bank_ref, bf16[1024,768]{1,0:T(8,128)(2,1)S(1)} %bitcast.14, ...), custom_call_target="tpu_custom_call", output_to_operand_aliasing={{0}: (4, {}), {1}: (5, {})} | custom-call | flops 402653184 | bytes 3342336 | tf_op jit(solution)/shard_map/absorb/pallas_call | solution.py:126
  38.6 1.8 %absorb.14 = (f32[8,2048]{1,0:T(8,128)S(1)}, f32[8,2048]{1,0:T(8,128)S(1)}) custom-call(s32[2]{0:T(128)S(1)} %pad_add_fusion.counts_ref, bf16[128,768]{1,0:T(8,128)(2,1)S(1)} %collective-permute-done.6.bank_ref, bf16[1024,768]{1,0:T(8,128)(2,1)S(1)} %bitcast.15, ...), custom_call_target="tpu_custom_call", output_to_operand_aliasing={{0}: (4, {}), {1}: (5, {})} | custom-call | flops 402653184 | bytes 3342336 | tf_op jit(solution)/shard_map/absorb/pallas_call | solution.py:126
  40.4 1.8 %absorb.15 = (f32[8,2048]{1,0:T(8,128)S(1)}, f32[8,2048]{1,0:T(8,128)S(1)}) custom-call(s32[2]{0:T(128)S(1)} %pad_add_fusion.counts_ref, bf16[128,768]{1,0:T(8,128)(2,1)S(1)} %collective-permute-done.4.bank_ref, bf16[1024,768]{1,0:T(8,128)(2,1)S(1)} %bitcast.16, ...), custom_call_target="tpu_custom_call", output_to_operand_aliasing={{0}: (4, {}), {1}: (5, {})} | custom-call | flops 402653184 | bytes 3342336 | tf_op jit(solution)/shard_map/absorb/pallas_call | solution.py:126
  42.2 0.6 %copy-done.2 = f32[8,2048]{1,0:T(8,128)} copy-done((f32[8,2048]{1,0:T(8,128)}, f32[8,2048]{1,0:T(8,128)S(1)}, u32[]{:S(2)}) %copy-start.2) | copy-done | bytes 65560
  42.8 0.6 %copy-done.3 = f32[8,2048]{1,0:T(8,128)} copy-done((f32[8,2048]{1,0:T(8,128)}, f32[8,2048]{1,0:T(8,128)S(1)}, u32[]{:S(2)}) %copy-start.3) | copy-done | bytes 65560
  43.4 1.6 %reduced.1 = (f32[2,1024]{1,0:T(2,128)}, f32[2,1024]{1,0:T(2,128)}) custom-call(f32[8,2048]{1,0:T(8,128)} %copy-done.2, f32[8,2048]{1,0:T(8,128)} %copy-done.3, f32[8,2048]{1,0:T(8,128)} %copy-done.4), custom_call_target="tpu_custom_call" | custom-call | tf_op jit(solution)/shard_map/reduced/pallas_call | solution.py:168
  45.1 0.6 %add_multiply_fusion.base_ref = s32[2]{0:T(128)} fusion(s32[1]{0:T(128)} %bitcast.1, s32[1]{0:T(128)} %bitcast), kind=kLoop, calls=%fused_computation.6 | loop fusion | flops 4 | bytes 16 | tf_op jit(solution)/shard_map/mul | solution.py:248
  45.6 0.8 %collective-permute-done.11.returned_ref = f32[2,1024]{1,0:T(2,128)S(1)} collective-permute-done((f32[2,1024]{1,0:T(2,128)}, f32[2,1024]{1,0:T(2,128)S(1)}, u32[]{:S(2)}, u32[]{:S(2)}) %collective-permute-start.11) | collective-permute-done | bytes 8224 | tf_op jit(solution)/shard_map/ppermute | solution.py:26
  46.4 0.6 %copy-done.5 = f32[2,1024]{1,0:T(2,128)} copy-done((f32[2,1024]{1,0:T(2,128)}, f32[2,1024]{1,0:T(2,128)S(1)}, u32[]{:S(2)}) %copy-start.5) | copy-done | bytes 8216
  47.0 1.7 %scattered.1 = (f32[2,8,64]{2,1,0:T(8,128)}, f32[2,8,64]{2,1,0:T(8,128)}) custom-call(s32[2]{0:T(128)} %add_multiply_fusion.base_ref, s32[1]{0:T(128)S(6)} %copy.40.count_ref, s32[16]{0:T(128)} %to_ref.1, f32[2,1024]{1,0:T(2,128)} %get-tuple-element.38.mine_ref, f32[2,1024]{1,0:T(2,128)} %copy-done.5), custom_call_target="tpu_custom_call" | custom-call | tf_op jit(solution)/shard_map/scattered/pallas_call | solution.py:205
  48.9 6.8 %collective-permute-done.12 = f32[2,8,64]{2,1,0:T(8,128)S(1)} collective-permute-done((f32[2,8,64]{2,1,0:T(8,128)}, f32[2,8,64]{2,1,0:T(8,128)S(1)}, u32[]{:S(2)}, u32[]{:S(2)}) %collective-permute-start.12) | collective-permute-done | bytes 4128 | tf_op jit(solution)/shard_map/ppermute | solution.py:26
  55.7 0.7 %min.3 = f32[2,8,64]{2,1,0:T(8,128)S(1)} minimum(f32[2,8,64]{2,1,0:T(8,128)} %get-tuple-element.40, f32[2,8,64]{2,1,0:T(8,128)S(1)} %collective-permute-done.12) | non-fusion elementwise | flops 1024 | bytes 12288 | tf_op jit(solution)/shard_map/min | solution.py:253
  56.4 0.6 %slice_bitcast_fusion = (f32[8,64]{1,0:T(8,128)}, f32[8,64]{1,0:T(8,128)}) fusion(f32[2,8,64]{2,1,0:T(8,128)S(1)} %min.3), kind=kLoop, calls=%fused_computation.4 | loop fusion | bytes 8192 | tf_op jit(solution)/shard_map/squeeze | solution.py:254
  (27 shorter events, 2.0 us)
Async XLA Ops:
  0.6 23.2 %collective-permute-start.5 = (bf16[1024,768]{1,0:T(8,128)(2,1)}, bf16[1024,768]{1,0:T(8,128)(2,1)S(1)}, u32[]{:S(2)}, u32[]{:S(2)}) collective-permute-start(bf16[1024,768]{1,0:T(8,128)(2,1)} %bitcast.7), channel_id=1, source_target_pairs={{0,2},{1,3},{2,0},{3,1},{4,6},{5,7},{6,4},{7,5},{8,10},{9,11},{10,... | collective-permute-start | bytes 4718600 | tf_op jit(solution)/shard_map/ppermute | solution.py:26
  1.1 6.2 %collective-permute-start.7 = (bf16[64,768]{1,0:T(8,128)(2,1)}, bf16[64,768]{1,0:T(8,128)(2,1)S(1)}, u32[]{:S(2)}, u32[]{:S(2)}) collective-permute-start(bf16[64,768]{1,0:T(8,128)(2,1)} %param.7), channel_id=1, source_target_pairs={{0,8},{1,9},{2,10},{3,11},{4,12},{5,13},{6,14},{7,15},{8,0},{9,1},... | collective-permute-start | bytes 294920 | tf_op jit(solution)/shard_map/ppermute | solution.py:26
  3.8 8.1 %collective-permute-start.1 = (bf16[64,768]{1,0:T(8,128)(2,1)}, bf16[64,768]{1,0:T(8,128)(2,1)S(1)}, u32[]{:S(2)}, u32[]{:S(2)}) collective-permute-start(bf16[64,768]{1,0:T(8,128)(2,1)} %param.7), channel_id=1, source_target_pairs={{0,16},{1,17},{2,18},{3,19},{4,20},{5,21},{6,22},{7,23},{8,24},{9,... | collective-permute-start | bytes 294920 | tf_op jit(solution)/shard_map/ppermute | solution.py:26
  7.4 12.9 %collective-permute-start.8 = (bf16[128,768]{1,0:T(8,128)(2,1)S(1)}, bf16[128,768]{1,0:T(8,128)(2,1)S(1)}, u32[]{:S(2)}, u32[]{:S(2)}) collective-permute-start(bf16[128,768]{1,0:T(8,128)(2,1)S(1)} %constant_dynamic-update-slice_fusion.2.bank_ref), channel_id=1, source_target_pairs={{0,1},{1,0},{2,6},{3,7},{4,5},{5,4},{6,2},{7,3},{8,9},{9,8},{10,14... | collective-permute-start | bytes 589832 | tf_op jit(solution)/shard_map/ppermute | solution.py:26
  11.9 4.6 %collective-permute-start.2 = (bf16[64,768]{1,0:T(8,128)(2,1)S(1)}, bf16[64,768]{1,0:T(8,128)(2,1)S(1)}, u32[]{:S(2)}, u32[]{:S(2)}) collective-permute-start(bf16[64,768]{1,0:T(8,128)(2,1)S(1)} %collective-permute-done.1), channel_id=1, source_target_pairs={{0,8},{1,9},{2,10},{3,11},{4,12},{5,13},{6,14},{7,15},{8,0},{9,1},... | collective-permute-start | bytes 294920 | tf_op jit(solution)/shard_map/ppermute | solution.py:26
  16.5 6.6 %collective-permute-start.3 = (bf16[128,768]{1,0:T(8,128)(2,1)S(1)}, bf16[128,768]{1,0:T(8,128)(2,1)S(1)}, u32[]{:S(2)}, u32[]{:S(2)}) collective-permute-start(bf16[128,768]{1,0:T(8,128)(2,1)S(1)} %constant_dynamic-update-slice_fusion.bank_ref), channel_id=1, source_target_pairs={{0,1},{1,0},{2,6},{3,7},{4,5},{5,4},{6,2},{7,3},{8,9},{9,8},{10,14... | collective-permute-start | bytes 589832 | tf_op jit(solution)/shard_map/ppermute | solution.py:26
  18.1 13.2 %collective-permute-start.10 = (bf16[128,768]{1,0:T(8,128)(2,1)S(1)}, bf16[128,768]{1,0:T(8,128)(2,1)S(1)}, u32[]{:S(2)}, u32[]{:S(2)}) collective-permute-start(bf16[128,768]{1,0:T(8,128)(2,1)S(1)} %constant_dynamic-update-slice_fusion.2.bank_ref), channel_id=1, source_target_pairs={{0,4},{1,5},{2,3},{3,2},{4,0},{5,1},{6,7},{7,6},{8,12},{9,13},{10,... | collective-permute-start | bytes 589832 | tf_op jit(solution)/shard_map/ppermute | solution.py:26
  19.6 1.4 %collective-permute-start = (s32[1]{0:T(128)}, s32[1]{0:T(128)}, u32[]{:S(2)}, u32[]{:S(2)}) collective-permute-start(s32[1]{0:T(128)} %param.5), channel_id=1, source_target_pairs={{0,2},{1,3},{2,0},{3,1},{4,6},{5,7},{6,4},{7,5},{8,10},{9,11},{10,... | collective-permute-start | bytes 20 | tf_op jit(solution)/shard_map/ppermute | solution.py:26
  20.3 12.8 %collective-permute-start.9 = (bf16[128,768]{1,0:T(8,128)(2,1)S(1)}, bf16[128,768]{1,0:T(8,128)(2,1)S(1)}, u32[]{:S(2)}, u32[]{:S(2)}) collective-permute-start(bf16[128,768]{1,0:T(8,128)(2,1)S(1)} %collective-permute-done.8.bank_ref), channel_id=1, source_target_pairs={{0,4},{1,5},{2,3},{3,2},{4,0},{5,1},{6,7},{7,6},{8,12},{9,13},{10,... | collective-permute-start | bytes 589832 | tf_op jit(solution)/shard_map/ppermute | solution.py:26
  21.7 16.9 %collective-permute-start.6 = (bf16[128,768]{1,0:T(8,128)(2,1)S(1)}, bf16[128,768]{1,0:T(8,128)(2,1)S(1)}, u32[]{:S(2)}, u32[]{:S(2)}) collective-permute-start(bf16[128,768]{1,0:T(8,128)(2,1)S(1)} %constant_dynamic-update-slice_fusion.bank_ref), channel_id=1, source_target_pairs={{0,4},{1,5},{2,3},{3,2},{4,0},{5,1},{6,7},{7,6},{8,12},{9,13},{10,... | collective-permute-start | bytes 589832 | tf_op jit(solution)/shard_map/ppermute | solution.py:26
  23.1 17.3 %collective-permute-start.4 = (bf16[128,768]{1,0:T(8,128)(2,1)S(1)}, bf16[128,768]{1,0:T(8,128)(2,1)S(1)}, u32[]{:S(2)}, u32[]{:S(2)}) collective-permute-start(bf16[128,768]{1,0:T(8,128)(2,1)S(1)} %collective-permute-done.3.bank_ref), channel_id=1, source_target_pairs={{0,4},{1,5},{2,3},{3,2},{4,0},{5,1},{6,7},{7,6},{8,12},{9,13},{10,... | collective-permute-start | bytes 589832 | tf_op jit(solution)/shard_map/ppermute | solution.py:26
  23.8 1.4 %copy-start = (bf16[16,64,768]{2,1,0:T(8,128)(2,1)S(1)}, bf16[16,64,768]{2,1,0:T(8,128)(2,1)}, u32[]{:S(2)}) copy-start(bf16[16,64,768]{2,1,0:T(8,128)(2,1)} %param.4) | copy-start | bytes 4718596
  25.2 1.8 %copy-start.1 = (bf16[16,64,768]{2,1,0:T(8,128)(2,1)S(1)}, bf16[16,64,768]{2,1,0:T(8,128)(2,1)}, u32[]{:S(2)}) copy-start(bf16[16,64,768]{2,1,0:T(8,128)(2,1)} %param.4) | copy-start | bytes 4718596
  30.6 0.6 %copy-start.4 = (f32[8,2048]{1,0:T(8,128)}, f32[8,2048]{1,0:T(8,128)S(1)}, u32[]{:S(2)}) copy-start(f32[8,2048]{1,0:T(8,128)S(1)} %line_norms.1.norms_ref) | copy-start | bytes 196612
  42.2 0.6 %copy-start.2 = (f32[8,2048]{1,0:T(8,128)}, f32[8,2048]{1,0:T(8,128)S(1)}, u32[]{:S(2)}) copy-start(f32[8,2048]{1,0:T(8,128)S(1)} %get-tuple-element.36.first_in) | copy-start | bytes 196612
  42.8 0.6 %copy-start.3 = (f32[8,2048]{1,0:T(8,128)}, f32[8,2048]{1,0:T(8,128)S(1)}, u32[]{:S(2)}) copy-start(f32[8,2048]{1,0:T(8,128)S(1)} %get-tuple-element.37.second_in) | copy-start | bytes 196612
  45.1 1.4 %collective-permute-start.11 = (f32[2,1024]{1,0:T(2,128)}, f32[2,1024]{1,0:T(2,128)S(1)}, u32[]{:S(2)}, u32[]{:S(2)}) collective-permute-start(f32[2,1024]{1,0:T(2,128)} %get-tuple-element.39), channel_id=1, source_target_pairs={{0,2},{1,3},{2,0},{3,1},{4,6},{5,7},{6,4},{7,5},{8,10},{9,11},{10,... | collective-permute-start | bytes 24584 | tf_op jit(solution)/shard_map/ppermute | solution.py:26
  46.4 0.6 %copy-start.5 = (f32[2,1024]{1,0:T(2,128)}, f32[2,1024]{1,0:T(2,128)S(1)}, u32[]{:S(2)}) copy-start(f32[2,1024]{1,0:T(2,128)S(1)} %collective-permute-done.11.returned_ref) | copy-start | bytes 24580
  48.7 7.0 %collective-permute-start.12 = (f32[2,8,64]{2,1,0:T(8,128)}, f32[2,8,64]{2,1,0:T(8,128)S(1)}, u32[]{:S(2)}, u32[]{:S(2)}) collective-permute-start(f32[2,8,64]{2,1,0:T(8,128)} %get-tuple-element.41), channel_id=1, source_target_pairs={{0,2},{1,3},{2,4},{3,5},{4,6},{5,7},{6,8},{7,9},{8,10},{9,11},{10,... | collective-permute-start | bytes 12296 | tf_op jit(solution)/shard_map/ppermute | solution.py:26

commit v2 on v0

v2 whole, which is shorter than its diff:
```python
import functools

import jax
import jax.numpy as jnp
from jax import lax
from jax.experimental import pallas as pl
from jax.experimental.pallas import tpu as pltpu
from jax.sharding import PartitionSpec as P

HUGE_DISTANCE = 3e38
AXES = ("line", "centroid")
BANK_TILE = 512
LINE_STEP = 1024
SUBLANES = 8
VMEM_LIMIT = 16 * 2**20
VMEM = pl.BlockSpec(memory_space=pltpu.VMEM)
SMEM = pl.BlockSpec(memory_space=pltpu.SMEM)


def moved(value, target):
    hosts, columns = (lax.axis_size(axis) for axis in AXES)
    route = []
    for host in range(hosts):
        for column in range(columns):
            to = target(host, column)
            route.append((host * columns + column, to[0] % hosts * columns + to[1]))
    return lax.ppermute(value, AXES, route)


def across(axis, bit):
    if axis == "line":
        return lambda host, column: (host ^ 1 << bit, column)
    return lambda host, column: (host, column ^ 1 << bit)


def by_parity(even, odd):
    return lambda host, column: (odd if host & 1 else even)(host, column)


def call(body, outs, operands, spaces, flops=0, scratch=(), aliases={}, name=None):
    traffic = sum(value.size * value.dtype.itemsize for value in operands)
    return pl.pallas_call(
        body,
        in_specs=list(spaces),
        out_specs=(VMEM,) * len(outs),
        out_shape=outs,
        scratch_shapes=list(scratch),
        input_output_aliases=aliases,
        compiler_params=pltpu.CompilerParams(vmem_limit_bytes=VMEM_LIMIT),
        cost_estimate=pl.CostEstimate(flops=flops, bytes_accessed=traffic, transcendentals=0),
        name=name,
    )(*operands)


def contract(left, right):
    return lax.dot_general(
        left, right, (((1,), (1,)), ((), ())), preferred_element_type=jnp.float32
    )


def fold(first, second, value):
    second = jnp.minimum(second, jnp.maximum(first, value))
    return jnp.minimum(first, value), second


def join(first, second, other_first, other_second):
    runner = jnp.minimum(jnp.minimum(second, other_second), jnp.maximum(first, other_first))
    return jnp.minimum(first, other_first), runner


def norm_kernel(own_ref, norms_ref):
    lines, features = own_ref.shape
    ones = jnp.ones((SUBLANES, features), jnp.bfloat16)
    step = min(lines, LINE_STEP)
    for at in range(0, lines, step):
        wide = own_ref[at : at + step, :].astype(jnp.float32)
        square = wide * wide
        high = square.astype(jnp.bfloat16)
        low = (square - high.astype(jnp.float32)).astype(jnp.bfloat16)
        norms_ref[:, at : at + step] = contract(ones, high) + contract(ones, low)


def line_norms(own):
    lines, features = own.shape
    out = jax.ShapeDtypeStruct((SUBLANES, lines), jnp.float32)
    return call(
        norm_kernel, (out,), (own,), (VMEM,), 32 * SUBLANES * lines * features, name="line_norms"
    )[0]


def prepared(banks):
    scaled = jnp.concatenate([bank * jnp.array(-2, jnp.bfloat16) for bank in banks], axis=0)
    wide = [bank.astype(jnp.float32) for bank in banks]
    norms = [jnp.sum(rows * rows, axis=1, keepdims=True) for rows in wide]
    return scaled, jnp.concatenate(norms, axis=0)


def absorbed(banks, lines, first, second):
    scaled, norms = prepared(banks)
    distance = contract(scaled, lines) + norms
    for row in range(0, distance.shape[0], SUBLANES):
        first, second = fold(first, second, distance[row : row + SUBLANES])
    return first, second


def tiles(bank_refs):
    plan, held, rows = [], [], 0
    for ref in bank_refs:
        tile = min(ref.shape[0], BANK_TILE)
        for at in range(0, ref.shape[0], tile):
            if rows + tile > BANK_TILE:
                plan.append(held)
                held, rows = [], 0
            held.append((ref, at, tile))
            rows += tile
    return plan + [held]


def absorb_kernel(line_count, bank_count, *refs):
    line_refs, refs = refs[:line_count], refs[line_count:]
    bank_refs, refs = refs[:bank_count], refs[bank_count:]
    for lines_ref, in_ref, out_ref in zip(line_refs, refs[:line_count], refs[line_count:]):
        lines = lines_ref.shape[0]
        step = min(lines, LINE_STEP)
        for at in range(0, lines, step):
            first, second = in_ref[:SUBLANES, at : at + step], in_ref[SUBLANES:, at : at + step]
            for group in tiles(bank_refs):
                banks = [ref[row : row + tile, :] for ref, row, tile in group]
                first, second = absorbed(banks, lines_ref[at : at + step, :], first, second)
            out_ref[:SUBLANES, at : at + step] = first
            out_ref[SUBLANES:, at : at + step] = second


def absorb(states, banks, line_sets):
    features = banks[0].shape[1]
    rows = sum(bank.shape[0] for bank in banks)
    total = sum(lines.shape[0] for lines in line_sets)
    count = len(line_sets)
    operands = (*line_sets, *banks, *states)
    return call(
        functools.partial(absorb_kernel, count, len(banks)),
        tuple(jax.ShapeDtypeStruct(state.shape, state.dtype) for state in states),
        operands,
        (VMEM,) * len(operands),
        2 * rows * total * features,
        aliases={count + len(banks) + i: i for i in range(count)},
        name="absorb",
    )


def last_kernel(slots, places, block_rows, bank_count, count_ref, to_ref, lines_ref, *refs):
    bank_refs, refs = refs[:bank_count], refs[bank_count:]
    mine_ref, returned_ref, norms_ref, keep_ref, send_ref, placed_ref = refs
    lines, features = lines_ref.shape
    per_slot = lines // slots
    hosts = lax.axis_size("line")
    host = lax.axis_index("line")
    following = lax.rem(host + 1, hosts)
    first, second = join(
        mine_ref[:SUBLANES], mine_ref[SUBLANES:], returned_ref[:SUBLANES], returned_ref[SUBLANES:]
    )
    for group in tiles(bank_refs):
        banks = [ref[row : row + tile, :] for ref, row, tile in group]
        first, second = absorbed(banks, lines_ref[...], first, second)
    lowest, runner = first[:1], second[:1]
    for row in range(1, SUBLANES):
        lowest, runner = join(lowest, runner, first[row : row + 1], second[row : row + 1])
    both = [(value + norms_ref[:1]) / features for value in (lowest, runner)]
    placed_ref[...] = jnp.full(placed_ref.shape, HUGE_DISTANCE, jnp.float32)
    for slot in range(slots):
        usable = slot * block_rows < count_ref[0]
        here = to_ref[slot] - host * places
        there = to_ref[slot] - following * places
        row = jnp.where(jnp.logical_and(there >= 0, there < places), places + there, 2 * places)
        row = jnp.where(jnp.logical_and(here >= 0, here < places), here, row)
        row = jnp.where(usable, row, 2 * places)
        for index, value in enumerate(both):
            placed_ref[index, pl.ds(row, 1), :] = value[:, slot * per_slot : (slot + 1) * per_slot]
    keep_ref[...] = placed_ref[:, :places]
    send_ref[...] = placed_ref[:, places : 2 * places]


def last(line_counts, destinations, own, banks, mine, returned, norms, places, block_rows):
    slots = destinations.shape[0]
    lines, features = own.shape
    per_slot = lines // slots
    operands = (line_counts, destinations, own, *banks, mine, returned, norms)
    placed = jax.ShapeDtypeStruct((2, places, per_slot), jnp.float32)
    return call(
        functools.partial(last_kernel, slots, places, block_rows, len(banks)),
        (placed, placed),
        operands,
        (SMEM, SMEM) + (VMEM,) * (len(operands) - 2),
        2 * lines * features * sum(bank.shape[0] for bank in banks),
        scratch=(pltpu.VMEM((2, 2 * places + SUBLANES, per_slot), jnp.float32),),
        name="last",
    )


def final_kernel(keep_ref, arrived_ref, nearest_ref, runner_ref):
    for index, ref in enumerate((nearest_ref, runner_ref)):
        ref[...] = jnp.minimum(keep_ref[index], arrived_ref[index])


def final(keep, arrived):
    out = jax.ShapeDtypeStruct(keep.shape[1:], keep.dtype)
    return call(final_kernel, (out, out), (keep, arrived), (VMEM, VMEM), name="final")


def doubled(piece, bits):
    for axis, bit in bits:
        piece = jnp.concatenate([piece, moved(piece, across(axis, bit))], axis=0)
    return piece


def shards(line_blocks, line_counts, destinations, centroids):
    hosts, columns = (lax.axis_size(axis) for axis in AXES)
    slots, sub_rows, features = line_blocks.shape
    block_rows = sub_rows * columns
    places = slots // 2
    own = line_blocks.reshape(slots * sub_rows, features)
    partner_of = across("line", 0)
    partner = moved(own, partner_of)

    far = [("line", bit) for bit in range(2, hosts.bit_length() - 1)]
    far += [("centroid", bit) for bit in range(1, columns.bit_length() - 1)]
    distant = moved(centroids, across(*far[-1]))
    norms = line_norms(own)
    by_line, by_column = across("line", 1), across("centroid", 0)
    turned, straight = by_parity(by_line, by_column), by_parity(by_column, by_line)

    held_a = doubled(centroids, far[:-1])
    held_a, norms = lax.optimization_barrier((held_a, norms))
    near_a = moved(held_a, straight)
    distant, held_late = lax.optimization_barrier((distant, held_a))
    held_b = doubled(distant, far[:-1])
    side_a = moved(held_late, turned)

    empty = jnp.full((2 * SUBLANES, own.shape[0]), HUGE_DISTANCE, jnp.float32)
    states = absorb((empty, empty), (held_late,), (own, partner))
    held_b, states = lax.optimization_barrier((held_b, states))
    corner_a = moved(near_a, turned)
    near_b = moved(held_b, straight)
    side_b = moved(held_b, turned)
    corner_b = moved(near_b, turned)
    states = absorb(states, (near_a, held_b), (own, partner))
    states = absorb(states, (side_a, corner_a), (own, partner))
    states = absorb(states, (near_b, side_b), (own, partner))
    corner_b, states = lax.optimization_barrier((corner_b, states))
    returned = moved(states[1], partner_of)
    shared = moved(corner_b, partner_of)
    keep, send = last(
        line_counts,
        destinations,
        own,
        (corner_b, shared),
        states[0],
        returned,
        norms,
        places,
        block_rows,
    )
    arrived = moved(send, lambda host, column: (host + 1, column))
    return tuple(final(keep, arrived))


def solution(mesh):
    in_specs = (P("line", "centroid", None), P("line"), P("line"), P(("centroid", "line"), None))
    out_specs = (P("line", "centroid"), P("line", "centroid"))
    return jax.shard_map(shards, mesh=mesh, in_specs=in_specs, out_specs=out_specs, check_vma=False)
```

time: 112 us -> 40.7 us (0.36)
  waiting for transfers between devices: 66.8 us -> 15.1 us
  between operations: 15 us -> 1.4 us
  blocking collectives: 8.65 us -> 0 us
  starting transfers between devices: 6.74 us -> 15.1 us
  matrix products: 7.97 us -> 0 us
  Pallas kernels: 0 us -> 7.42 us
  other arithmetic: 3.36 us -> 0.03 us
  local copies, waits for them, and re-layouts: 3.11 us -> 1.44 us
    all_gather x1 -> x0, waiting for transfers between devices: 26.3 us -> none  [shards(): gathered = lax.all_gather(resident, 'centroid', axis=1, tiled=True)]
    ppermute x7 -> x13, waiting for transfers between devices: 40.4 us -> 15.1 us  [moved(): return lax.ppermute(value, AXES, route)]
    all_gather x2 -> x0, blocking collectives: 8.65 us -> none  [combined_all(): pieces = jax.tree.map(lambda part: lax.all_gather(part, axis), value)]
    ppermute x7 -> x13, starting transfers between devices: 6.7 us -> 15.1 us  [moved(): return lax.ppermute(value, AXES, route)]
    dot_general x6 -> x0, matrix products: 7.97 us -> none  [the longest x4 4.48 us: absorb(): jnp.einsum('nd,kd->nk', line_rows, bank_piece, preferred_element_type=jnp...]
    pallas_call x0 -> x7, Pallas kernels: none -> 7.42 us  [call(): pl.pallas_call(body, in_specs=list(spaces), out_specs=(VMEM,) * len(outs)...]
    reduce_sum x8 -> x0, other arithmetic: 2.29 us -> none  [the longest x3 1.09 us: second_smallest(): tie_count = jnp.sum((values == lowest).astype(jnp.int32), axis=along)]
    all_gather x1 -> x0, local copies, waits for them, and re-layouts: 1.74 us -> none  [shards(): gathered = lax.all_gather(resident, 'centroid', axis=1, tiled=True)]
  transfers between devices with their start and end apart: 8 -> 13, of which waited for: 7 -> 6; matrix products, arithmetic and copies ran while one was open for 1% -> 0% of each run, Pallas kernels for 0% -> 14%
where the time goes in v2:
time: 40.7 us; the launch traced here: 40.6 us
  starting transfers between devices  15.1 us (37%)
  waiting for transfers between devices  15.1 us (37%)
  Pallas kernels  7.42 us (18%)
  local copies, waits for them, and re-layouts  1.44 us (4%)
  between operations  1.4 us (3%)
    ppermute x13, waiting for transfers between devices, moved(): return lax.ppermute(value, AXES, route)  15.1 us
    ppermute x13, starting transfers between devices, moved(): return lax.ppermute(value, AXES, route)  15.1 us
    pallas_call x7, Pallas kernels, call(): pl.pallas_call(body, in_specs=list(spaces), out_specs=(VMEM,) * len(outs)...  7.42 us
    unnamed x6, local copies, waits for them, and re-layouts  1.43 us
  transfers between devices with their start and end apart: 13, of which 6 were waited for; matrix products, arithmetic and copies ran while one was open for 0% of the time, Pallas kernels for 14%

profile of v2, /device:TPU:0, one launch (start us, length us, event | category | flops | bytes accessed | tf_op | source)
XLA Modules:
  0.0 40.6 jit_solution(6802796428704878797)
XLA Ops:
  0.6 0.5 %collective-permute-start.3 = (bf16[1024,768]{1,0:T(8,128)(2,1)}, bf16[1024,768]{1,0:T(8,128)(2,1)S(1)}, u32[]{:S(2)}, u32[]{:S(2)}) collective-permute-start(bf16[1024,768]{1,0:T(8,128)(2,1)} %bitcast.1), channel_id=1, source_target_pairs={{0,2},{1,3},{2,0},{3,1},{4,6},{5,7},{6,4},{7,5},{8,10},{9,11},{10,... | collective-permute-start | bytes 4718600 | tf_op jit(solution)/shard_map/ppermute | solution.py:27
  1.1 2.6 %collective-permute-start.1 = (bf16[64,768]{1,0:T(8,128)(2,1)}, bf16[64,768]{1,0:T(8,128)(2,1)S(1)}, u32[]{:S(2)}, u32[]{:S(2)}) collective-permute-start(bf16[64,768]{1,0:T(8,128)(2,1)} %param.7), channel_id=1, source_target_pairs={{0,8},{1,9},{2,10},{3,11},{4,12},{5,13},{6,14},{7,15},{8,0},{9,1},... | collective-permute-start | bytes 294920 | tf_op jit(solution)/shard_map/ppermute | solution.py:27
  3.8 2.6 %collective-permute-start = (bf16[64,768]{1,0:T(8,128)(2,1)}, bf16[64,768]{1,0:T(8,128)(2,1)S(1)}, u32[]{:S(2)}, u32[]{:S(2)}) collective-permute-start(bf16[64,768]{1,0:T(8,128)(2,1)} %param.7), channel_id=1, source_target_pairs={{0,16},{1,17},{2,18},{3,19},{4,20},{5,21},{6,22},{7,23},{8,24},{9,... | collective-permute-start | bytes 294920 | tf_op jit(solution)/shard_map/ppermute | solution.py:27
  6.4 1.4 %copy-done = bf16[16,64,768]{2,1,0:T(8,128)(2,1)S(1)} copy-done((bf16[16,64,768]{2,1,0:T(8,128)(2,1)S(1)}, bf16[16,64,768]{2,1,0:T(8,128)(2,1)}, u32[]{:S(2)}) %copy-start) | copy-done | bytes 1572888
  7.8 1.0 %line_norms.1.refs_4_ = f32[8,1024]{1,0:T(8,128)S(1)} custom-call(bf16[1024,768]{1,0:T(8,128)(2,1)S(1)} %bitcast.2), custom_call_target="tpu_custom_call" | custom-call | flops 201326592 | bytes 1572864 | tf_op jit(solution)/shard_map/line_norms/pallas_call | solution.py:42
  8.8 0.0 collective-permute-done.1
  8.8 0.0 copy-done.2
  8.9 3.0 %collective-permute-done = bf16[64,768]{1,0:T(8,128)(2,1)S(1)} collective-permute-done((bf16[64,768]{1,0:T(8,128)(2,1)}, bf16[64,768]{1,0:T(8,128)(2,1)S(1)}, u32[]{:S(2)}, u32[]{:S(2)}) %collective-permute-start) | collective-permute-done | bytes 98336 | tf_op jit(solution)/shard_map/ppermute | solution.py:27
  11.9 0.5 %collective-permute-start.2 = (bf16[64,768]{1,0:T(8,128)(2,1)S(1)}, bf16[64,768]{1,0:T(8,128)(2,1)S(1)}, u32[]{:S(2)}, u32[]{:S(2)}) collective-permute-start(bf16[64,768]{1,0:T(8,128)(2,1)S(1)} %collective-permute-done), channel_id=1, source_target_pairs={{0,8},{1,9},{2,10},{3,11},{4,12},{5,13},{6,14},{7,15},{8,0},{9,1},... | collective-permute-start | bytes 294920 | tf_op jit(solution)/shard_map/ppermute | solution.py:27
  12.4 1.5 %collective-permute-start.8 = (bf16[128,768]{1,0:T(8,128)(2,1)S(1)}, bf16[128,768]{1,0:T(8,128)(2,1)S(1)}, u32[]{:S(2)}, u32[]{:S(2)}) collective-permute-start(bf16[128,768]{1,0:T(8,128)(2,1)S(1)} %pad_maximum_fusion.refs_2_), channel_id=1, source_target_pairs={{0,1},{1,0},{2,6},{3,7},{4,5},{5,4},{6,2},{7,3},{8,9},{9,8},{10,14... | collective-permute-start | bytes 589832 | tf_op jit(solution)/shard_map/ppermute | solution.py:27
  13.9 2.6 %collective-permute-done.2 = bf16[64,768]{1,0:T(8,128)(2,1)S(1)} collective-permute-done((bf16[64,768]{1,0:T(8,128)(2,1)S(1)}, bf16[64,768]{1,0:T(8,128)(2,1)S(1)}, u32[]{:S(2)}, u32[]{:S(2)}) %collective-permute-start.2) | collective-permute-done | bytes 98336 | tf_op jit(solution)/shard_map/ppermute | solution.py:27
  16.5 0.0 collective-permute-done.3.refs_1_
  16.6 1.1 %absorb.4 = (f32[16,1024]{1,0:T(8,128)S(1)}, f32[16,1024]{1,0:T(8,128)S(1)}) custom-call(bf16[1024,768]{1,0:T(8,128)(2,1)S(1)} %bitcast.3, bf16[1024,768]{1,0:T(8,128)(2,1)S(1)} %collective-permute-done.3.refs_1_, bf16[128,768]{1,0:T(8,128)(2,1)S(1)} %pad_maximum_fusion.refs_2_, ...), custom_call_target="tpu_custom_call", output_to_operand_aliasing={{0}: (3, {}), {1}: (4, {})} | custom-call | flops 402653184 | bytes 3473408 | tf_op jit(solution)/shard_map/absorb/pallas_call | solution.py:42
  17.7 1.6 %collective-permute-start.4 = (bf16[128,768]{1,0:T(8,128)(2,1)S(1)}, bf16[128,768]{1,0:T(8,128)(2,1)S(1)}, u32[]{:S(2)}, u32[]{:S(2)}) collective-permute-start(bf16[128,768]{1,0:T(8,128)(2,1)S(1)} %pad_maximum_fusion.1.refs_3_), channel_id=1, source_target_pairs={{0,1},{1,0},{2,6},{3,7},{4,5},{5,4},{6,2},{7,3},{8,9},{9,8},{10,14... | collective-permute-start | bytes 589832 | tf_op jit(solution)/shard_map/ppermute | solution.py:27
  19.3 1.5 %collective-permute-start.7 = (bf16[128,768]{1,0:T(8,128)(2,1)S(1)}, bf16[128,768]{1,0:T(8,128)(2,1)S(1)}, u32[]{:S(2)}, u32[]{:S(2)}) collective-permute-start(bf16[128,768]{1,0:T(8,128)(2,1)S(1)} %pad_maximum_fusion.refs_2_), channel_id=1, source_target_pairs={{0,4},{1,5},{2,3},{3,2},{4,0},{5,1},{6,7},{7,6},{8,12},{9,13},{10,... | collective-permute-start | bytes 589832 | tf_op jit(solution)/shard_map/ppermute | solution.py:27
  20.8 0.0 collective-permute-done.8.refs_2_
  20.8 0.5 %collective-permute-start.9 = (bf16[128,768]{1,0:T(8,128)(2,1)S(1)}, bf16[128,768]{1,0:T(8,128)(2,1)S(1)}, u32[]{:S(2)}, u32[]{:S(2)}) collective-permute-start(bf16[128,768]{1,0:T(8,128)(2,1)S(1)} %collective-permute-done.8.refs_2_), channel_id=1, source_target_pairs={{0,4},{1,5},{2,3},{3,2},{4,0},{5,1},{6,7},{7,6},{8,12},{9,13},{10,... | collective-permute-start | bytes 589832 | tf_op jit(solution)/shard_map/ppermute | solution.py:27
  21.3 1.5 %collective-permute-start.6 = (bf16[128,768]{1,0:T(8,128)(2,1)S(1)}, bf16[128,768]{1,0:T(8,128)(2,1)S(1)}, u32[]{:S(2)}, u32[]{:S(2)}) collective-permute-start(bf16[128,768]{1,0:T(8,128)(2,1)S(1)} %pad_maximum_fusion.1.refs_3_), channel_id=1, source_target_pairs={{0,4},{1,5},{2,3},{3,2},{4,0},{5,1},{6,7},{7,6},{8,12},{9,13},{10,... | collective-permute-start | bytes 589832 | tf_op jit(solution)/shard_map/ppermute | solution.py:27
  22.8 2.8 %collective-permute-done.4.refs_2_ = bf16[128,768]{1,0:T(8,128)(2,1)S(1)} collective-permute-done((bf16[128,768]{1,0:T(8,128)(2,1)S(1)}, bf16[128,768]{1,0:T(8,128)(2,1)S(1)}, u32[]{:S(2)}, u32[]{:S(2)}) %collective-permute-start.4) | collective-permute-done | bytes 196640 | tf_op jit(solution)/shard_map/ppermute | solution.py:27
  25.6 1.5 %collective-permute-start.5 = (bf16[128,768]{1,0:T(8,128)(2,1)S(1)}, bf16[128,768]{1,0:T(8,128)(2,1)S(1)}, u32[]{:S(2)}, u32[]{:S(2)}) collective-permute-start(bf16[128,768]{1,0:T(8,128)(2,1)S(1)} %collective-permute-done.4.refs_2_), channel_id=1, source_target_pairs={{0,4},{1,5},{2,3},{3,2},{4,0},{5,1},{6,7},{7,6},{8,12},{9,13},{10,... | collective-permute-start | bytes 589832 | tf_op jit(solution)/shard_map/ppermute | solution.py:27
  27.1 1.1 %absorb.5 = (f32[16,1024]{1,0:T(8,128)S(1)}, f32[16,1024]{1,0:T(8,128)S(1)}) custom-call(bf16[1024,768]{1,0:T(8,128)(2,1)S(1)} %bitcast.4, bf16[1024,768]{1,0:T(8,128)(2,1)S(1)} %collective-permute-done.3.refs_1_, bf16[128,768]{1,0:T(8,128)(2,1)S(1)} %collective-permute-done.8.refs_2_, ...), custom_call_target="tpu_custom_call", output_to_operand_aliasing={{0}: (4, {}), {1}: (5, {})} | custom-call | flops 805306368 | bytes 3670016 | tf_op jit(solution)/shard_map/absorb/pallas_call | solution.py:42
  28.3 0.0 collective-permute-done.7.refs_2_
  28.3 1.1 %absorb.6 = (f32[16,1024]{1,0:T(8,128)S(1)}, f32[16,1024]{1,0:T(8,128)S(1)}) custom-call(bf16[1024,768]{1,0:T(8,128)(2,1)S(1)} %bitcast.5, bf16[1024,768]{1,0:T(8,128)(2,1)S(1)} %collective-permute-done.3.refs_1_, bf16[128,768]{1,0:T(8,128)(2,1)S(1)} %collective-permute-done.7.refs_2_, ...), custom_call_target="tpu_custom_call", output_to_operand_aliasing={{0}: (4, {}), {1}: (5, {})} | custom-call | flops 805306368 | bytes 3670016 | tf_op jit(solution)/shard_map/absorb/pallas_call | solution.py:42
  29.4 0.0 copy-start.1
  29.4 1.1 %absorb.7 = (f32[16,1024]{1,0:T(8,128)S(1)}, f32[16,1024]{1,0:T(8,128)S(1)}) custom-call(bf16[1024,768]{1,0:T(8,128)(2,1)S(1)} %bitcast.6, bf16[1024,768]{1,0:T(8,128)(2,1)S(1)} %collective-permute-done.3.refs_1_, bf16[128,768]{1,0:T(8,128)(2,1)S(1)} %collective-permute-done.4.refs_2_, ...), custom_call_target="tpu_custom_call", output_to_operand_aliasing={{0}: (4, {}), {1}: (5, {})} | custom-call | flops 805306368 | bytes 3670016 | tf_op jit(solution)/shard_map/absorb/pallas_call | solution.py:42
  30.6 0.7 %collective-permute-done.5.refs_0_ = bf16[128,768]{1,0:T(8,128)(2,1)S(1)} collective-permute-done((bf16[128,768]{1,0:T(8,128)(2,1)S(1)}, bf16[128,768]{1,0:T(8,128)(2,1)S(1)}, u32[]{:S(2)}, u32[]{:S(2)}) %collective-permute-start.5) | collective-permute-done | bytes 196640 | tf_op jit(solution)/shard_map/ppermute | solution.py:27
  31.3 0.5 %collective-permute-start.11 = (f32[16,1024]{1,0:T(8,128)S(1)}, f32[16,1024]{1,0:T(8,128)S(1)}, u32[]{:S(2)}, u32[]{:S(2)}) collective-permute-start(f32[16,1024]{1,0:T(8,128)S(1)} %get-tuple-element.38), channel_id=1, source_target_pairs={{0,2},{1,3},{2,0},{3,1},{4,6},{5,7},{6,4},{7,5},{8,10},{9,11},{10,... | collective-permute-start | bytes 196616 | tf_op jit(solution)/shard_map/ppermute | solution.py:27
  32.5 0.4 collective-permute-done.11.refs_3_
  32.8 1.3 %last.1 = (f32[2,8,64]{2,1,0:T(8,128)S(1)}, f32[2,8,64]{2,1,0:T(8,128)S(1)}) custom-call(s32[1]{0:T(128)S(6)} %copy.22.count_ref, s32[16]{0:T(128)S(1)} %copy-done.1, bf16[1024,768]{1,0:T(8,128)(2,1)S(1)} %bitcast.7, bf16[128,768]{1,0:T(8,128)(2,1)S(1)} %collective-permute-done.5.refs_0_, bf16[128,768]{1,0:T(8,128)(2,1)S(1)} %collective-permute-done.10.refs_1_, ...), custom_call_target="tpu_custom_call" | custom-call | flops 402653184 | bytes 2129988 | tf_op jit(solution)/shard_map/last/pallas_call | solution.py:42
  34.1 0.3 collective-permute-start.12
  34.4 5.5 %collective-permute-done.12.arrived_ref = f32[2,8,64]{2,1,0:T(8,128)S(1)} collective-permute-done((f32[2,8,64]{2,1,0:T(8,128)S(1)}, f32[2,8,64]{2,1,0:T(8,128)S(1)}, u32[]{:S(2)}, u32[]{:S(2)}) %collective-permute-start.12) | collective-permute-done | bytes 4128 | tf_op jit(solution)/shard_map/ppermute | solution.py:27
  40.0 0.6 %final.1 = (f32[8,64]{1,0:T(8,128)}, f32[8,64]{1,0:T(8,128)}) custom-call(f32[2,8,64]{2,1,0:T(8,128)S(1)} %get-tuple-element.40.keep_ref, f32[2,8,64]{2,1,0:T(8,128)S(1)} %collective-permute-done.12.arrived_ref), custom_call_target="tpu_custom_call" | custom-call | bytes 8192 | tf_op jit(solution)/shard_map/final/pallas_call | solution.py:42
  (11 shorter events, 0.1 us)
Async XLA Ops:
  0.6 15.9 %collective-permute-start.3 = (bf16[1024,768]{1,0:T(8,128)(2,1)}, bf16[1024,768]{1,0:T(8,128)(2,1)S(1)}, u32[]{:S(2)}, u32[]{:S(2)}) collective-permute-start(bf16[1024,768]{1,0:T(8,128)(2,1)} %bitcast.1), channel_id=1, source_target_pairs={{0,2},{1,3},{2,0},{3,1},{4,6},{5,7},{6,4},{7,5},{8,10},{9,11},{10,... | collective-permute-start | bytes 4718600 | tf_op jit(solution)/shard_map/ppermute | solution.py:27
  1.1 7.7 %collective-permute-start.1 = (bf16[64,768]{1,0:T(8,128)(2,1)}, bf16[64,768]{1,0:T(8,128)(2,1)S(1)}, u32[]{:S(2)}, u32[]{:S(2)}) collective-permute-start(bf16[64,768]{1,0:T(8,128)(2,1)} %param.7), channel_id=1, source_target_pairs={{0,8},{1,9},{2,10},{3,11},{4,12},{5,13},{6,14},{7,15},{8,0},{9,1},... | collective-permute-start | bytes 294920 | tf_op jit(solution)/shard_map/ppermute | solution.py:27
  3.8 8.1 %collective-permute-start = (bf16[64,768]{1,0:T(8,128)(2,1)}, bf16[64,768]{1,0:T(8,128)(2,1)S(1)}, u32[]{:S(2)}, u32[]{:S(2)}) collective-permute-start(bf16[64,768]{1,0:T(8,128)(2,1)} %param.7), channel_id=1, source_target_pairs={{0,16},{1,17},{2,18},{3,19},{4,20},{5,21},{6,22},{7,23},{8,24},{9,... | collective-permute-start | bytes 294920 | tf_op jit(solution)/shard_map/ppermute | solution.py:27
  6.4 1.4 %copy-start = (bf16[16,64,768]{2,1,0:T(8,128)(2,1)S(1)}, bf16[16,64,768]{2,1,0:T(8,128)(2,1)}, u32[]{:S(2)}) copy-start(bf16[16,64,768]{2,1,0:T(8,128)(2,1)} %param.4) | copy-start | bytes 4718596
  7.8 1.0 %copy-start.2 = (bf16[64,768]{1,0:T(8,128)(2,1)S(1)}, bf16[64,768]{1,0:T(8,128)(2,1)}, u32[]{:S(2)}) copy-start(bf16[64,768]{1,0:T(8,128)(2,1)} %param.7) | copy-start | bytes 294916
  11.9 4.6 %collective-permute-start.2 = (bf16[64,768]{1,0:T(8,128)(2,1)S(1)}, bf16[64,768]{1,0:T(8,128)(2,1)S(1)}, u32[]{:S(2)}, u32[]{:S(2)}) collective-permute-start(bf16[64,768]{1,0:T(8,128)(2,1)S(1)} %collective-permute-done), channel_id=1, source_target_pairs={{0,8},{1,9},{2,10},{3,11},{4,12},{5,13},{6,14},{7,15},{8,0},{9,1},... | collective-permute-start | bytes 294920 | tf_op jit(solution)/shard_map/ppermute | solution.py:27
  12.4 8.4 %collective-permute-start.8 = (bf16[128,768]{1,0:T(8,128)(2,1)S(1)}, bf16[128,768]{1,0:T(8,128)(2,1)S(1)}, u32[]{:S(2)}, u32[]{:S(2)}) collective-permute-start(bf16[128,768]{1,0:T(8,128)(2,1)S(1)} %pad_maximum_fusion.refs_2_), channel_id=1, source_target_pairs={{0,1},{1,0},{2,6},{3,7},{4,5},{5,4},{6,2},{7,3},{8,9},{9,8},{10,14... | collective-permute-start | bytes 589832 | tf_op jit(solution)/shard_map/ppermute | solution.py:27
  17.7 7.9 %collective-permute-start.4 = (bf16[128,768]{1,0:T(8,128)(2,1)S(1)}, bf16[128,768]{1,0:T(8,128)(2,1)S(1)}, u32[]{:S(2)}, u32[]{:S(2)}) collective-permute-start(bf16[128,768]{1,0:T(8,128)(2,1)S(1)} %pad_maximum_fusion.1.refs_3_), channel_id=1, source_target_pairs={{0,1},{1,0},{2,6},{3,7},{4,5},{5,4},{6,2},{7,3},{8,9},{9,8},{10,14... | collective-permute-start | bytes 589832 | tf_op jit(solution)/shard_map/ppermute | solution.py:27
  19.3 9.0 %collective-permute-start.7 = (bf16[128,768]{1,0:T(8,128)(2,1)S(1)}, bf16[128,768]{1,0:T(8,128)(2,1)S(1)}, u32[]{:S(2)}, u32[]{:S(2)}) collective-permute-start(bf16[128,768]{1,0:T(8,128)(2,1)S(1)} %pad_maximum_fusion.refs_2_), channel_id=1, source_target_pairs={{0,4},{1,5},{2,3},{3,2},{4,0},{5,1},{6,7},{7,6},{8,12},{9,13},{10,... | collective-permute-start | bytes 589832 | tf_op jit(solution)/shard_map/ppermute | solution.py:27
  20.8 7.5 %collective-permute-start.9 = (bf16[128,768]{1,0:T(8,128)(2,1)S(1)}, bf16[128,768]{1,0:T(8,128)(2,1)S(1)}, u32[]{:S(2)}, u32[]{:S(2)}) collective-permute-start(bf16[128,768]{1,0:T(8,128)(2,1)S(1)} %collective-permute-done.8.refs_2_), channel_id=1, source_target_pairs={{0,4},{1,5},{2,3},{3,2},{4,0},{5,1},{6,7},{7,6},{8,12},{9,13},{10,... | collective-permute-start | bytes 589832 | tf_op jit(solution)/shard_map/ppermute | solution.py:27
  21.3 8.1 %collective-permute-start.6 = (bf16[128,768]{1,0:T(8,128)(2,1)S(1)}, bf16[128,768]{1,0:T(8,128)(2,1)S(1)}, u32[]{:S(2)}, u32[]{:S(2)}) collective-permute-start(bf16[128,768]{1,0:T(8,128)(2,1)S(1)} %pad_maximum_fusion.1.refs_3_), channel_id=1, source_target_pairs={{0,4},{1,5},{2,3},{3,2},{4,0},{5,1},{6,7},{7,6},{8,12},{9,13},{10,... | collective-permute-start | bytes 589832 | tf_op jit(solution)/shard_map/ppermute | solution.py:27
  25.6 5.7 %collective-permute-start.5 = (bf16[128,768]{1,0:T(8,128)(2,1)S(1)}, bf16[128,768]{1,0:T(8,128)(2,1)S(1)}, u32[]{:S(2)}, u32[]{:S(2)}) collective-permute-start(bf16[128,768]{1,0:T(8,128)(2,1)S(1)} %collective-permute-done.4.refs_2_), channel_id=1, source_target_pairs={{0,4},{1,5},{2,3},{3,2},{4,0},{5,1},{6,7},{7,6},{8,12},{9,13},{10,... | collective-permute-start | bytes 589832 | tf_op jit(solution)/shard_map/ppermute | solution.py:27
  29.4 3.4 %copy-start.1 = (s32[16]{0:T(128)S(1)}, s32[16]{0:T(128)}, u32[]{:S(2)}) copy-start(s32[16]{0:T(128)} %to_ref.1) | copy-start | bytes 196
  31.3 1.5 %collective-permute-start.10 = (bf16[128,768]{1,0:T(8,128)(2,1)S(1)}, bf16[128,768]{1,0:T(8,128)(2,1)S(1)}, u32[]{:S(2)}, u32[]{:S(2)}) collective-permute-start(bf16[128,768]{1,0:T(8,128)(2,1)S(1)} %collective-permute-done.5.refs_0_), channel_id=1, source_target_pairs={{0,2},{1,3},{2,0},{3,1},{4,6},{5,7},{6,4},{7,5},{8,10},{9,11},{10,... | collective-permute-start | bytes 589832 | tf_op jit(solution)/shard_map/ppermute | solution.py:27
  31.3 1.5 %collective-permute-start.11 = (f32[16,1024]{1,0:T(8,128)S(1)}, f32[16,1024]{1,0:T(8,128)S(1)}, u32[]{:S(2)}, u32[]{:S(2)}) collective-permute-start(f32[16,1024]{1,0:T(8,128)S(1)} %get-tuple-element.38), channel_id=1, source_target_pairs={{0,2},{1,3},{2,0},{3,1},{4,6},{5,7},{6,4},{7,5},{8,10},{9,11},{10,... | collective-permute-start | bytes 196616 | tf_op jit(solution)/shard_map/ppermute | solution.py:27
  34.1 5.8 %collective-permute-start.12 = (f32[2,8,64]{2,1,0:T(8,128)S(1)}, f32[2,8,64]{2,1,0:T(8,128)S(1)}, u32[]{:S(2)}, u32[]{:S(2)}) collective-permute-start(f32[2,8,64]{2,1,0:T(8,128)S(1)} %get-tuple-element.41), channel_id=1, source_target_pairs={{0,2},{1,3},{2,4},{3,5},{4,6},{5,7},{6,8},{7,9},{8,10},{9,11},{10,... | collective-permute-start | bytes 12296 | tf_op jit(solution)/shard_map/ppermute | solution.py:27

commit v3 on v2

--- a/solution.py
+++ b/solution.py
@@ -23,6 +23,8 @@
     for host in range(hosts):
         for column in range(columns):
             to = target(host, column)
+            if to is None:
+                continue
             route.append((host * columns + column, to[0] % hosts * columns + to[1]))
     return lax.ppermute(value, AXES, route)
 
@@ -148,69 +150,100 @@
     )
 
 
-def last_kernel(slots, places, block_rows, bank_count, count_ref, to_ref, lines_ref, *refs):
-    bank_refs, refs = refs[:bank_count], refs[bank_count:]
-    mine_ref, returned_ref, norms_ref, keep_ref, send_ref, placed_ref = refs
+def last_kernel(parity, places, block_rows, count_ref, to_ref, lines_ref, *refs):
+    bank_refs, refs = refs[:2], refs[2:]
+    mine_ref, returned_ref, norms_ref, _, keep_ref, send_ref, placed_ref = refs
     lines, features = lines_ref.shape
+    slots = to_ref.shape[0]
     per_slot = lines // slots
-    hosts = lax.axis_size("line")
     host = lax.axis_index("line")
-    following = lax.rem(host + 1, hosts)
-    first, second = join(
-        mine_ref[:SUBLANES], mine_ref[SUBLANES:], returned_ref[:SUBLANES], returned_ref[SUBLANES:]
-    )
-    for group in tiles(bank_refs):
-        banks = [ref[row : row + tile, :] for ref, row, tile in group]
-        first, second = absorbed(banks, lines_ref[...], first, second)
-    lowest, runner = first[:1], second[:1]
-    for row in range(1, SUBLANES):
-        lowest, runner = join(lowest, runner, first[row : row + 1], second[row : row + 1])
-    both = [(value + norms_ref[:1]) / features for value in (lowest, runner)]
-    placed_ref[...] = jnp.full(placed_ref.shape, HUGE_DISTANCE, jnp.float32)
-    for slot in range(slots):
-        usable = slot * block_rows < count_ref[0]
-        here = to_ref[slot] - host * places
-        there = to_ref[slot] - following * places
-        row = jnp.where(jnp.logical_and(there >= 0, there < places), places + there, 2 * places)
-        row = jnp.where(jnp.logical_and(here >= 0, here < places), here, row)
-        row = jnp.where(usable, row, 2 * places)
-        for index, value in enumerate(both):
-            placed_ref[index, pl.ds(row, 1), :] = value[:, slot * per_slot : (slot + 1) * per_slot]
-    keep_ref[...] = placed_ref[:, :places]
-    send_ref[...] = placed_ref[:, places : 2 * places]
-
-
-def last(line_counts, destinations, own, banks, mine, returned, norms, places, block_rows):
-    slots = destinations.shape[0]
+
+    @pl.when(lax.rem(host, 2) == parity)
+    def work():
+        following = lax.rem(host + 1, lax.axis_size("line"))
+        first, second = join(
+            mine_ref[:SUBLANES],
+            mine_ref[SUBLANES:],
+            returned_ref[:SUBLANES],
+            returned_ref[SUBLANES:],
+        )
+        for group in tiles(bank_refs):
+            banks = [ref[row : row + tile, :] for ref, row, tile in group]
+            first, second = absorbed(banks, lines_ref[...], first, second)
+        lowest, runner = first[:1], second[:1]
+        for row in range(1, SUBLANES):
+            lowest, runner = join(lowest, runner, first[row : row + 1], second[row : row + 1])
+        both = [(value + norms_ref[:1]) / features for value in (lowest, runner)]
+        placed_ref[...] = jnp.full(placed_ref.shape, HUGE_DISTANCE, jnp.float32)
+        for slot in range(slots):
+            usable = slot * block_rows < count_ref[0]
+            here = to_ref[slot] - host * places
+            there = to_ref[slot] - following * places
+            row = jnp.where(jnp.logical_and(there >= 0, there < places), places + there, 2 * places)
+            row = jnp.where(jnp.logical_and(here >= 0, here < places), here, row)
+            row = jnp.where(usable, row, 2 * places)
+            for index, value in enumerate(both):
+                placed_ref[index, pl.ds(row, 1), :] = value[:, slot * per_slot : (slot + 1) * per_slot]
+        keep_ref[...] = placed_ref[:, :places]
+        send_ref[...] = placed_ref[:, places : 2 * places]
+
+
+def last(parity, keep, line_counts, destinations, own, banks, mine, returned, norms, block_rows):
     lines, features = own.shape
-    per_slot = lines // slots
-    operands = (line_counts, destinations, own, *banks, mine, returned, norms)
-    placed = jax.ShapeDtypeStruct((2, places, per_slot), jnp.float32)
+    places, per_slot = keep.shape[1:]
+    operands = (line_counts, destinations, own, *banks, mine, returned, norms, keep)
+    placed = jax.ShapeDtypeStruct(keep.shape, keep.dtype)
     return call(
-        functools.partial(last_kernel, slots, places, block_rows, len(banks)),
+        functools.partial(last_kernel, parity, places, block_rows),
         (placed, placed),
         operands,
         (SMEM, SMEM) + (VMEM,) * (len(operands) - 2),
         2 * lines * features * sum(bank.shape[0] for bank in banks),
         scratch=(pltpu.VMEM((2, 2 * places + SUBLANES, per_slot), jnp.float32),),
+        aliases={len(operands) - 1: 0},
         name="last",
     )
 
 
-def final_kernel(keep_ref, arrived_ref, nearest_ref, runner_ref):
+def merge_kernel(placed_ref, arrived_ref, out_ref):
+    @pl.when(lax.rem(lax.axis_index("line"), 2) == 0)
+    def merge():
+        out_ref[...] = jnp.minimum(placed_ref[...], arrived_ref[...])
+
+
+def merged(placed, arrived):
+    out = jax.ShapeDtypeStruct(placed.shape, placed.dtype)
+    return call(
+        merge_kernel, (out,), (placed, arrived), (VMEM,) * 2, 10**9, aliases={0: 0}, name="merged"
+    )[0]
+
+
+def final_kernel(placed_ref, arrived_ref, nearest_ref, runner_ref):
+    even = lax.rem(lax.axis_index("line"), 2) == 0
     for index, ref in enumerate((nearest_ref, runner_ref)):
-        ref[...] = jnp.minimum(keep_ref[index], arrived_ref[index])
-
-
-def final(keep, arrived):
-    out = jax.ShapeDtypeStruct(keep.shape[1:], keep.dtype)
-    return call(final_kernel, (out, out), (keep, arrived), (VMEM, VMEM), name="final")
-
-
-def doubled(piece, bits):
+
+        @pl.when(even)
+        def ready(index=index, ref=ref):
+            ref[...] = placed_ref[index]
+
+        @pl.when(jnp.logical_not(even))
+        def merge(index=index, ref=ref):
+            ref[...] = jnp.minimum(placed_ref[index], arrived_ref[index])
+
+
+def final(placed, arrived):
+    out = jax.ShapeDtypeStruct(placed.shape[1:], placed.dtype)
+    return call(final_kernel, (out, out), (placed, arrived), (VMEM,) * 2, name="final")
+
+
+def stacked(pieces):
+    return jnp.concatenate(pieces, axis=0) if len(pieces) > 1 else pieces[0]
+
+
+def doubled(pieces, bits):
     for axis, bit in bits:
-        piece = jnp.concatenate([piece, moved(piece, across(axis, bit))], axis=0)
-    return piece
+        pieces = [*pieces, moved(stacked(pieces), across(axis, bit))]
+    return pieces
 
 
 def shards(line_blocks, line_counts, destinations, centroids):
@@ -224,44 +257,49 @@
 
     far = [("line", bit) for bit in range(2, hosts.bit_length() - 1)]
     far += [("centroid", bit) for bit in range(1, columns.bit_length() - 1)]
-    distant = moved(centroids, across(*far[-1]))
-    norms = line_norms(own)
     by_line, by_column = across("line", 1), across("centroid", 0)
     turned, straight = by_parity(by_line, by_column), by_parity(by_column, by_line)
 
-    held_a = doubled(centroids, far[:-1])
-    held_a, norms = lax.optimization_barrier((held_a, norms))
-    near_a = moved(held_a, straight)
-    distant, held_late = lax.optimization_barrier((distant, held_a))
-    held_b = doubled(distant, far[:-1])
-    side_a = moved(held_late, turned)
-
+    distant = moved(centroids, across(*far[-1]))
+    level = doubled([centroids], far[:-1])[1:]
+    near = moved(centroids, straight)
+    side = moved(centroids, turned)
+    distant, near, side = lax.optimization_barrier((distant, near, side))
+    beyond = doubled([distant], far[:-1])[1:]
+    norms = line_norms(own)
+    beyond, norms = lax.optimization_barrier((beyond, norms))
+    near_level = moved(stacked([*level, distant]), straight)
+    near_beyond = moved(stacked(beyond), straight)
+    crossed_level = moved(stacked([near, *level, distant, *beyond]), turned)
+    crossed_beyond = moved(stacked([near_level, near_beyond]), turned)
+
+    lines = (own, partner)
     empty = jnp.full((2 * SUBLANES, own.shape[0]), HUGE_DISTANCE, jnp.float32)
-    states = absorb((empty, empty), (held_late,), (own, partner))
-    held_b, states = lax.optimization_barrier((held_b, states))
-    corner_a = moved(near_a, turned)
-    near_b = moved(held_b, straight)
-    side_b = moved(held_b, turned)
-    corner_b = moved(near_b, turned)
-    states = absorb(states, (near_a, held_b), (own, partner))
-    states = absorb(states, (side_a, corner_a), (own, partner))
-    states = absorb(states, (near_b, side_b), (own, partner))
-    corner_b, states = lax.optimization_barrier((corner_b, states))
-    returned = moved(states[1], partner_of)
-    shared = moved(corner_b, partner_of)
-    keep, send = last(
-        line_counts,
-        destinations,
-        own,
-        (corner_b, shared),
-        states[0],
-        returned,
-        norms,
-        places,
-        block_rows,
-    )
-    arrived = moved(send, lambda host, column: (host + 1, column))
-    return tuple(final(keep, arrived))
+    states = absorb((empty, empty), (centroids, near, side, *level), lines)
+    states = absorb(states, (distant, near_level, *beyond), lines)
+    mine, theirs = absorb(states, (near_beyond, crossed_level), lines)
+    returned = moved(theirs, partner_of)
+    crossed_beyond, mine = lax.optimization_barrier((crossed_beyond, mine))
+    banks = (crossed_beyond, moved(crossed_beyond, partner_of))
+
+    placed = jnp.zeros((2, places, sub_rows), jnp.float32)
+    sends = [None, None]
+    for parity in (1, 0):
+        placed, sends[parity] = last(
+            parity,
+            placed,
+            line_counts,
+            destinations,
+            own,
+            banks,
+            mine,
+            returned,
+            norms,
+            block_rows,
+        )
+    to_even = moved(sends[1], lambda host, column: (host + 1, column))
+    to_odd = moved(sends[0], partner_of)
+    return tuple(final(merged(placed, to_even), to_odd))
 
 
 def solution(mesh):

time: 40.7 us -> 37.7 us (0.926)
  waiting for transfers between devices: 15.1 us -> 10.6 us
  starting transfers between devices: 15.1 us -> 16.8 us
    ppermute x13 -> x14, waiting for transfers between devices: 15.1 us -> 10.6 us  [moved(): return lax.ppermute(value, AXES, route)]
    ppermute x13 -> x14, starting transfers between devices: 15.1 us -> 16.8 us  [moved(): return lax.ppermute(value, AXES, route)]
    pallas_call x7 -> x8, Pallas kernels: 7.42 us -> 7.3 us  [call(): pl.pallas_call(body, in_specs=list(spaces), out_specs=(VMEM,) * len(outs)...]
  transfers between devices with their start and end apart: 13 -> 14, of which waited for: 6 -> 6; matrix products, arithmetic and copies ran while one was open for 0% -> 0% of each run, Pallas kernels for 14% -> 16%
where the time goes in v3:
time: 37.7 us; the launch traced here: 37.6 us
  starting transfers between devices  16.8 us (45%)
  waiting for transfers between devices  10.6 us (28%)
  Pallas kernels  7.3 us (19%)
  local copies, waits for them, and re-layouts  1.43 us (4%)
  between operations  1.39 us (4%)
    ppermute x14, starting transfers between devices, moved(): return lax.ppermute(value, AXES, route)  16.8 us
    ppermute x14, waiting for transfers between devices, moved(): return lax.ppermute(value, AXES, route)  10.6 us
    pallas_call x8, Pallas kernels, call(): pl.pallas_call(body, in_specs=list(spaces), out_specs=(VMEM,) * len(outs)...  7.3 us
    unnamed x6, local copies, waits for them, and re-layouts  1.42 us
  transfers between devices with their start and end apart: 14, of which 6 were waited for; matrix products, arithmetic and copies ran while one was open for 0% of the time, Pallas kernels for 16%

profile of v3, /device:TPU:0, one launch (start us, length us, event | category | flops | bytes accessed | tf_op | source)
XLA Modules:
  0.0 37.6 jit_solution(17292858126520797283)
XLA Ops:
  0.6 0.5 %collective-permute-start.8 = (bf16[1024,768]{1,0:T(8,128)(2,1)}, bf16[1024,768]{1,0:T(8,128)(2,1)S(1)}, u32[]{:S(2)}, u32[]{:S(2)}) collective-permute-start(bf16[1024,768]{1,0:T(8,128)(2,1)} %bitcast.1), channel_id=1, source_target_pairs={{0,2},{1,3},{2,0},{3,1},{4,6},{5,7},{6,4},{7,5},{8,10},{9,11},{10,... | collective-permute-start | bytes 4718600 | tf_op jit(solution)/shard_map/ppermute | solution.py:29
  1.1 3.7 %collective-permute-start.1 = (bf16[64,768]{1,0:T(8,128)(2,1)}, bf16[64,768]{1,0:T(8,128)(2,1)S(1)}, u32[]{:S(2)}, u32[]{:S(2)}) collective-permute-start(bf16[64,768]{1,0:T(8,128)(2,1)} %refs_2_.1), channel_id=1, source_target_pairs={{0,16},{1,17},{2,18},{3,19},{4,20},{5,21},{6,22},{7,23},{8,24},{9,... | collective-permute-start | bytes 294920 | tf_op jit(solution)/shard_map/ppermute | solution.py:29
  4.8 1.5 %collective-permute-start.2 = (bf16[64,768]{1,0:T(8,128)(2,1)}, bf16[64,768]{1,0:T(8,128)(2,1)S(1)}, u32[]{:S(2)}, u32[]{:S(2)}) collective-permute-start(bf16[64,768]{1,0:T(8,128)(2,1)} %refs_2_.1), channel_id=1, source_target_pairs={{0,1},{1,0},{2,6},{3,7},{4,5},{5,4},{6,2},{7,3},{8,9},{9,8},{10,14... | collective-permute-start | bytes 294920 | tf_op jit(solution)/shard_map/ppermute | solution.py:29
  6.3 1.5 %collective-permute-start.3 = (bf16[64,768]{1,0:T(8,128)(2,1)}, bf16[64,768]{1,0:T(8,128)(2,1)S(1)}, u32[]{:S(2)}, u32[]{:S(2)}) collective-permute-start(bf16[64,768]{1,0:T(8,128)(2,1)} %refs_2_.1), channel_id=1, source_target_pairs={{0,4},{1,5},{2,3},{3,2},{4,0},{5,1},{6,7},{7,6},{8,12},{9,13},{10,... | collective-permute-start | bytes 294920 | tf_op jit(solution)/shard_map/ppermute | solution.py:29
  7.9 1.6 %collective-permute-start = (bf16[64,768]{1,0:T(8,128)(2,1)}, bf16[64,768]{1,0:T(8,128)(2,1)S(1)}, u32[]{:S(2)}, u32[]{:S(2)}) collective-permute-start(bf16[64,768]{1,0:T(8,128)(2,1)} %refs_2_.1), channel_id=1, source_target_pairs={{0,8},{1,9},{2,10},{3,11},{4,12},{5,13},{6,14},{7,15},{8,0},{9,1},... | collective-permute-start | bytes 294920 | tf_op jit(solution)/shard_map/ppermute | solution.py:29
  9.4 1.1 %collective-permute-done.1.refs_2_ = bf16[64,768]{1,0:T(8,128)(2,1)S(1)} collective-permute-done((bf16[64,768]{1,0:T(8,128)(2,1)}, bf16[64,768]{1,0:T(8,128)(2,1)S(1)}, u32[]{:S(2)}, u32[]{:S(2)}) %collective-permute-start.1) | collective-permute-done | bytes 98336 | tf_op jit(solution)/shard_map/ppermute | solution.py:29
  10.5 0.6 %collective-permute-done.3.refs_4_ = bf16[64,768]{1,0:T(8,128)(2,1)S(1)} collective-permute-done((bf16[64,768]{1,0:T(8,128)(2,1)}, bf16[64,768]{1,0:T(8,128)(2,1)S(1)}, u32[]{:S(2)}, u32[]{:S(2)}) %collective-permute-start.3) | collective-permute-done | bytes 98336 | tf_op jit(solution)/shard_map/ppermute | solution.py:29
  11.1 1.6 %collective-permute-start.5 = (bf16[64,768]{1,0:T(8,128)(2,1)S(1)}, bf16[64,768]{1,0:T(8,128)(2,1)S(1)}, u32[]{:S(2)}, u32[]{:S(2)}) collective-permute-start(bf16[64,768]{1,0:T(8,128)(2,1)S(1)} %collective-permute-done.1.refs_2_), channel_id=1, source_target_pairs={{0,8},{1,9},{2,10},{3,11},{4,12},{5,13},{6,14},{7,15},{8,0},{9,1},... | collective-permute-start | bytes 294920 | tf_op jit(solution)/shard_map/ppermute | solution.py:29
  12.7 1.2 %collective-permute-start.4 = (bf16[128,768]{1,0:T(8,128)(2,1)S(1)}, bf16[128,768]{1,0:T(8,128)(2,1)S(1)}, u32[]{:S(2)}, u32[]{:S(2)}) collective-permute-start(bf16[128,768]{1,0:T(8,128)(2,1)S(1)} %pad_maximum_fusion.2), channel_id=1, source_target_pairs={{0,1},{1,0},{2,6},{3,7},{4,5},{5,4},{6,2},{7,3},{8,9},{9,8},{10,14... | collective-permute-start | bytes 589832 | tf_op jit(solution)/shard_map/ppermute | solution.py:29
  13.9 1.4 %copy-done = bf16[16,64,768]{2,1,0:T(8,128)(2,1)S(1)} copy-done((bf16[16,64,768]{2,1,0:T(8,128)(2,1)S(1)}, bf16[16,64,768]{2,1,0:T(8,128)(2,1)}, u32[]{:S(2)}) %copy-start) | copy-done | bytes 1572888
  15.3 1.0 %line_norms.1.refs_4_ = f32[8,1024]{1,0:T(8,128)S(1)} custom-call(bf16[1024,768]{1,0:T(8,128)(2,1)S(1)} %bitcast.2), custom_call_target="tpu_custom_call" | custom-call | flops 201326592 | bytes 1572864 | tf_op jit(solution)/shard_map/line_norms/pallas_call | solution.py:44
  16.3 0.9 %collective-permute-start.6 = (bf16[64,768]{1,0:T(8,128)(2,1)S(1)}, bf16[64,768]{1,0:T(8,128)(2,1)S(1)}, u32[]{:S(2)}, u32[]{:S(2)}) collective-permute-start(bf16[64,768]{1,0:T(8,128)(2,1)S(1)} %collective-permute-done.5.refs_4_), channel_id=1, source_target_pairs={{0,1},{1,0},{2,6},{3,7},{4,5},{5,4},{6,2},{7,3},{8,9},{9,8},{10,14... | collective-permute-start | bytes 294920 | tf_op jit(solution)/shard_map/ppermute | solution.py:29
  17.3 1.6 %collective-permute-start.9 = (bf16[256,768]{1,0:T(8,128)(2,1)S(1)}, bf16[256,768]{1,0:T(8,128)(2,1)S(1)}, u32[]{:S(2)}, u32[]{:S(2)}) collective-permute-start(bf16[256,768]{1,0:T(8,128)(2,1)S(1)} %pad_maximum_fusion), channel_id=1, source_target_pairs={{0,4},{1,5},{2,3},{3,2},{4,0},{5,1},{6,7},{7,6},{8,12},{9,13},{10,... | collective-permute-start | bytes 1179656 | tf_op jit(solution)/shard_map/ppermute | solution.py:29
  18.9 0.0 collective-permute-done.4.refs_3_
  18.9 3.1 %collective-permute-done.6.refs_2_ = bf16[64,768]{1,0:T(8,128)(2,1)S(1)} collective-permute-done((bf16[64,768]{1,0:T(8,128)(2,1)S(1)}, bf16[64,768]{1,0:T(8,128)(2,1)S(1)}, u32[]{:S(2)}, u32[]{:S(2)}) %collective-permute-start.6) | collective-permute-done | bytes 98336 | tf_op jit(solution)/shard_map/ppermute | solution.py:29
  22.1 1.0 %collective-permute-start.7 = (bf16[192,768]{1,0:T(8,128)(2,1)S(1)}, bf16[192,768]{1,0:T(8,128)(2,1)S(1)}, u32[]{:S(2)}, u32[]{:S(2)}) collective-permute-start(bf16[192,768]{1,0:T(8,128)(2,1)S(1)} %pad_maximum_fusion.1), channel_id=1, source_target_pairs={{0,4},{1,5},{2,3},{3,2},{4,0},{5,1},{6,7},{7,6},{8,12},{9,13},{10,... | collective-permute-start | bytes 884744 | tf_op jit(solution)/shard_map/ppermute | solution.py:29
  23.1 0.0 collective-permute-done.8.refs_1_
  23.1 1.1 %absorb.3 = (f32[16,1024]{1,0:T(8,128)S(1)}, f32[16,1024]{1,0:T(8,128)S(1)}) custom-call(bf16[1024,768]{1,0:T(8,128)(2,1)S(1)} %bitcast.3, bf16[1024,768]{1,0:T(8,128)(2,1)S(1)} %collective-permute-done.8.refs_1_, bf16[64,768]{1,0:T(8,128)(2,1)S(1)} %copy-done.1, ...), custom_call_target="tpu_custom_call", output_to_operand_aliasing={{0}: (6, {}), {1}: (7, {})} | custom-call | flops 805306368 | bytes 3670016 | tf_op jit(solution)/shard_map/absorb/pallas_call | solution.py:44
  24.2 1.1 %absorb.4 = (f32[16,1024]{1,0:T(8,128)S(1)}, f32[16,1024]{1,0:T(8,128)S(1)}) custom-call(bf16[1024,768]{1,0:T(8,128)(2,1)S(1)} %bitcast.4, bf16[1024,768]{1,0:T(8,128)(2,1)S(1)} %collective-permute-done.8.refs_1_, bf16[64,768]{1,0:T(8,128)(2,1)S(1)} %collective-permute-done.1.refs_2_, ...), custom_call_target="tpu_custom_call", output_to_operand_aliasing={{0}: (5, {}), {1}: (6, {})} | custom-call | flops 805306368 | bytes 3670016 | tf_op jit(solution)/shard_map/absorb/pallas_call | solution.py:44
  25.3 0.0 copy-start.2
  25.4 1.3 %absorb.5 = (f32[16,1024]{1,0:T(8,128)S(1)}, f32[16,1024]{1,0:T(8,128)S(1)}) custom-call(bf16[1024,768]{1,0:T(8,128)(2,1)S(1)} %bitcast.5, bf16[1024,768]{1,0:T(8,128)(2,1)S(1)} %collective-permute-done.8.refs_1_, bf16[64,768]{1,0:T(8,128)(2,1)S(1)} %collective-permute-done.6.refs_2_, ...), custom_call_target="tpu_custom_call", output_to_operand_aliasing={{0}: (4, {}), {1}: (5, {})} | custom-call | flops 1006632960 | bytes 3768320 | tf_op jit(solution)/shard_map/absorb/pallas_call | solution.py:44
  26.7 2.1 %collective-permute-done.7.refs_0_ = bf16[192,768]{1,0:T(8,128)(2,1)S(1)} collective-permute-done((bf16[192,768]{1,0:T(8,128)(2,1)S(1)}, bf16[192,768]{1,0:T(8,128)(2,1)S(1)}, u32[]{:S(2)}, u32[]{:S(2)}) %collective-permute-start.7) | collective-permute-done | bytes 294944 | tf_op jit(solution)/shard_map/ppermute | solution.py:29
  28.9 0.0 collective-permute-start.10
  28.9 0.5 %collective-permute-start.11 = (f32[16,1024]{1,0:T(8,128)S(1)}, f32[16,1024]{1,0:T(8,128)S(1)}, u32[]{:S(2)}, u32[]{:S(2)}) collective-permute-start(f32[16,1024]{1,0:T(8,128)S(1)} %get-tuple-element.30), channel_id=1, source_target_pairs={{0,2},{1,3},{2,0},{3,1},{4,6},{5,7},{6,4},{7,5},{8,10},{9,11},{10,... | collective-permute-start | bytes 196616 | tf_op jit(solution)/shard_map/ppermute | solution.py:29
  30.0 0.5 %collective-permute-done.11.refs_3_ = f32[16,1024]{1,0:T(8,128)S(1)} collective-permute-done((f32[16,1024]{1,0:T(8,128)S(1)}, f32[16,1024]{1,0:T(8,128)S(1)}, u32[]{:S(2)}, u32[]{:S(2)}) %collective-permute-start.11) | collective-permute-done | bytes 65568 | tf_op jit(solution)/shard_map/ppermute | solution.py:29
  30.5 0.0 collective-permute-done.10.refs_1_
  30.5 0.6 %last.2 = (f32[2,8,64]{2,1,0:T(8,128)S(1)}, f32[2,8,64]{2,1,0:T(8,128)S(1)}) custom-call(s32[1]{0:T(128)S(6)} %copy.24.count_ref, s32[16]{0:T(128)S(1)} %copy-done.2, bf16[1024,768]{1,0:T(8,128)(2,1)S(1)} %bitcast.6, bf16[192,768]{1,0:T(8,128)(2,1)S(1)} %collective-permute-done.7.refs_0_, ...), custom_call_target="tpu_custom_call", output_to_operand_aliasing={{0}: (8, {})} | custom-call | flops 603979776 | bytes 2330692 | tf_op jit(solution)/shard_map/last/pallas_call | solution.py:44
  31.1 1.1 %collective-permute-start.12 = (f32[2,8,64]{2,1,0:T(8,128)S(1)}, f32[2,8,64]{2,1,0:T(8,128)S(1)}, u32[]{:S(2)}, u32[]{:S(2)}) collective-permute-start(f32[2,8,64]{2,1,0:T(8,128)S(1)} %get-tuple-element.34), channel_id=1, source_target_pairs={{0,2},{1,3},{2,4},{3,5},{4,6},{5,7},{6,8},{7,9},{8,10},{9,11},{10,... | collective-permute-start | bytes 12296 | tf_op jit(solution)/shard_map/ppermute | solution.py:29
  32.2 1.5 %last.3 = (f32[2,8,64]{2,1,0:T(8,128)S(1)}, f32[2,8,64]{2,1,0:T(8,128)S(1)}) custom-call(s32[1]{0:T(128)S(6)} %copy.24.count_ref, s32[16]{0:T(128)S(1)} %copy-done.2, bf16[1024,768]{1,0:T(8,128)(2,1)S(1)} %bitcast.7, bf16[192,768]{1,0:T(8,128)(2,1)S(1)} %collective-permute-done.7.refs_0_, ...), custom_call_target="tpu_custom_call", output_to_operand_aliasing={{0}: (8, {})} | custom-call | flops 603979776 | bytes 2330692 | tf_op jit(solution)/shard_map/last/pallas_call | solution.py:44
  33.8 0.1 collective-permute-start.13
  33.8 3.1 %collective-permute-done.12.arrived_ref = f32[2,8,64]{2,1,0:T(8,128)S(1)} collective-permute-done((f32[2,8,64]{2,1,0:T(8,128)S(1)}, f32[2,8,64]{2,1,0:T(8,128)S(1)}, u32[]{:S(2)}, u32[]{:S(2)}) %collective-permute-start.12) | collective-permute-done | bytes 4128 | tf_op jit(solution)/shard_map/ppermute | solution.py:29
  36.9 0.6 %final.1 = (f32[8,64]{1,0:T(8,128)}, f32[8,64]{1,0:T(8,128)}) custom-call(f32[2,8,64]{2,1,0:T(8,128)S(1)} %merged.1.placed_ref, f32[2,8,64]{2,1,0:T(8,128)S(1)} %collective-permute-done.13.arrived_ref), custom_call_target="tpu_custom_call" | custom-call | bytes 8192 | tf_op jit(solution)/shard_map/final/pallas_call | solution.py:44
  (16 shorter events, 0.1 us)
Async XLA Ops:
  0.6 22.4 %collective-permute-start.8 = (bf16[1024,768]{1,0:T(8,128)(2,1)}, bf16[1024,768]{1,0:T(8,128)(2,1)S(1)}, u32[]{:S(2)}, u32[]{:S(2)}) collective-permute-start(bf16[1024,768]{1,0:T(8,128)(2,1)} %bitcast.1), channel_id=1, source_target_pairs={{0,2},{1,3},{2,0},{3,1},{4,6},{5,7},{6,4},{7,5},{8,10},{9,11},{10,... | collective-permute-start | bytes 4718600 | tf_op jit(solution)/shard_map/ppermute | solution.py:29
  1.1 9.4 %collective-permute-start.1 = (bf16[64,768]{1,0:T(8,128)(2,1)}, bf16[64,768]{1,0:T(8,128)(2,1)S(1)}, u32[]{:S(2)}, u32[]{:S(2)}) collective-permute-start(bf16[64,768]{1,0:T(8,128)(2,1)} %refs_2_.1), channel_id=1, source_target_pairs={{0,16},{1,17},{2,18},{3,19},{4,20},{5,21},{6,22},{7,23},{8,24},{9,... | collective-permute-start | bytes 294920 | tf_op jit(solution)/shard_map/ppermute | solution.py:29
  4.8 5.7 %collective-permute-start.2 = (bf16[64,768]{1,0:T(8,128)(2,1)}, bf16[64,768]{1,0:T(8,128)(2,1)S(1)}, u32[]{:S(2)}, u32[]{:S(2)}) collective-permute-start(bf16[64,768]{1,0:T(8,128)(2,1)} %refs_2_.1), channel_id=1, source_target_pairs={{0,1},{1,0},{2,6},{3,7},{4,5},{5,4},{6,2},{7,3},{8,9},{9,8},{10,14... | collective-permute-start | bytes 294920 | tf_op jit(solution)/shard_map/ppermute | solution.py:29
  6.3 4.8 %collective-permute-start.3 = (bf16[64,768]{1,0:T(8,128)(2,1)}, bf16[64,768]{1,0:T(8,128)(2,1)S(1)}, u32[]{:S(2)}, u32[]{:S(2)}) collective-permute-start(bf16[64,768]{1,0:T(8,128)(2,1)} %refs_2_.1), channel_id=1, source_target_pairs={{0,4},{1,5},{2,3},{3,2},{4,0},{5,1},{6,7},{7,6},{8,12},{9,13},{10,... | collective-permute-start | bytes 294920 | tf_op jit(solution)/shard_map/ppermute | solution.py:29
  7.9 4.9 %collective-permute-start = (bf16[64,768]{1,0:T(8,128)(2,1)}, bf16[64,768]{1,0:T(8,128)(2,1)S(1)}, u32[]{:S(2)}, u32[]{:S(2)}) collective-permute-start(bf16[64,768]{1,0:T(8,128)(2,1)} %refs_2_.1), channel_id=1, source_target_pairs={{0,8},{1,9},{2,10},{3,11},{4,12},{5,13},{6,14},{7,15},{8,0},{9,1},... | collective-permute-start | bytes 294920 | tf_op jit(solution)/shard_map/ppermute | solution.py:29
  11.1 5.2 %collective-permute-start.5 = (bf16[64,768]{1,0:T(8,128)(2,1)S(1)}, bf16[64,768]{1,0:T(8,128)(2,1)S(1)}, u32[]{:S(2)}, u32[]{:S(2)}) collective-permute-start(bf16[64,768]{1,0:T(8,128)(2,1)S(1)} %collective-permute-done.1.refs_2_), channel_id=1, source_target_pairs={{0,8},{1,9},{2,10},{3,11},{4,12},{5,13},{6,14},{7,15},{8,0},{9,1},... | collective-permute-start | bytes 294920 | tf_op jit(solution)/shard_map/ppermute | solution.py:29
  12.7 6.2 %collective-permute-start.4 = (bf16[128,768]{1,0:T(8,128)(2,1)S(1)}, bf16[128,768]{1,0:T(8,128)(2,1)S(1)}, u32[]{:S(2)}, u32[]{:S(2)}) collective-permute-start(bf16[128,768]{1,0:T(8,128)(2,1)S(1)} %pad_maximum_fusion.2), channel_id=1, source_target_pairs={{0,1},{1,0},{2,6},{3,7},{4,5},{5,4},{6,2},{7,3},{8,9},{9,8},{10,14... | collective-permute-start | bytes 589832 | tf_op jit(solution)/shard_map/ppermute | solution.py:29
  13.9 1.4 %copy-start = (bf16[16,64,768]{2,1,0:T(8,128)(2,1)S(1)}, bf16[16,64,768]{2,1,0:T(8,128)(2,1)}, u32[]{:S(2)}) copy-start(bf16[16,64,768]{2,1,0:T(8,128)(2,1)} %param.4) | copy-start | bytes 4718596
  15.3 7.8 %copy-start.1 = (bf16[64,768]{1,0:T(8,128)(2,1)S(1)}, bf16[64,768]{1,0:T(8,128)(2,1)}, u32[]{:S(2)}) copy-start(bf16[64,768]{1,0:T(8,128)(2,1)} %refs_2_.1) | copy-start | bytes 294916
  16.3 5.7 %collective-permute-start.6 = (bf16[64,768]{1,0:T(8,128)(2,1)S(1)}, bf16[64,768]{1,0:T(8,128)(2,1)S(1)}, u32[]{:S(2)}, u32[]{:S(2)}) collective-permute-start(bf16[64,768]{1,0:T(8,128)(2,1)S(1)} %collective-permute-done.5.refs_4_), channel_id=1, source_target_pairs={{0,1},{1,0},{2,6},{3,7},{4,5},{5,4},{6,2},{7,3},{8,9},{9,8},{10,14... | collective-permute-start | bytes 294920 | tf_op jit(solution)/shard_map/ppermute | solution.py:29
  17.3 8.0 %collective-permute-start.9 = (bf16[256,768]{1,0:T(8,128)(2,1)S(1)}, bf16[256,768]{1,0:T(8,128)(2,1)S(1)}, u32[]{:S(2)}, u32[]{:S(2)}) collective-permute-start(bf16[256,768]{1,0:T(8,128)(2,1)S(1)} %pad_maximum_fusion), channel_id=1, source_target_pairs={{0,4},{1,5},{2,3},{3,2},{4,0},{5,1},{6,7},{7,6},{8,12},{9,13},{10,... | collective-permute-start | bytes 1179656 | tf_op jit(solution)/shard_map/ppermute | solution.py:29
  22.1 6.8 %collective-permute-start.7 = (bf16[192,768]{1,0:T(8,128)(2,1)S(1)}, bf16[192,768]{1,0:T(8,128)(2,1)S(1)}, u32[]{:S(2)}, u32[]{:S(2)}) collective-permute-start(bf16[192,768]{1,0:T(8,128)(2,1)S(1)} %pad_maximum_fusion.1), channel_id=1, source_target_pairs={{0,4},{1,5},{2,3},{3,2},{4,0},{5,1},{6,7},{7,6},{8,12},{9,13},{10,... | collective-permute-start | bytes 884744 | tf_op jit(solution)/shard_map/ppermute | solution.py:29
  25.3 5.2 %copy-start.2 = (s32[16]{0:T(128)S(1)}, s32[16]{0:T(128)}, u32[]{:S(2)}) copy-start(s32[16]{0:T(128)} %to_ref.3) | copy-start | bytes 196
  28.9 1.7 %collective-permute-start.10 = (bf16[192,768]{1,0:T(8,128)(2,1)S(1)}, bf16[192,768]{1,0:T(8,128)(2,1)S(1)}, u32[]{:S(2)}, u32[]{:S(2)}) collective-permute-start(bf16[192,768]{1,0:T(8,128)(2,1)S(1)} %collective-permute-done.7.refs_0_), channel_id=1, source_target_pairs={{0,2},{1,3},{2,0},{3,1},{4,6},{5,7},{6,4},{7,5},{8,10},{9,11},{10,... | collective-permute-start | bytes 884744 | tf_op jit(solution)/shard_map/ppermute | solution.py:29
  28.9 1.7 %collective-permute-start.11 = (f32[16,1024]{1,0:T(8,128)S(1)}, f32[16,1024]{1,0:T(8,128)S(1)}, u32[]{:S(2)}, u32[]{:S(2)}) collective-permute-start(f32[16,1024]{1,0:T(8,128)S(1)} %get-tuple-element.30), channel_id=1, source_target_pairs={{0,2},{1,3},{2,0},{3,1},{4,6},{5,7},{6,4},{7,5},{8,10},{9,11},{10,... | collective-permute-start | bytes 196616 | tf_op jit(solution)/shard_map/ppermute | solution.py:29
  31.1 5.8 %collective-permute-start.12 = (f32[2,8,64]{2,1,0:T(8,128)S(1)}, f32[2,8,64]{2,1,0:T(8,128)S(1)}, u32[]{:S(2)}, u32[]{:S(2)}) collective-permute-start(f32[2,8,64]{2,1,0:T(8,128)S(1)} %get-tuple-element.34), channel_id=1, source_target_pairs={{0,2},{1,3},{2,4},{3,5},{4,6},{5,7},{6,8},{7,9},{8,10},{9,11},{10,... | collective-permute-start | bytes 12296 | tf_op jit(solution)/shard_map/ppermute | solution.py:29
  33.8 3.2 %collective-permute-start.13 = (f32[2,8,64]{2,1,0:T(8,128)S(1)}, f32[2,8,64]{2,1,0:T(8,128)S(1)}, u32[]{:S(2)}, u32[]{:S(2)}) collective-permute-start(f32[2,8,64]{2,1,0:T(8,128)S(1)} %get-tuple-element.35), channel_id=1, source_target_pairs={{0,2},{1,3},{2,0},{3,1},{4,6},{5,7},{6,4},{7,5},{8,10},{9,11},{10,... | collective-permute-start | bytes 12296 | tf_op jit(solution)/shard_map/ppermute | solution.py:29

commit v4 on v3

--- a/solution.py
+++ b/solution.py
@@ -70,21 +70,50 @@
     return jnp.minimum(first, other_first), runner
 
 
+def pack_kernel(slots, block_rows, count_ref, own_ref, partner_ref, packed_ref):
+    lines = own_ref.shape[0]
+    per_slot = lines // slots
+    half = lines // 2
+    packed_ref[:half, :] = own_ref[:half, :]
+    for slot in range(slots // 2, slots):
+        here = slice(slot * per_slot, (slot + 1) * per_slot)
+        other = 3 * slots // 2 - 1 - slot
+        theirs = slice(other * per_slot, (other + 1) * per_slot)
+        usable = slot * block_rows < count_ref[...]
+        packed_ref[here, :] = jnp.where(usable, own_ref[here, :], partner_ref[theirs, :])
+
+
+def pack(line_counts, own, partner, slots, block_rows):
+    return call(
+        functools.partial(pack_kernel, slots, block_rows),
+        (jax.ShapeDtypeStruct(own.shape, own.dtype),),
+        (line_counts.reshape(1, 1), own, partner),
+        (VMEM, VMEM, VMEM),
+        name="pack",
+    )[0]
+
+
+def spread(ref, row, order=None):
+    slots, per_slot = ref.shape
+    for place in range(slots):
+        slot = place if order is None else order[place]
+        ref[slot : slot + 1, :] = row[:, place * per_slot : (place + 1) * per_slot]
+
+
 def norm_kernel(own_ref, norms_ref):
+    slots, per_slot = norms_ref.shape
     lines, features = own_ref.shape
     ones = jnp.ones((SUBLANES, features), jnp.bfloat16)
-    step = min(lines, LINE_STEP)
-    for at in range(0, lines, step):
-        wide = own_ref[at : at + step, :].astype(jnp.float32)
-        square = wide * wide
-        high = square.astype(jnp.bfloat16)
-        low = (square - high.astype(jnp.float32)).astype(jnp.bfloat16)
-        norms_ref[:, at : at + step] = contract(ones, high) + contract(ones, low)
-
-
-def line_norms(own):
+    wide = own_ref[...].astype(jnp.float32)
+    square = wide * wide
+    high = square.astype(jnp.bfloat16)
+    low = (square - high.astype(jnp.float32)).astype(jnp.bfloat16)
+    spread(norms_ref, (contract(ones, high) + contract(ones, low))[:1])
+
+
+def line_norms(own, slots):
     lines, features = own.shape
-    out = jax.ShapeDtypeStruct((SUBLANES, lines), jnp.float32)
+    out = jax.ShapeDtypeStruct((slots, lines // slots), jnp.float32)
     return call(
         norm_kernel, (out,), (own,), (VMEM,), 32 * SUBLANES * lines * features, name="line_norms"
     )[0]
@@ -118,11 +147,13 @@
     return plan + [held]
 
 
-def absorb_kernel(line_count, bank_count, *refs):
+def absorb_kernel(line_count, bank_count, give, *refs):
     line_refs, refs = refs[:line_count], refs[line_count:]
     bank_refs, refs = refs[:bank_count], refs[bank_count:]
     for lines_ref, in_ref, out_ref in zip(line_refs, refs[:line_count], refs[line_count:]):
         lines = lines_ref.shape[0]
+        if in_ref is not refs[0]:
+            lines //= 2
         step = min(lines, LINE_STEP)
         for at in range(0, lines, step):
             first, second = in_ref[:SUBLANES, at : at + step], in_ref[SUBLANES:, at : at + step]
@@ -131,16 +162,20 @@
                 first, second = absorbed(banks, lines_ref[at : at + step, :], first, second)
             out_ref[:SUBLANES, at : at + step] = first
             out_ref[SUBLANES:, at : at + step] = second
-
-
-def absorb(states, banks, line_sets):
+    if give:
+        mine_ref, theirs_ref = refs[line_count:]
+        half = mine_ref.shape[1] // 2
+        theirs_ref[:, half:] = mine_ref[:, half:]
+
+
+def absorb(states, banks, line_sets, give=False):
     features = banks[0].shape[1]
     rows = sum(bank.shape[0] for bank in banks)
     total = sum(lines.shape[0] for lines in line_sets)
     count = len(line_sets)
     operands = (*line_sets, *banks, *states)
     return call(
-        functools.partial(absorb_kernel, count, len(banks)),
+        functools.partial(absorb_kernel, count, len(banks), give),
         tuple(jax.ShapeDtypeStruct(state.shape, state.dtype) for state in states),
         operands,
         (VMEM,) * len(operands),
@@ -150,56 +185,64 @@
     )
 
 
-def last_kernel(parity, places, block_rows, count_ref, to_ref, lines_ref, *refs):
+def folded(first, second):
+    rows = first.shape[0]
+    while rows > 1:
+        rows //= 2
+        first, second = join(first[:rows], second[:rows], first[rows:], second[rows:])
+    return first, second
+
+
+def last_kernel(parity, block_rows, count_ref, to_ref, lines_ref, *refs):
     bank_refs, refs = refs[:2], refs[2:]
-    mine_ref, returned_ref, norms_ref, _, keep_ref, send_ref, placed_ref = refs
+    mine_ref, returned_ref, norms_ref, _, keep_ref, send_ref, slot_ref = refs
     lines, features = lines_ref.shape
-    slots = to_ref.shape[0]
-    per_slot = lines // slots
+    slots, per_slot = norms_ref.shape
+    places = keep_ref.shape[1]
     host = lax.axis_index("line")
 
     @pl.when(lax.rem(host, 2) == parity)
     def work():
-        following = lax.rem(host + 1, lax.axis_size("line"))
-        first, second = join(
-            mine_ref[:SUBLANES],
-            mine_ref[SUBLANES:],
-            returned_ref[:SUBLANES],
-            returned_ref[SUBLANES:],
-        )
+        given = folded(returned_ref[:SUBLANES], returned_ref[SUBLANES:])
+        order = [*range(slots // 2), *reversed(range(slots // 2, slots))]
+        for index, value in enumerate(given):
+            spread(slot_ref.at[2 + index], value, order)
+        first, second = mine_ref[:SUBLANES], mine_ref[SUBLANES:]
         for group in tiles(bank_refs):
             banks = [ref[row : row + tile, :] for ref, row, tile in group]
             first, second = absorbed(banks, lines_ref[...], first, second)
-        lowest, runner = first[:1], second[:1]
-        for row in range(1, SUBLANES):
-            lowest, runner = join(lowest, runner, first[row : row + 1], second[row : row + 1])
-        both = [(value + norms_ref[:1]) / features for value in (lowest, runner)]
-        placed_ref[...] = jnp.full(placed_ref.shape, HUGE_DISTANCE, jnp.float32)
-        for slot in range(slots):
-            usable = slot * block_rows < count_ref[0]
-            here = to_ref[slot] - host * places
-            there = to_ref[slot] - following * places
-            row = jnp.where(jnp.logical_and(there >= 0, there < places), places + there, 2 * places)
-            row = jnp.where(jnp.logical_and(here >= 0, here < places), here, row)
-            row = jnp.where(usable, row, 2 * places)
-            for index, value in enumerate(both):
-                placed_ref[index, pl.ds(row, 1), :] = value[:, slot * per_slot : (slot + 1) * per_slot]
-        keep_ref[...] = placed_ref[:, :places]
-        send_ref[...] = placed_ref[:, places : 2 * places]
+        for index, value in enumerate(folded(first, second)):
+            spread(slot_ref.at[index], value)
+        both = join(slot_ref[0], slot_ref[1], slot_ref[2], slot_ref[3])
+        both = [(value + norms_ref[...]) / features for value in both]
+
+        following = lax.rem(host + 1, lax.axis_size("line"))
+        slot = lax.broadcasted_iota(jnp.int32, (slots, slots), 0)
+        across_slots = lax.broadcasted_iota(jnp.int32, (slots, slots), 1)
+        to = jnp.where(slot == across_slots, to_ref[...], 0)
+        to = jnp.sum(to, axis=1, keepdims=True)
+        usable = slot[:, :1] * block_rows < count_ref[...]
+        for ref, base in ((keep_ref, host * places), (send_ref, following * places)):
+            place = jnp.where(usable, to - base, -1)
+            for row in range(places):
+                chosen = place == row
+                for index, value in enumerate(both):
+                    picked = jnp.where(chosen, value, HUGE_DISTANCE)
+                    ref[index, row : row + 1, :] = jnp.min(picked, axis=0, keepdims=True)
 
 
 def last(parity, keep, line_counts, destinations, own, banks, mine, returned, norms, block_rows):
     lines, features = own.shape
-    places, per_slot = keep.shape[1:]
-    operands = (line_counts, destinations, own, *banks, mine, returned, norms, keep)
+    counts, to = line_counts.reshape(1, 1), destinations.reshape(1, -1)
+    operands = (counts, to, own, *banks, mine, returned, norms, keep)
     placed = jax.ShapeDtypeStruct(keep.shape, keep.dtype)
     return call(
-        functools.partial(last_kernel, parity, places, block_rows),
+        functools.partial(last_kernel, parity, block_rows),
         (placed, placed),
         operands,
-        (SMEM, SMEM) + (VMEM,) * (len(operands) - 2),
+        (VMEM,) * len(operands),
         2 * lines * features * sum(bank.shape[0] for bank in banks),
-        scratch=(pltpu.VMEM((2, 2 * places + SUBLANES, per_slot), jnp.float32),),
+        scratch=(pltpu.VMEM((4, *norms.shape), jnp.float32),),
         aliases={len(operands) - 1: 0},
         name="last",
     )
@@ -262,25 +305,28 @@
 
     distant = moved(centroids, across(*far[-1]))
     level = doubled([centroids], far[:-1])[1:]
+    level, partner = lax.optimization_barrier((level, partner))
     near = moved(centroids, straight)
     side = moved(centroids, turned)
     distant, near, side = lax.optimization_barrier((distant, near, side))
     beyond = doubled([distant], far[:-1])[1:]
-    norms = line_norms(own)
-    beyond, norms = lax.optimization_barrier((beyond, norms))
+    packed = pack(line_counts, own, partner, slots, block_rows)
+    beyond, packed = lax.optimization_barrier((beyond, packed))
+    norms = line_norms(packed, slots)
     near_level = moved(stacked([*level, distant]), straight)
+    crossed_level = moved(stacked([near, *level, distant]), turned)
     near_beyond = moved(stacked(beyond), straight)
-    crossed_level = moved(stacked([near, *level, distant, *beyond]), turned)
-    crossed_beyond = moved(stacked([near_level, near_beyond]), turned)
-
-    lines = (own, partner)
+    crossed_beyond = moved(stacked([near_level, *beyond]), turned)
+    corner = moved(near_beyond, turned)
+
+    lines = (packed, partner)
     empty = jnp.full((2 * SUBLANES, own.shape[0]), HUGE_DISTANCE, jnp.float32)
-    states = absorb((empty, empty), (centroids, near, side, *level), lines)
-    states = absorb(states, (distant, near_level, *beyond), lines)
-    mine, theirs = absorb(states, (near_beyond, crossed_level), lines)
+    states = absorb((empty, empty), (centroids, near, side, *level, distant, near_level, *beyond), lines)
+    states = absorb(states, (near_beyond, crossed_level), lines)
+    mine, theirs = absorb(states, (crossed_beyond,), lines, give=True)
     returned = moved(theirs, partner_of)
-    crossed_beyond, mine = lax.optimization_barrier((crossed_beyond, mine))
-    banks = (crossed_beyond, moved(crossed_beyond, partner_of))
+    corner, mine, norms = lax.optimization_barrier((corner, mine, norms))
+    banks = (corner, moved(corner, partner_of))
 
     placed = jnp.zeros((2, places, sub_rows), jnp.float32)
     sends = [None, None]
@@ -290,7 +336,7 @@
             placed,
             line_counts,
             destinations,
-            own,
+            packed,
             banks,
             mine,
             returned,

time: 37.7 us -> 36.7 us (0.973)
  starting transfers between devices: 16.8 us -> 18.3 us
  waiting for transfers between devices: 10.6 us -> 9.25 us
  Pallas kernels: 7.3 us -> 6.11 us
    ppermute x14 -> x15, starting transfers between devices: 16.8 us -> 18.3 us  [moved(): return lax.ppermute(value, AXES, route)]
    ppermute x14 -> x15, waiting for transfers between devices: 10.6 us -> 9.25 us  [moved(): return lax.ppermute(value, AXES, route)]
    pallas_call x8 -> x9, Pallas kernels: 7.3 us -> 6.11 us  [call(): pl.pallas_call(body, in_specs=list(spaces), out_specs=(VMEM,) * len(outs)...]
  transfers between devices with their start and end apart: 14 -> 15, of which waited for: 6 -> 7; matrix products, arithmetic and copies ran while one was open for 0% -> 0% of each run, Pallas kernels for 16% -> 15%
where the time goes in v4:
time: 36.7 us; the launch traced here: 36.5 us
  starting transfers between devices  18.3 us (50%)
  waiting for transfers between devices  9.25 us (25%)
  Pallas kernels  6.11 us (17%)
  local copies, waits for them, and re-layouts  1.43 us (4%)
  between operations  1.4 us (4%)
    ppermute x15, starting transfers between devices, moved(): return lax.ppermute(value, AXES, route)  18.3 us
    ppermute x15, waiting for transfers between devices, moved(): return lax.ppermute(value, AXES, route)  9.25 us
    pallas_call x9, Pallas kernels, call(): pl.pallas_call(body, in_specs=list(spaces), out_specs=(VMEM,) * len(outs)...  6.11 us
    unnamed x6, local copies, waits for them, and re-layouts  1.41 us
  transfers between devices with their start and end apart: 15, of which 7 were waited for; matrix products, arithmetic and copies ran while one was open for 0% of the time, Pallas kernels for 15%

profile of v4, /device:TPU:0, one launch (start us, length us, event | category | flops | bytes accessed | tf_op | source)
XLA Modules:
  0.0 36.5 jit_solution(2946732532912597645)
XLA Ops:
  0.6 0.5 %collective-permute-start.5 = (bf16[1024,768]{1,0:T(8,128)(2,1)}, bf16[1024,768]{1,0:T(8,128)(2,1)S(1)}, u32[]{:S(2)}, u32[]{:S(2)}) collective-permute-start(bf16[1024,768]{1,0:T(8,128)(2,1)} %bitcast.6), channel_id=1, source_target_pairs={{0,2},{1,3},{2,0},{3,1},{4,6},{5,7},{6,4},{7,5},{8,10},{9,11},{10,... | collective-permute-start | bytes 4718600 | tf_op jit(solution)/shard_map/ppermute | solution.py:29
  1.1 3.7 %collective-permute-start = (bf16[64,768]{1,0:T(8,128)(2,1)}, bf16[64,768]{1,0:T(8,128)(2,1)S(1)}, u32[]{:S(2)}, u32[]{:S(2)}) collective-permute-start(bf16[64,768]{1,0:T(8,128)(2,1)} %refs_2_.1), channel_id=1, source_target_pairs={{0,16},{1,17},{2,18},{3,19},{4,20},{5,21},{6,22},{7,23},{8,24},{9,... | collective-permute-start | bytes 294920 | tf_op jit(solution)/shard_map/ppermute | solution.py:29
  4.8 1.5 %collective-permute-start.1 = (bf16[64,768]{1,0:T(8,128)(2,1)}, bf16[64,768]{1,0:T(8,128)(2,1)S(1)}, u32[]{:S(2)}, u32[]{:S(2)}) collective-permute-start(bf16[64,768]{1,0:T(8,128)(2,1)} %refs_2_.1), channel_id=1, source_target_pairs={{0,1},{1,0},{2,6},{3,7},{4,5},{5,4},{6,2},{7,3},{8,9},{9,8},{10,14... | collective-permute-start | bytes 294920 | tf_op jit(solution)/shard_map/ppermute | solution.py:29
  6.3 1.5 %collective-permute-start.2 = (bf16[64,768]{1,0:T(8,128)(2,1)}, bf16[64,768]{1,0:T(8,128)(2,1)S(1)}, u32[]{:S(2)}, u32[]{:S(2)}) collective-permute-start(bf16[64,768]{1,0:T(8,128)(2,1)} %refs_2_.1), channel_id=1, source_target_pairs={{0,4},{1,5},{2,3},{3,2},{4,0},{5,1},{6,7},{7,6},{8,12},{9,13},{10,... | collective-permute-start | bytes 294920 | tf_op jit(solution)/shard_map/ppermute | solution.py:29
  7.9 1.6 %collective-permute-start.4 = (bf16[64,768]{1,0:T(8,128)(2,1)}, bf16[64,768]{1,0:T(8,128)(2,1)S(1)}, u32[]{:S(2)}, u32[]{:S(2)}) collective-permute-start(bf16[64,768]{1,0:T(8,128)(2,1)} %refs_2_.1), channel_id=1, source_target_pairs={{0,8},{1,9},{2,10},{3,11},{4,12},{5,13},{6,14},{7,15},{8,0},{9,1},... | collective-permute-start | bytes 294920 | tf_op jit(solution)/shard_map/ppermute | solution.py:29
  9.4 1.1 %collective-permute-done.refs_6_ = bf16[64,768]{1,0:T(8,128)(2,1)S(1)} collective-permute-done((bf16[64,768]{1,0:T(8,128)(2,1)}, bf16[64,768]{1,0:T(8,128)(2,1)S(1)}, u32[]{:S(2)}, u32[]{:S(2)}) %collective-permute-start) | collective-permute-done | bytes 98336 | tf_op jit(solution)/shard_map/ppermute | solution.py:29
  10.5 0.6 %collective-permute-done.2.refs_4_ = bf16[64,768]{1,0:T(8,128)(2,1)S(1)} collective-permute-done((bf16[64,768]{1,0:T(8,128)(2,1)}, bf16[64,768]{1,0:T(8,128)(2,1)S(1)}, u32[]{:S(2)}, u32[]{:S(2)}) %collective-permute-start.2) | collective-permute-done | bytes 98336 | tf_op jit(solution)/shard_map/ppermute | solution.py:29
  11.1 1.6 %collective-permute-start.3 = (bf16[64,768]{1,0:T(8,128)(2,1)S(1)}, bf16[64,768]{1,0:T(8,128)(2,1)S(1)}, u32[]{:S(2)}, u32[]{:S(2)}) collective-permute-start(bf16[64,768]{1,0:T(8,128)(2,1)S(1)} %collective-permute-done.refs_6_), channel_id=1, source_target_pairs={{0,8},{1,9},{2,10},{3,11},{4,12},{5,13},{6,14},{7,15},{8,0},{9,1},... | collective-permute-start | bytes 294920 | tf_op jit(solution)/shard_map/ppermute | solution.py:29
  12.7 0.0 collective-permute-done.4.refs_5_
  12.7 1.2 %collective-permute-start.8 = (bf16[128,768]{1,0:T(8,128)(2,1)S(1)}, bf16[128,768]{1,0:T(8,128)(2,1)S(1)}, u32[]{:S(2)}, u32[]{:S(2)}) collective-permute-start(bf16[128,768]{1,0:T(8,128)(2,1)S(1)} %pad_maximum_fusion.2), channel_id=1, source_target_pairs={{0,1},{1,0},{2,6},{3,7},{4,5},{5,4},{6,2},{7,3},{8,9},{9,8},{10,14... | collective-permute-start | bytes 589832 | tf_op jit(solution)/shard_map/ppermute | solution.py:29
  14.6 0.0 copy-start
  14.6 1.4 %copy-done = bf16[16,64,768]{2,1,0:T(8,128)(2,1)S(1)} copy-done((bf16[16,64,768]{2,1,0:T(8,128)(2,1)S(1)}, bf16[16,64,768]{2,1,0:T(8,128)(2,1)}, u32[]{:S(2)}) %copy-start) | copy-done | bytes 1572888
  16.0 0.1 pack.1.refs_0_.own_ref.lines_ref
  16.1 0.0 copy-start.2
  16.1 1.0 %collective-permute-start.6 = (bf16[64,768]{1,0:T(8,128)(2,1)S(1)}, bf16[64,768]{1,0:T(8,128)(2,1)S(1)}, u32[]{:S(2)}, u32[]{:S(2)}) collective-permute-start(bf16[64,768]{1,0:T(8,128)(2,1)S(1)} %collective-permute-done.3.refs_8_), channel_id=1, source_target_pairs={{0,1},{1,0},{2,6},{3,7},{4,5},{5,4},{6,2},{7,3},{8,9},{9,8},{10,14... | collective-permute-start | bytes 294920 | tf_op jit(solution)/shard_map/ppermute | solution.py:29
  17.2 1.6 %collective-permute-start.10 = (bf16[192,768]{1,0:T(8,128)(2,1)S(1)}, bf16[192,768]{1,0:T(8,128)(2,1)S(1)}, u32[]{:S(2)}, u32[]{:S(2)}) collective-permute-start(bf16[192,768]{1,0:T(8,128)(2,1)S(1)} %pad_maximum_fusion.1), channel_id=1, source_target_pairs={{0,4},{1,5},{2,3},{3,2},{4,0},{5,1},{6,7},{7,6},{8,12},{9,13},{10,... | collective-permute-start | bytes 884744 | tf_op jit(solution)/shard_map/ppermute | solution.py:29
  18.8 1.3 %collective-permute-start.9 = (bf16[192,768]{1,0:T(8,128)(2,1)S(1)}, bf16[192,768]{1,0:T(8,128)(2,1)S(1)}, u32[]{:S(2)}, u32[]{:S(2)}) collective-permute-start(bf16[192,768]{1,0:T(8,128)(2,1)S(1)} %pad_maximum_fusion), channel_id=1, source_target_pairs={{0,4},{1,5},{2,3},{3,2},{4,0},{5,1},{6,7},{7,6},{8,12},{9,13},{10,... | collective-permute-start | bytes 884744 | tf_op jit(solution)/shard_map/ppermute | solution.py:29
  20.1 1.1 %line_norms.1.refs_4_ = f32[16,64]{1,0:T(8,128)S(1)} custom-call(bf16[1024,768]{1,0:T(8,128)(2,1)S(1)} %pack.1.refs_0_.own_ref.lines_ref), custom_call_target="tpu_custom_call" | custom-call | flops 201326592 | bytes 1572864 | tf_op jit(solution)/shard_map/line_norms/pallas_call | solution.py:44
  21.2 0.7 %collective-permute-done.6.refs_2_ = bf16[64,768]{1,0:T(8,128)(2,1)S(1)} collective-permute-done((bf16[64,768]{1,0:T(8,128)(2,1)S(1)}, bf16[64,768]{1,0:T(8,128)(2,1)S(1)}, u32[]{:S(2)}, u32[]{:S(2)}) %collective-permute-start.6) | collective-permute-done | bytes 98336 | tf_op jit(solution)/shard_map/ppermute | solution.py:29
  21.9 1.0 %collective-permute-start.7 = (bf16[64,768]{1,0:T(8,128)(2,1)S(1)}, bf16[64,768]{1,0:T(8,128)(2,1)S(1)}, u32[]{:S(2)}, u32[]{:S(2)}) collective-permute-start(bf16[64,768]{1,0:T(8,128)(2,1)S(1)} %collective-permute-done.6.refs_2_), channel_id=1, source_target_pairs={{0,4},{1,5},{2,3},{3,2},{4,0},{5,1},{6,7},{7,6},{8,12},{9,13},{10,... | collective-permute-start | bytes 294920 | tf_op jit(solution)/shard_map/ppermute | solution.py:29
  23.0 1.6 %absorb.3 = (f32[16,1024]{1,0:T(8,128)S(1)}, f32[16,1024]{1,0:T(8,128)S(1)}) custom-call(bf16[1024,768]{1,0:T(8,128)(2,1)S(1)} %pack.1.refs_0_.own_ref.lines_ref, bf16[1024,768]{1,0:T(8,128)(2,1)S(1)} %collective-permute-done.5.partner_ref.refs_1_, bf16[64,768]{1,0:T(8,128)(2,1)S(1)} %copy-done.2, ...), custom_call_target="tpu_custom_call", output_to_operand_aliasing={{0}: (9, {}), {1}: (10, {})} | custom-call | flops 1610612736 | bytes 4063232 | tf_op jit(solution)/shard_map/absorb/pallas_call | solution.py:44
  24.6 0.9 %absorb.4 = (f32[16,1024]{1,0:T(8,128)S(1)}, f32[16,1024]{1,0:T(8,128)S(1)}) custom-call(bf16[1024,768]{1,0:T(8,128)(2,1)S(1)} %pack.1.refs_0_.own_ref.lines_ref, bf16[1024,768]{1,0:T(8,128)(2,1)S(1)} %collective-permute-done.5.partner_ref.refs_1_, bf16[64,768]{1,0:T(8,128)(2,1)S(1)} %collective-permute-done.6.refs_2_, ...), custom_call_target="tpu_custom_call", output_to_operand_aliasing={{0}: (4, {}), {1}: (5, {})} | custom-call | flops 805306368 | bytes 3670016 | tf_op jit(solution)/shard_map/absorb/pallas_call | solution.py:44
  25.5 1.6 %collective-permute-done.9.refs_2_ = bf16[192,768]{1,0:T(8,128)(2,1)S(1)} collective-permute-done((bf16[192,768]{1,0:T(8,128)(2,1)S(1)}, bf16[192,768]{1,0:T(8,128)(2,1)S(1)}, u32[]{:S(2)}, u32[]{:S(2)}) %collective-permute-start.9) | collective-permute-done | bytes 294944 | tf_op jit(solution)/shard_map/ppermute | solution.py:29
  27.1 0.9 %absorb.5 = (f32[16,1024]{1,0:T(8,128)S(1)}, f32[16,1024]{1,0:T(8,128)S(1)}) custom-call(bf16[1024,768]{1,0:T(8,128)(2,1)S(1)} %pack.1.refs_0_.own_ref.lines_ref, bf16[1024,768]{1,0:T(8,128)(2,1)S(1)} %collective-permute-done.5.partner_ref.refs_1_, ...), custom_call_target="tpu_custom_call", output_to_operand_aliasing={{0}: (3, {}), {1}: (4, {})} | custom-call | flops 603979776 | bytes 3571712 | tf_op jit(solution)/shard_map/absorb/pallas_call | solution.py:44
  28.0 0.1 collective-permute-done.7.refs_0_
  28.2 0.5 %collective-permute-start.12 = (f32[16,1024]{1,0:T(8,128)S(1)}, f32[16,1024]{1,0:T(8,128)S(1)}, u32[]{:S(2)}, u32[]{:S(2)}) collective-permute-start(f32[16,1024]{1,0:T(8,128)S(1)} %get-tuple-element.36), channel_id=1, source_target_pairs={{0,2},{1,3},{2,0},{3,1},{4,6},{5,7},{6,4},{7,5},{8,10},{9,11},{10,... | collective-permute-start | bytes 196616 | tf_op jit(solution)/shard_map/ppermute | solution.py:29
  28.7 0.9 %collective-permute-done.12.refs_3_ = f32[16,1024]{1,0:T(8,128)S(1)} collective-permute-done((f32[16,1024]{1,0:T(8,128)S(1)}, f32[16,1024]{1,0:T(8,128)S(1)}, u32[]{:S(2)}, u32[]{:S(2)}) %collective-permute-start.12) | collective-permute-done | bytes 65568 | tf_op jit(solution)/shard_map/ppermute | solution.py:29
  29.6 1.2 %collective-permute-start.13 = (f32[2,8,64]{2,1,0:T(8,128)S(1)}, f32[2,8,64]{2,1,0:T(8,128)S(1)}, u32[]{:S(2)}, u32[]{:S(2)}) collective-permute-start(f32[2,8,64]{2,1,0:T(8,128)S(1)} %get-tuple-element.40), channel_id=1, source_target_pairs={{0,2},{1,3},{2,4},{3,5},{4,6},{5,7},{6,8},{7,9},{8,10},{9,11},{10,... | collective-permute-start | bytes 12296 | tf_op jit(solution)/shard_map/ppermute | solution.py:29
  30.8 0.8 %last.3 = (f32[2,8,64]{2,1,0:T(8,128)S(1)}, f32[2,8,64]{2,1,0:T(8,128)S(1)}) custom-call(s32[1,1]{1,0:T(1,128)} %bitcast.5.count_ref, s32[1,16]{1,0:T(1,128)S(1)} %bitcast.9, bf16[1024,768]{1,0:T(8,128)(2,1)S(1)} %pack.1.refs_0_.own_ref.lines_ref, bf16[64,768]{1,0:T(8,128)(2,1)S(1)} %collective-permute-done.7.refs_0_, ...), custom_call_target="tpu_custom_call", output_to_operand_aliasing={{0}: (8, {})} | custom-call | flops 201326592 | bytes 1908804 | tf_op jit(solution)/shard_map/last/pallas_call | solution.py:44
  31.6 0.1 collective-permute-start.14
  31.7 4.2 %collective-permute-done.13.arrived_ref = f32[2,8,64]{2,1,0:T(8,128)S(1)} collective-permute-done((f32[2,8,64]{2,1,0:T(8,128)S(1)}, f32[2,8,64]{2,1,0:T(8,128)S(1)}, u32[]{:S(2)}, u32[]{:S(2)}) %collective-permute-start.13) | collective-permute-done | bytes 4128 | tf_op jit(solution)/shard_map/ppermute | solution.py:29
  35.9 0.6 %final.1 = (f32[8,64]{1,0:T(8,128)}, f32[8,64]{1,0:T(8,128)}) custom-call(f32[2,8,64]{2,1,0:T(8,128)S(1)} %merged.1.placed_ref, f32[2,8,64]{2,1,0:T(8,128)S(1)} %collective-permute-done.14.arrived_ref), custom_call_target="tpu_custom_call" | custom-call | bytes 8192 | tf_op jit(solution)/shard_map/final/pallas_call | solution.py:44
  (19 shorter events, 0.1 us)
Async XLA Ops:
  0.6 12.1 %collective-permute-start.5 = (bf16[1024,768]{1,0:T(8,128)(2,1)}, bf16[1024,768]{1,0:T(8,128)(2,1)S(1)}, u32[]{:S(2)}, u32[]{:S(2)}) collective-permute-start(bf16[1024,768]{1,0:T(8,128)(2,1)} %bitcast.6), channel_id=1, source_target_pairs={{0,2},{1,3},{2,0},{3,1},{4,6},{5,7},{6,4},{7,5},{8,10},{9,11},{10,... | collective-permute-start | bytes 4718600 | tf_op jit(solution)/shard_map/ppermute | solution.py:29
  1.1 9.4 %collective-permute-start = (bf16[64,768]{1,0:T(8,128)(2,1)}, bf16[64,768]{1,0:T(8,128)(2,1)S(1)}, u32[]{:S(2)}, u32[]{:S(2)}) collective-permute-start(bf16[64,768]{1,0:T(8,128)(2,1)} %refs_2_.1), channel_id=1, source_target_pairs={{0,16},{1,17},{2,18},{3,19},{4,20},{5,21},{6,22},{7,23},{8,24},{9,... | collective-permute-start | bytes 294920 | tf_op jit(solution)/shard_map/ppermute | solution.py:29
  4.8 5.7 %collective-permute-start.1 = (bf16[64,768]{1,0:T(8,128)(2,1)}, bf16[64,768]{1,0:T(8,128)(2,1)S(1)}, u32[]{:S(2)}, u32[]{:S(2)}) collective-permute-start(bf16[64,768]{1,0:T(8,128)(2,1)} %refs_2_.1), channel_id=1, source_target_pairs={{0,1},{1,0},{2,6},{3,7},{4,5},{5,4},{6,2},{7,3},{8,9},{9,8},{10,14... | collective-permute-start | bytes 294920 | tf_op jit(solution)/shard_map/ppermute | solution.py:29
  6.3 4.8 %collective-permute-start.2 = (bf16[64,768]{1,0:T(8,128)(2,1)}, bf16[64,768]{1,0:T(8,128)(2,1)S(1)}, u32[]{:S(2)}, u32[]{:S(2)}) collective-permute-start(bf16[64,768]{1,0:T(8,128)(2,1)} %refs_2_.1), channel_id=1, source_target_pairs={{0,4},{1,5},{2,3},{3,2},{4,0},{5,1},{6,7},{7,6},{8,12},{9,13},{10,... | collective-permute-start | bytes 294920 | tf_op jit(solution)/shard_map/ppermute | solution.py:29
  7.9 4.9 %collective-permute-start.4 = (bf16[64,768]{1,0:T(8,128)(2,1)}, bf16[64,768]{1,0:T(8,128)(2,1)S(1)}, u32[]{:S(2)}, u32[]{:S(2)}) collective-permute-start(bf16[64,768]{1,0:T(8,128)(2,1)} %refs_2_.1), channel_id=1, source_target_pairs={{0,8},{1,9},{2,10},{3,11},{4,12},{5,13},{6,14},{7,15},{8,0},{9,1},... | collective-permute-start | bytes 294920 | tf_op jit(solution)/shard_map/ppermute | solution.py:29
  11.1 5.0 %collective-permute-start.3 = (bf16[64,768]{1,0:T(8,128)(2,1)S(1)}, bf16[64,768]{1,0:T(8,128)(2,1)S(1)}, u32[]{:S(2)}, u32[]{:S(2)}) collective-permute-start(bf16[64,768]{1,0:T(8,128)(2,1)S(1)} %collective-permute-done.refs_6_), channel_id=1, source_target_pairs={{0,8},{1,9},{2,10},{3,11},{4,12},{5,13},{6,14},{7,15},{8,0},{9,1},... | collective-permute-start | bytes 294920 | tf_op jit(solution)/shard_map/ppermute | solution.py:29
  12.7 6.0 %collective-permute-start.8 = (bf16[128,768]{1,0:T(8,128)(2,1)S(1)}, bf16[128,768]{1,0:T(8,128)(2,1)S(1)}, u32[]{:S(2)}, u32[]{:S(2)}) collective-permute-start(bf16[128,768]{1,0:T(8,128)(2,1)S(1)} %pad_maximum_fusion.2), channel_id=1, source_target_pairs={{0,1},{1,0},{2,6},{3,7},{4,5},{5,4},{6,2},{7,3},{8,9},{9,8},{10,14... | collective-permute-start | bytes 589832 | tf_op jit(solution)/shard_map/ppermute | solution.py:29
  14.6 1.4 %copy-start = (bf16[16,64,768]{2,1,0:T(8,128)(2,1)S(1)}, bf16[16,64,768]{2,1,0:T(8,128)(2,1)}, u32[]{:S(2)}) copy-start(bf16[16,64,768]{2,1,0:T(8,128)(2,1)} %param.4) | copy-start | bytes 4718596
  16.1 6.8 %copy-start.2 = (bf16[64,768]{1,0:T(8,128)(2,1)S(1)}, bf16[64,768]{1,0:T(8,128)(2,1)}, u32[]{:S(2)}) copy-start(bf16[64,768]{1,0:T(8,128)(2,1)} %refs_2_.1) | copy-start | bytes 294916
  16.1 5.8 %collective-permute-start.6 = (bf16[64,768]{1,0:T(8,128)(2,1)S(1)}, bf16[64,768]{1,0:T(8,128)(2,1)S(1)}, u32[]{:S(2)}, u32[]{:S(2)}) collective-permute-start(bf16[64,768]{1,0:T(8,128)(2,1)S(1)} %collective-permute-done.3.refs_8_), channel_id=1, source_target_pairs={{0,1},{1,0},{2,6},{3,7},{4,5},{5,4},{6,2},{7,3},{8,9},{9,8},{10,14... | collective-permute-start | bytes 294920 | tf_op jit(solution)/shard_map/ppermute | solution.py:29
  17.2 7.5 %collective-permute-start.10 = (bf16[192,768]{1,0:T(8,128)(2,1)S(1)}, bf16[192,768]{1,0:T(8,128)(2,1)S(1)}, u32[]{:S(2)}, u32[]{:S(2)}) collective-permute-start(bf16[192,768]{1,0:T(8,128)(2,1)S(1)} %pad_maximum_fusion.1), channel_id=1, source_target_pairs={{0,4},{1,5},{2,3},{3,2},{4,0},{5,1},{6,7},{7,6},{8,12},{9,13},{10,... | collective-permute-start | bytes 884744 | tf_op jit(solution)/shard_map/ppermute | solution.py:29
  18.8 8.3 %collective-permute-start.9 = (bf16[192,768]{1,0:T(8,128)(2,1)S(1)}, bf16[192,768]{1,0:T(8,128)(2,1)S(1)}, u32[]{:S(2)}, u32[]{:S(2)}) collective-permute-start(bf16[192,768]{1,0:T(8,128)(2,1)S(1)} %pad_maximum_fusion), channel_id=1, source_target_pairs={{0,4},{1,5},{2,3},{3,2},{4,0},{5,1},{6,7},{7,6},{8,12},{9,13},{10,... | collective-permute-start | bytes 884744 | tf_op jit(solution)/shard_map/ppermute | solution.py:29
  21.9 6.3 %collective-permute-start.7 = (bf16[64,768]{1,0:T(8,128)(2,1)S(1)}, bf16[64,768]{1,0:T(8,128)(2,1)S(1)}, u32[]{:S(2)}, u32[]{:S(2)}) collective-permute-start(bf16[64,768]{1,0:T(8,128)(2,1)S(1)} %collective-permute-done.6.refs_2_), channel_id=1, source_target_pairs={{0,4},{1,5},{2,3},{3,2},{4,0},{5,1},{6,7},{7,6},{8,12},{9,13},{10,... | collective-permute-start | bytes 294920 | tf_op jit(solution)/shard_map/ppermute | solution.py:29
  27.1 2.5 %copy-start.1 = (s32[16]{0:T(128)S(1)}, s32[16]{0:T(128)}, u32[]{:S(2)}) copy-start(s32[16]{0:T(128)} %param.6) | copy-start | bytes 196
  28.2 1.4 %collective-permute-start.11 = (bf16[64,768]{1,0:T(8,128)(2,1)S(1)}, bf16[64,768]{1,0:T(8,128)(2,1)S(1)}, u32[]{:S(2)}, u32[]{:S(2)}) collective-permute-start(bf16[64,768]{1,0:T(8,128)(2,1)S(1)} %collective-permute-done.7.refs_0_), channel_id=1, source_target_pairs={{0,2},{1,3},{2,0},{3,1},{4,6},{5,7},{6,4},{7,5},{8,10},{9,11},{10,... | collective-permute-start | bytes 294920 | tf_op jit(solution)/shard_map/ppermute | solution.py:29
  28.2 1.4 %collective-permute-start.12 = (f32[16,1024]{1,0:T(8,128)S(1)}, f32[16,1024]{1,0:T(8,128)S(1)}, u32[]{:S(2)}, u32[]{:S(2)}) collective-permute-start(f32[16,1024]{1,0:T(8,128)S(1)} %get-tuple-element.36), channel_id=1, source_target_pairs={{0,2},{1,3},{2,0},{3,1},{4,6},{5,7},{6,4},{7,5},{8,10},{9,11},{10,... | collective-permute-start | bytes 196616 | tf_op jit(solution)/shard_map/ppermute | solution.py:29
  29.6 6.3 %collective-permute-start.13 = (f32[2,8,64]{2,1,0:T(8,128)S(1)}, f32[2,8,64]{2,1,0:T(8,128)S(1)}, u32[]{:S(2)}, u32[]{:S(2)}) collective-permute-start(f32[2,8,64]{2,1,0:T(8,128)S(1)} %get-tuple-element.40), channel_id=1, source_target_pairs={{0,2},{1,3},{2,4},{3,5},{4,6},{5,7},{6,8},{7,9},{8,10},{9,11},{10,... | collective-permute-start | bytes 12296 | tf_op jit(solution)/shard_map/ppermute | solution.py:29
  31.6 4.3 %collective-permute-start.14 = (f32[2,8,64]{2,1,0:T(8,128)S(1)}, f32[2,8,64]{2,1,0:T(8,128)S(1)}, u32[]{:S(2)}, u32[]{:S(2)}) collective-permute-start(f32[2,8,64]{2,1,0:T(8,128)S(1)} %get-tuple-element.41), channel_id=1, source_target_pairs={{0,2},{1,3},{2,0},{3,1},{4,6},{5,7},{6,4},{7,5},{8,10},{9,11},{10,... | collective-permute-start | bytes 12296 | tf_op jit(solution)/shard_map/ppermute | solution.py:29

commit v5 on v4

--- a/solution.py
+++ b/solution.py
@@ -83,11 +83,11 @@
         packed_ref[here, :] = jnp.where(usable, own_ref[here, :], partner_ref[theirs, :])
 
 
-def pack(line_counts, own, partner, slots, block_rows):
+def pack(counts, own, partner, slots, block_rows):
     return call(
         functools.partial(pack_kernel, slots, block_rows),
         (jax.ShapeDtypeStruct(own.shape, own.dtype),),
-        (line_counts.reshape(1, 1), own, partner),
+        (counts, own, partner),
         (VMEM, VMEM, VMEM),
         name="pack",
     )[0]
@@ -231,9 +231,9 @@
                     ref[index, row : row + 1, :] = jnp.min(picked, axis=0, keepdims=True)
 
 
-def last(parity, keep, line_counts, destinations, own, banks, mine, returned, norms, block_rows):
+def last(parity, keep, counts, destinations, own, banks, mine, returned, norms, block_rows):
     lines, features = own.shape
-    counts, to = line_counts.reshape(1, 1), destinations.reshape(1, -1)
+    to = destinations.reshape(1, -1)
     operands = (counts, to, own, *banks, mine, returned, norms, keep)
     placed = jax.ShapeDtypeStruct(keep.shape, keep.dtype)
     return call(
@@ -296,6 +296,7 @@
     places = slots // 2
     own = line_blocks.reshape(slots * sub_rows, features)
     partner_of = across("line", 0)
+    counts = line_counts.reshape(1, 1)
     partner = moved(own, partner_of)
 
     far = [("line", bit) for bit in range(2, hosts.bit_length() - 1)]
@@ -304,25 +305,26 @@
     turned, straight = by_parity(by_line, by_column), by_parity(by_column, by_line)
 
     distant = moved(centroids, across(*far[-1]))
+    near = moved(centroids, straight)
     level = doubled([centroids], far[:-1])[1:]
+    packed = pack(counts, own, partner, slots, block_rows)
+    norms = line_norms(packed, slots)
+    empty = jnp.full((2 * SUBLANES, own.shape[0]), HUGE_DISTANCE, jnp.float32)
+    distant, near, counts = lax.optimization_barrier((distant, near, counts))
+    beyond = doubled([distant], far[:-1])[1:]
     level, partner = lax.optimization_barrier((level, partner))
-    near = moved(centroids, straight)
-    side = moved(centroids, turned)
-    distant, near, side = lax.optimization_barrier((distant, near, side))
-    beyond = doubled([distant], far[:-1])[1:]
-    packed = pack(line_counts, own, partner, slots, block_rows)
-    beyond, packed = lax.optimization_barrier((beyond, packed))
-    norms = line_norms(packed, slots)
     near_level = moved(stacked([*level, distant]), straight)
-    crossed_level = moved(stacked([near, *level, distant]), turned)
-    near_beyond = moved(stacked(beyond), straight)
-    crossed_beyond = moved(stacked([near_level, *beyond]), turned)
-    corner = moved(near_beyond, turned)
-
+    crossed_level = moved(stacked([centroids, near, *level, distant]), turned)
+    near_beyond = moved(stacked([*beyond]), straight)
     lines = (packed, partner)
-    empty = jnp.full((2 * SUBLANES, own.shape[0]), HUGE_DISTANCE, jnp.float32)
-    states = absorb((empty, empty), (centroids, near, side, *level, distant, near_level, *beyond), lines)
-    states = absorb(states, (near_beyond, crossed_level), lines)
+    states = (empty, empty)
+    to_turned = stacked([near_level, *beyond])
+    crossed_beyond = moved(to_turned, turned)
+    near_last = near_beyond
+    near_last, norms = lax.optimization_barrier((near_last, norms))
+    corner = moved(near_last, turned)
+    states = absorb(states, (centroids, near, *level, distant, near_level), lines)
+    states = absorb(states, (near_beyond, *beyond, crossed_level), lines)
     mine, theirs = absorb(states, (crossed_beyond,), lines, give=True)
     returned = moved(theirs, partner_of)
     corner, mine, norms = lax.optimization_barrier((corner, mine, norms))
@@ -334,7 +336,7 @@
         placed, sends[parity] = last(
             parity,
             placed,
-            line_counts,
+            counts,
             destinations,
             packed,
             banks,

time: 36.7 us -> 35.5 us (0.967)
  starting transfers between devices: 18.3 us -> 15.7 us
  waiting for transfers between devices: 9.25 us -> 11.1 us
  local copies, waits for them, and re-layouts: 1.43 us -> 0.03 us
  other arithmetic: 0.05 us -> 0.95 us
    ppermute x15 -> x14, starting transfers between devices: 18.3 us -> 15.7 us  [moved(): return lax.ppermute(value, AXES, route)]
    ppermute x15 -> x14, waiting for transfers between devices: 9.25 us -> 11.1 us  [moved(): return lax.ppermute(value, AXES, route)]
    unnamed x6, local copies, waits for them, and re-layouts: 1.41 us -> 0.01 us
    concatenate x3, other arithmetic: 0.05 us -> 0.95 us  [stacked(): return jnp.concatenate(pieces, axis=0) if len(pieces) > 1 else pieces[0]]
  transfers between devices with their start and end apart: 15 -> 14, of which waited for: 7 -> 7; matrix products, arithmetic and copies ran while one was open for 0% -> 3% of each run, Pallas kernels for 15% -> 16%
where the time goes in v5:
time: 35.5 us; the launch traced here: 35.4 us
  starting transfers between devices  15.7 us (44%)
  waiting for transfers between devices  11.1 us (31%)
  Pallas kernels  6.14 us (17%)
  between operations  1.4 us (4%)
  other arithmetic  0.95 us (3%)
    ppermute x14, starting transfers between devices, moved(): return lax.ppermute(value, AXES, route)  15.7 us
    ppermute x14, waiting for transfers between devices, moved(): return lax.ppermute(value, AXES, route)  11.1 us
    pallas_call x9, Pallas kernels, call(): pl.pallas_call(body, in_specs=list(spaces), out_specs=(VMEM,) * len(outs)...  6.14 us
    concatenate x3, other arithmetic, stacked(): return jnp.concatenate(pieces, axis=0) if len(pieces) > 1 else pieces[0]  0.95 us
  transfers between devices with their start and end apart: 14, of which 7 were waited for; matrix products, arithmetic and copies ran while one was open for 3% of the time, Pallas kernels for 16%

profile of v5, /device:TPU:0, one launch (start us, length us, event | category | flops | bytes accessed | tf_op | source)
XLA Modules:
  0.0 35.4 jit_solution(8668400558382667955)
XLA Ops:
  0.6 0.5 %collective-permute-start.2 = (bf16[1024,768]{1,0:T(8,128)(2,1)}, bf16[1024,768]{1,0:T(8,128)(2,1)S(1)}, u32[]{:S(2)}, u32[]{:S(2)}) collective-permute-start(bf16[1024,768]{1,0:T(8,128)(2,1)} %bitcast.6), channel_id=1, source_target_pairs={{0,2},{1,3},{2,0},{3,1},{4,6},{5,7},{6,4},{7,5},{8,10},{9,11},{10,... | collective-permute-start | bytes 4718600 | tf_op jit(solution)/shard_map/ppermute | solution.py:29
  1.2 3.7 %collective-permute-start = (bf16[64,768]{1,0:T(8,128)(2,1)}, bf16[64,768]{1,0:T(8,128)(2,1)S(1)}, u32[]{:S(2)}, u32[]{:S(2)}) collective-permute-start(bf16[64,768]{1,0:T(8,128)(2,1)} %refs_2_.1), channel_id=1, source_target_pairs={{0,16},{1,17},{2,18},{3,19},{4,20},{5,21},{6,22},{7,23},{8,24},{9,... | collective-permute-start | bytes 294920 | tf_op jit(solution)/shard_map/ppermute | solution.py:29
  4.8 1.5 %collective-permute-start.1 = (bf16[64,768]{1,0:T(8,128)(2,1)}, bf16[64,768]{1,0:T(8,128)(2,1)S(1)}, u32[]{:S(2)}, u32[]{:S(2)}) collective-permute-start(bf16[64,768]{1,0:T(8,128)(2,1)} %refs_2_.1), channel_id=1, source_target_pairs={{0,1},{1,0},{2,6},{3,7},{4,5},{5,4},{6,2},{7,3},{8,9},{9,8},{10,14... | collective-permute-start | bytes 294920 | tf_op jit(solution)/shard_map/ppermute | solution.py:29
  6.3 1.6 %collective-permute-start.6 = (bf16[64,768]{1,0:T(8,128)(2,1)}, bf16[64,768]{1,0:T(8,128)(2,1)S(1)}, u32[]{:S(2)}, u32[]{:S(2)}) collective-permute-start(bf16[64,768]{1,0:T(8,128)(2,1)} %refs_2_.1), channel_id=1, source_target_pairs={{0,8},{1,9},{2,10},{3,11},{4,12},{5,13},{6,14},{7,15},{8,0},{9,1},... | collective-permute-start | bytes 294920 | tf_op jit(solution)/shard_map/ppermute | solution.py:29
  7.9 2.7 %collective-permute-done.refs_5_ = bf16[64,768]{1,0:T(8,128)(2,1)S(1)} collective-permute-done((bf16[64,768]{1,0:T(8,128)(2,1)}, bf16[64,768]{1,0:T(8,128)(2,1)S(1)}, u32[]{:S(2)}, u32[]{:S(2)}) %collective-permute-start) | collective-permute-done | bytes 98336 | tf_op jit(solution)/shard_map/ppermute | solution.py:29
  10.6 0.8 %collective-permute-start.3 = (bf16[64,768]{1,0:T(8,128)(2,1)S(1)}, bf16[64,768]{1,0:T(8,128)(2,1)S(1)}, u32[]{:S(2)}, u32[]{:S(2)}) collective-permute-start(bf16[64,768]{1,0:T(8,128)(2,1)S(1)} %collective-permute-done.refs_5_), channel_id=1, source_target_pairs={{0,8},{1,9},{2,10},{3,11},{4,12},{5,13},{6,14},{7,15},{8,0},{9,1},... | collective-permute-start | bytes 294920 | tf_op jit(solution)/shard_map/ppermute | solution.py:29
  11.4 0.6 %collective-permute-done.6.refs_4_ = bf16[64,768]{1,0:T(8,128)(2,1)S(1)} collective-permute-done((bf16[64,768]{1,0:T(8,128)(2,1)}, bf16[64,768]{1,0:T(8,128)(2,1)S(1)}, u32[]{:S(2)}, u32[]{:S(2)}) %collective-permute-start.6) | collective-permute-done | bytes 98336 | tf_op jit(solution)/shard_map/ppermute | solution.py:29
  12.1 1.6 %collective-permute-start.7 = (bf16[128,768]{1,0:T(8,128)(2,1)S(1)}, bf16[128,768]{1,0:T(8,128)(2,1)S(1)}, u32[]{:S(2)}, u32[]{:S(2)}) collective-permute-start(bf16[128,768]{1,0:T(8,128)(2,1)S(1)} %pad_maximum_fusion.2), channel_id=1, source_target_pairs={{0,1},{1,0},{2,6},{3,7},{4,5},{5,4},{6,2},{7,3},{8,9},{9,8},{10,14... | collective-permute-start | bytes 589832 | tf_op jit(solution)/shard_map/ppermute | solution.py:29
  13.7 0.9 %pad_maximum_fusion = bf16[256,768]{1,0:T(8,128)(2,1)S(1)} fusion(bf16[64,768]{1,0:T(8,128)(2,1)S(1)} %collective-permute-done.refs_5_, bf16[64,768]{1,0:T(8,128)(2,1)S(1)} %collective-permute-done.6.refs_4_, bf16[64,768]{1,0:T(8,128)(2,1)S(1)} %collective-permute-done.1.refs_3_, bf16[64,768]{1,0:T(8,128)(2,1)} %refs_2_.1), kind=kLoop, calls=%fused_computation | loop fusion | flops 1572864 | bytes 786432 | tf_op jit(solution)/shard_map/concatenate | solution.py:283
  14.6 0.8 %collective-permute-start.9 = (bf16[256,768]{1,0:T(8,128)(2,1)S(1)}, bf16[256,768]{1,0:T(8,128)(2,1)S(1)}, u32[]{:S(2)}, u32[]{:S(2)}) collective-permute-start(bf16[256,768]{1,0:T(8,128)(2,1)S(1)} %pad_maximum_fusion), channel_id=1, source_target_pairs={{0,4},{1,5},{2,3},{3,2},{4,0},{5,1},{6,7},{7,6},{8,12},{9,13},{10,... | collective-permute-start | bytes 1179656 | tf_op jit(solution)/shard_map/ppermute | solution.py:29
  15.5 0.0 collective-permute-done.3.refs_3_
  15.5 1.3 %collective-permute-start.4 = (bf16[64,768]{1,0:T(8,128)(2,1)S(1)}, bf16[64,768]{1,0:T(8,128)(2,1)S(1)}, u32[]{:S(2)}, u32[]{:S(2)}) collective-permute-start(bf16[64,768]{1,0:T(8,128)(2,1)S(1)} %collective-permute-done.3.refs_3_), channel_id=1, source_target_pairs={{0,1},{1,0},{2,6},{3,7},{4,5},{5,4},{6,2},{7,3},{8,9},{9,8},{10,14... | collective-permute-start | bytes 294920 | tf_op jit(solution)/shard_map/ppermute | solution.py:29
  16.8 2.8 %collective-permute-done.7.refs_6_ = bf16[128,768]{1,0:T(8,128)(2,1)S(1)} collective-permute-done((bf16[128,768]{1,0:T(8,128)(2,1)S(1)}, bf16[128,768]{1,0:T(8,128)(2,1)S(1)}, u32[]{:S(2)}, u32[]{:S(2)}) %collective-permute-start.7) | collective-permute-done | bytes 196640 | tf_op jit(solution)/shard_map/ppermute | solution.py:29
  19.6 1.1 %collective-permute-start.8 = (bf16[192,768]{1,0:T(8,128)(2,1)S(1)}, bf16[192,768]{1,0:T(8,128)(2,1)S(1)}, u32[]{:S(2)}, u32[]{:S(2)}) collective-permute-start(bf16[192,768]{1,0:T(8,128)(2,1)S(1)} %pad_maximum_fusion.1), channel_id=1, source_target_pairs={{0,4},{1,5},{2,3},{3,2},{4,0},{5,1},{6,7},{7,6},{8,12},{9,13},{10,... | collective-permute-start | bytes 884744 | tf_op jit(solution)/shard_map/ppermute | solution.py:29
  21.4 0.1 pack.1.own_ref.refs_0_.lines_ref
  21.5 0.0 copy-start.1
  21.5 1.1 %line_norms.1.refs_4_ = f32[16,64]{1,0:T(8,128)S(1)} custom-call(bf16[1024,768]{1,0:T(8,128)(2,1)S(1)} %pack.1.own_ref.refs_0_.lines_ref), custom_call_target="tpu_custom_call" | custom-call | flops 201326592 | bytes 1572864 | tf_op jit(solution)/shard_map/line_norms/pallas_call | solution.py:44
  22.6 0.0 collective-permute-done.4.refs_2_
  22.6 1.0 %collective-permute-start.5 = (bf16[64,768]{1,0:T(8,128)(2,1)S(1)}, bf16[64,768]{1,0:T(8,128)(2,1)S(1)}, u32[]{:S(2)}, u32[]{:S(2)}) collective-permute-start(bf16[64,768]{1,0:T(8,128)(2,1)S(1)} %collective-permute-done.4.refs_2_), channel_id=1, source_target_pairs={{0,4},{1,5},{2,3},{3,2},{4,0},{5,1},{6,7},{7,6},{8,12},{9,13},{10,... | collective-permute-start | bytes 294920 | tf_op jit(solution)/shard_map/ppermute | solution.py:29
  23.7 1.3 %absorb.3 = (f32[16,1024]{1,0:T(8,128)S(1)}, f32[16,1024]{1,0:T(8,128)S(1)}) custom-call(bf16[1024,768]{1,0:T(8,128)(2,1)S(1)} %pack.1.own_ref.refs_0_.lines_ref, bf16[1024,768]{1,0:T(8,128)(2,1)S(1)} %collective-permute-done.2.partner_ref.refs_1_, bf16[64,768]{1,0:T(8,128)(2,1)S(1)} %copy-done.1, ...), custom_call_target="tpu_custom_call", output_to_operand_aliasing={{0}: (7, {}), {1}: (8, {})} | custom-call | flops 1207959552 | bytes 3866624 | tf_op jit(solution)/shard_map/absorb/pallas_call | solution.py:44
  25.0 1.3 %absorb.4 = (f32[16,1024]{1,0:T(8,128)S(1)}, f32[16,1024]{1,0:T(8,128)S(1)}) custom-call(bf16[1024,768]{1,0:T(8,128)(2,1)S(1)} %pack.1.own_ref.refs_0_.lines_ref, bf16[1024,768]{1,0:T(8,128)(2,1)S(1)} %collective-permute-done.2.partner_ref.refs_1_, bf16[64,768]{1,0:T(8,128)(2,1)S(1)} %collective-permute-done.4.refs_2_, ...), custom_call_target="tpu_custom_call", output_to_operand_aliasing={{0}: (5, {}), {1}: (6, {})} | custom-call | flops 1207959552 | bytes 3866624 | tf_op jit(solution)/shard_map/absorb/pallas_call | solution.py:44
  26.3 0.1 collective-permute-done.8.refs_2_
  26.4 0.9 %absorb.5 = (f32[16,1024]{1,0:T(8,128)S(1)}, f32[16,1024]{1,0:T(8,128)S(1)}) custom-call(bf16[1024,768]{1,0:T(8,128)(2,1)S(1)} %pack.1.own_ref.refs_0_.lines_ref, bf16[1024,768]{1,0:T(8,128)(2,1)S(1)} %collective-permute-done.2.partner_ref.refs_1_, ...), custom_call_target="tpu_custom_call", output_to_operand_aliasing={{0}: (3, {}), {1}: (4, {})} | custom-call | flops 603979776 | bytes 3571712 | tf_op jit(solution)/shard_map/absorb/pallas_call | solution.py:44
  27.4 0.1 collective-permute-done.5.refs_0_
  27.5 0.0 collective-permute-start.10
  27.5 0.5 %collective-permute-start.11 = (f32[16,1024]{1,0:T(8,128)S(1)}, f32[16,1024]{1,0:T(8,128)S(1)}, u32[]{:S(2)}, u32[]{:S(2)}) collective-permute-start(f32[16,1024]{1,0:T(8,128)S(1)} %get-tuple-element.36), channel_id=1, source_target_pairs={{0,2},{1,3},{2,0},{3,1},{4,6},{5,7},{6,4},{7,5},{8,10},{9,11},{10,... | collective-permute-start | bytes 196616 | tf_op jit(solution)/shard_map/ppermute | solution.py:29
  28.0 0.9 %collective-permute-done.11.refs_3_ = f32[16,1024]{1,0:T(8,128)S(1)} collective-permute-done((f32[16,1024]{1,0:T(8,128)S(1)}, f32[16,1024]{1,0:T(8,128)S(1)}, u32[]{:S(2)}, u32[]{:S(2)}) %collective-permute-start.11) | collective-permute-done | bytes 65568 | tf_op jit(solution)/shard_map/ppermute | solution.py:29
  28.9 1.2 %collective-permute-start.12 = (f32[2,8,64]{2,1,0:T(8,128)S(1)}, f32[2,8,64]{2,1,0:T(8,128)S(1)}, u32[]{:S(2)}, u32[]{:S(2)}) collective-permute-start(f32[2,8,64]{2,1,0:T(8,128)S(1)} %get-tuple-element.40), channel_id=1, source_target_pairs={{0,2},{1,3},{2,4},{3,5},{4,6},{5,7},{6,8},{7,9},{8,10},{9,11},{10,... | collective-permute-start | bytes 12296 | tf_op jit(solution)/shard_map/ppermute | solution.py:29
  30.1 0.8 %last.3 = (f32[2,8,64]{2,1,0:T(8,128)S(1)}, f32[2,8,64]{2,1,0:T(8,128)S(1)}) custom-call(s32[1,1]{1,0:T(1,128)} %bitcast.4.count_ref, s32[1,16]{1,0:T(1,128)S(1)} %bitcast.9, bf16[1024,768]{1,0:T(8,128)(2,1)S(1)} %pack.1.own_ref.refs_0_.lines_ref, bf16[64,768]{1,0:T(8,128)(2,1)S(1)} %collective-permute-done.5.refs_0_, ...), custom_call_target="tpu_custom_call", output_to_operand_aliasing={{0}: (8, {})} | custom-call | flops 201326592 | bytes 1908804 | tf_op jit(solution)/shard_map/last/pallas_call | solution.py:44
  30.9 0.1 collective-permute-start.13
  31.0 3.8 %collective-permute-done.12.arrived_ref = f32[2,8,64]{2,1,0:T(8,128)S(1)} collective-permute-done((f32[2,8,64]{2,1,0:T(8,128)S(1)}, f32[2,8,64]{2,1,0:T(8,128)S(1)}, u32[]{:S(2)}, u32[]{:S(2)}) %collective-permute-start.12) | collective-permute-done | bytes 4128 | tf_op jit(solution)/shard_map/ppermute | solution.py:29
  34.8 0.6 %final.1 = (f32[8,64]{1,0:T(8,128)}, f32[8,64]{1,0:T(8,128)}) custom-call(f32[2,8,64]{2,1,0:T(8,128)S(1)} %merged.1.placed_ref, f32[2,8,64]{2,1,0:T(8,128)S(1)} %collective-permute-done.13.arrived_ref), custom_call_target="tpu_custom_call" | custom-call | bytes 8192 | tf_op jit(solution)/shard_map/final/pallas_call | solution.py:44
  (17 shorter events, 0.1 us)
Async XLA Ops:
  0.6 20.7 %copy-start = (bf16[16,64,768]{2,1,0:T(8,128)(2,1)S(1)}, bf16[16,64,768]{2,1,0:T(8,128)(2,1)}, u32[]{:S(2)}) copy-start(bf16[16,64,768]{2,1,0:T(8,128)(2,1)} %param.4) | copy-start | bytes 4718596
  0.6 11.4 %collective-permute-start.2 = (bf16[1024,768]{1,0:T(8,128)(2,1)}, bf16[1024,768]{1,0:T(8,128)(2,1)S(1)}, u32[]{:S(2)}, u32[]{:S(2)}) collective-permute-start(bf16[1024,768]{1,0:T(8,128)(2,1)} %bitcast.6), channel_id=1, source_target_pairs={{0,2},{1,3},{2,0},{3,1},{4,6},{5,7},{6,4},{7,5},{8,10},{9,11},{10,... | collective-permute-start | bytes 4718600 | tf_op jit(solution)/shard_map/ppermute | solution.py:29
  1.2 9.5 %collective-permute-start = (bf16[64,768]{1,0:T(8,128)(2,1)}, bf16[64,768]{1,0:T(8,128)(2,1)S(1)}, u32[]{:S(2)}, u32[]{:S(2)}) collective-permute-start(bf16[64,768]{1,0:T(8,128)(2,1)} %refs_2_.1), channel_id=1, source_target_pairs={{0,16},{1,17},{2,18},{3,19},{4,20},{5,21},{6,22},{7,23},{8,24},{9,... | collective-permute-start | bytes 294920 | tf_op jit(solution)/shard_map/ppermute | solution.py:29
  4.8 5.8 %collective-permute-start.1 = (bf16[64,768]{1,0:T(8,128)(2,1)}, bf16[64,768]{1,0:T(8,128)(2,1)S(1)}, u32[]{:S(2)}, u32[]{:S(2)}) collective-permute-start(bf16[64,768]{1,0:T(8,128)(2,1)} %refs_2_.1), channel_id=1, source_target_pairs={{0,1},{1,0},{2,6},{3,7},{4,5},{5,4},{6,2},{7,3},{8,9},{9,8},{10,14... | collective-permute-start | bytes 294920 | tf_op jit(solution)/shard_map/ppermute | solution.py:29
  6.3 5.8 %collective-permute-start.6 = (bf16[64,768]{1,0:T(8,128)(2,1)}, bf16[64,768]{1,0:T(8,128)(2,1)S(1)}, u32[]{:S(2)}, u32[]{:S(2)}) collective-permute-start(bf16[64,768]{1,0:T(8,128)(2,1)} %refs_2_.1), channel_id=1, source_target_pairs={{0,8},{1,9},{2,10},{3,11},{4,12},{5,13},{6,14},{7,15},{8,0},{9,1},... | collective-permute-start | bytes 294920 | tf_op jit(solution)/shard_map/ppermute | solution.py:29
  10.6 4.8 %collective-permute-start.3 = (bf16[64,768]{1,0:T(8,128)(2,1)S(1)}, bf16[64,768]{1,0:T(8,128)(2,1)S(1)}, u32[]{:S(2)}, u32[]{:S(2)}) collective-permute-start(bf16[64,768]{1,0:T(8,128)(2,1)S(1)} %collective-permute-done.refs_5_), channel_id=1, source_target_pairs={{0,8},{1,9},{2,10},{3,11},{4,12},{5,13},{6,14},{7,15},{8,0},{9,1},... | collective-permute-start | bytes 294920 | tf_op jit(solution)/shard_map/ppermute | solution.py:29
  12.1 7.5 %collective-permute-start.7 = (bf16[128,768]{1,0:T(8,128)(2,1)S(1)}, bf16[128,768]{1,0:T(8,128)(2,1)S(1)}, u32[]{:S(2)}, u32[]{:S(2)}) collective-permute-start(bf16[128,768]{1,0:T(8,128)(2,1)S(1)} %pad_maximum_fusion.2), channel_id=1, source_target_pairs={{0,1},{1,0},{2,6},{3,7},{4,5},{5,4},{6,2},{7,3},{8,9},{9,8},{10,14... | collective-permute-start | bytes 589832 | tf_op jit(solution)/shard_map/ppermute | solution.py:29
  14.6 10.3 %collective-permute-start.9 = (bf16[256,768]{1,0:T(8,128)(2,1)S(1)}, bf16[256,768]{1,0:T(8,128)(2,1)S(1)}, u32[]{:S(2)}, u32[]{:S(2)}) collective-permute-start(bf16[256,768]{1,0:T(8,128)(2,1)S(1)} %pad_maximum_fusion), channel_id=1, source_target_pairs={{0,4},{1,5},{2,3},{3,2},{4,0},{5,1},{6,7},{7,6},{8,12},{9,13},{10,... | collective-permute-start | bytes 1179656 | tf_op jit(solution)/shard_map/ppermute | solution.py:29
  15.5 7.1 %collective-permute-start.4 = (bf16[64,768]{1,0:T(8,128)(2,1)S(1)}, bf16[64,768]{1,0:T(8,128)(2,1)S(1)}, u32[]{:S(2)}, u32[]{:S(2)}) collective-permute-start(bf16[64,768]{1,0:T(8,128)(2,1)S(1)} %collective-permute-done.3.refs_3_), channel_id=1, source_target_pairs={{0,1},{1,0},{2,6},{3,7},{4,5},{5,4},{6,2},{7,3},{8,9},{9,8},{10,14... | collective-permute-start | bytes 294920 | tf_op jit(solution)/shard_map/ppermute | solution.py:29
  19.6 6.8 %collective-permute-start.8 = (bf16[192,768]{1,0:T(8,128)(2,1)S(1)}, bf16[192,768]{1,0:T(8,128)(2,1)S(1)}, u32[]{:S(2)}, u32[]{:S(2)}) collective-permute-start(bf16[192,768]{1,0:T(8,128)(2,1)S(1)} %pad_maximum_fusion.1), channel_id=1, source_target_pairs={{0,4},{1,5},{2,3},{3,2},{4,0},{5,1},{6,7},{7,6},{8,12},{9,13},{10,... | collective-permute-start | bytes 884744 | tf_op jit(solution)/shard_map/ppermute | solution.py:29
  21.5 2.2 %copy-start.1 = (bf16[64,768]{1,0:T(8,128)(2,1)S(1)}, bf16[64,768]{1,0:T(8,128)(2,1)}, u32[]{:S(2)}) copy-start(bf16[64,768]{1,0:T(8,128)(2,1)} %refs_2_.1) | copy-start | bytes 294916
  22.6 4.9 %collective-permute-start.5 = (bf16[64,768]{1,0:T(8,128)(2,1)S(1)}, bf16[64,768]{1,0:T(8,128)(2,1)S(1)}, u32[]{:S(2)}, u32[]{:S(2)}) collective-permute-start(bf16[64,768]{1,0:T(8,128)(2,1)S(1)} %collective-permute-done.4.refs_2_), channel_id=1, source_target_pairs={{0,4},{1,5},{2,3},{3,2},{4,0},{5,1},{6,7},{7,6},{8,12},{9,13},{10,... | collective-permute-start | bytes 294920 | tf_op jit(solution)/shard_map/ppermute | solution.py:29
  26.4 2.5 %copy-start.2 = (s32[16]{0:T(128)S(1)}, s32[16]{0:T(128)}, u32[]{:S(2)}) copy-start(s32[16]{0:T(128)} %param.6) | copy-start | bytes 196
  27.5 1.4 %collective-permute-start.10 = (bf16[64,768]{1,0:T(8,128)(2,1)S(1)}, bf16[64,768]{1,0:T(8,128)(2,1)S(1)}, u32[]{:S(2)}, u32[]{:S(2)}) collective-permute-start(bf16[64,768]{1,0:T(8,128)(2,1)S(1)} %collective-permute-done.5.refs_0_), channel_id=1, source_target_pairs={{0,2},{1,3},{2,0},{3,1},{4,6},{5,7},{6,4},{7,5},{8,10},{9,11},{10,... | collective-permute-start | bytes 294920 | tf_op jit(solution)/shard_map/ppermute | solution.py:29
  27.5 1.4 %collective-permute-start.11 = (f32[16,1024]{1,0:T(8,128)S(1)}, f32[16,1024]{1,0:T(8,128)S(1)}, u32[]{:S(2)}, u32[]{:S(2)}) collective-permute-start(f32[16,1024]{1,0:T(8,128)S(1)} %get-tuple-element.36), channel_id=1, source_target_pairs={{0,2},{1,3},{2,0},{3,1},{4,6},{5,7},{6,4},{7,5},{8,10},{9,11},{10,... | collective-permute-start | bytes 196616 | tf_op jit(solution)/shard_map/ppermute | solution.py:29
  28.9 5.8 %collective-permute-start.12 = (f32[2,8,64]{2,1,0:T(8,128)S(1)}, f32[2,8,64]{2,1,0:T(8,128)S(1)}, u32[]{:S(2)}, u32[]{:S(2)}) collective-permute-start(f32[2,8,64]{2,1,0:T(8,128)S(1)} %get-tuple-element.40), channel_id=1, source_target_pairs={{0,2},{1,3},{2,4},{3,5},{4,6},{5,7},{6,8},{7,9},{8,10},{9,11},{10,... | collective-permute-start | bytes 12296 | tf_op jit(solution)/shard_map/ppermute | solution.py:29
  30.9 3.8 %collective-permute-start.13 = (f32[2,8,64]{2,1,0:T(8,128)S(1)}, f32[2,8,64]{2,1,0:T(8,128)S(1)}, u32[]{:S(2)}, u32[]{:S(2)}) collective-permute-start(f32[2,8,64]{2,1,0:T(8,128)S(1)} %get-tuple-element.41), channel_id=1, source_target_pairs={{0,2},{1,3},{2,0},{3,1},{4,6},{5,7},{6,4},{7,5},{8,10},{9,11},{10,... | collective-permute-start | bytes 12296 | tf_op jit(solution)/shard_map/ppermute | solution.py:29

commit v6 on v5

--- a/solution.py
+++ b/solution.py
@@ -1,4 +1,5 @@
 import functools
+import math
 
 import jax
 import jax.numpy as jnp
@@ -12,6 +13,7 @@
 BANK_TILE = 512
 LINE_STEP = 1024
 SUBLANES = 8
+LANES = 128
 VMEM_LIMIT = 16 * 2**20
 VMEM = pl.BlockSpec(memory_space=pltpu.VMEM)
 SMEM = pl.BlockSpec(memory_space=pltpu.SMEM)
@@ -103,12 +105,16 @@
 def norm_kernel(own_ref, norms_ref):
     slots, per_slot = norms_ref.shape
     lines, features = own_ref.shape
-    ones = jnp.ones((SUBLANES, features), jnp.bfloat16)
+    lanes = math.gcd(features, LANES)
     wide = own_ref[...].astype(jnp.float32)
     square = wide * wide
-    high = square.astype(jnp.bfloat16)
-    low = (square - high.astype(jnp.float32)).astype(jnp.bfloat16)
-    spread(norms_ref, (contract(ones, high) + contract(ones, low))[:1])
+    rest = sum(square[:, at : at + lanes] for at in range(0, features, lanes))
+    parts = []
+    for _ in range(3):
+        parts.append(rest.astype(jnp.bfloat16))
+        rest = rest - parts[-1].astype(jnp.float32)
+    ones = jnp.ones((SUBLANES, 3 * lanes), jnp.bfloat16)
+    spread(norms_ref, contract(ones, jnp.concatenate(parts, axis=1))[:1])
 
 
 def line_norms(own, slots):
@@ -129,8 +135,10 @@
 def absorbed(banks, lines, first, second):
     scaled, norms = prepared(banks)
     distance = contract(scaled, lines) + norms
-    for row in range(0, distance.shape[0], SUBLANES):
-        first, second = fold(first, second, distance[row : row + SUBLANES])
+    rows = distance.shape[0]
+    for row in range(0, rows, 2 * SUBLANES):
+        low, high = distance[row : row + SUBLANES], distance[row + SUBLANES : row + 2 * SUBLANES]
+        first, second = join(first, second, jnp.minimum(low, high), jnp.maximum(low, high))
     return first, second
 
 
@@ -310,7 +318,7 @@
     packed = pack(counts, own, partner, slots, block_rows)
     norms = line_norms(packed, slots)
     empty = jnp.full((2 * SUBLANES, own.shape[0]), HUGE_DISTANCE, jnp.float32)
-    distant, near, counts = lax.optimization_barrier((distant, near, counts))
+    distant, counts = lax.optimization_barrier((distant, counts))
     beyond = doubled([distant], far[:-1])[1:]
     level, partner = lax.optimization_barrier((level, partner))
     near_level = moved(stacked([*level, distant]), straight)

time: 35.5 us -> 35 us (0.986)
  starting transfers between devices: 15.7 us -> 17.4 us
  waiting for transfers between devices: 11.1 us -> 9.43 us
  Pallas kernels: 6.14 us -> 5.61 us
    ppermute x14, starting transfers between devices: 15.7 us -> 17.4 us  [moved(): return lax.ppermute(value, AXES, route)]
    ppermute x14, waiting for transfers between devices: 11.1 us -> 9.43 us  [moved(): return lax.ppermute(value, AXES, route)]
    pallas_call x9, Pallas kernels: 6.14 us -> 5.61 us  [call(): pl.pallas_call(body, in_specs=list(spaces), out_specs=(VMEM,) * len(outs)...]
  transfers between devices with their start and end apart: 14 -> 14, of which waited for: 7 -> 6; matrix products, arithmetic and copies ran while one was open for 3% -> 3% of each run, Pallas kernels for 16% -> 14%
where the time goes in v6:
time: 35 us; the launch traced here: 34.9 us
  starting transfers between devices  17.4 us (50%)
  waiting for transfers between devices  9.43 us (27%)
  Pallas kernels  5.61 us (16%)
  between operations  1.4 us (4%)
  other arithmetic  0.95 us (3%)
    ppermute x14, starting transfers between devices, moved(): return lax.ppermute(value, AXES, route)  17.4 us
    ppermute x14, waiting for transfers between devices, moved(): return lax.ppermute(value, AXES, route)  9.43 us
    pallas_call x9, Pallas kernels, call(): pl.pallas_call(body, in_specs=list(spaces), out_specs=(VMEM,) * len(outs)...  5.61 us
    concatenate x3, other arithmetic, stacked(): return jnp.concatenate(pieces, axis=0) if len(pieces) > 1 else pieces[0]  0.95 us
  transfers between devices with their start and end apart: 14, of which 6 were waited for; matrix products, arithmetic and copies ran while one was open for 3% of the time, Pallas kernels for 14%

profile of v6, /device:TPU:0, one launch (start us, length us, event | category | flops | bytes accessed | tf_op | source)
XLA Modules:
  0.0 34.9 jit_solution(4119406303226346993)
XLA Ops:
  0.6 0.5 %collective-permute-start.1 = (bf16[1024,768]{1,0:T(8,128)(2,1)}, bf16[1024,768]{1,0:T(8,128)(2,1)S(1)}, u32[]{:S(2)}, u32[]{:S(2)}) collective-permute-start(bf16[1024,768]{1,0:T(8,128)(2,1)} %bitcast.6), channel_id=1, source_target_pairs={{0,2},{1,3},{2,0},{3,1},{4,6},{5,7},{6,4},{7,5},{8,10},{9,11},{10,... | collective-permute-start | bytes 4718600 | tf_op jit(solution)/shard_map/ppermute | solution.py:31
  1.2 3.7 %collective-permute-start = (bf16[64,768]{1,0:T(8,128)(2,1)}, bf16[64,768]{1,0:T(8,128)(2,1)S(1)}, u32[]{:S(2)}, u32[]{:S(2)}) collective-permute-start(bf16[64,768]{1,0:T(8,128)(2,1)} %refs_2_.1), channel_id=1, source_target_pairs={{0,16},{1,17},{2,18},{3,19},{4,20},{5,21},{6,22},{7,23},{8,24},{9,... | collective-permute-start | bytes 294920 | tf_op jit(solution)/shard_map/ppermute | solution.py:31
  4.8 1.6 %collective-permute-start.5 = (bf16[64,768]{1,0:T(8,128)(2,1)}, bf16[64,768]{1,0:T(8,128)(2,1)S(1)}, u32[]{:S(2)}, u32[]{:S(2)}) collective-permute-start(bf16[64,768]{1,0:T(8,128)(2,1)} %refs_2_.1), channel_id=1, source_target_pairs={{0,8},{1,9},{2,10},{3,11},{4,12},{5,13},{6,14},{7,15},{8,0},{9,1},... | collective-permute-start | bytes 294920 | tf_op jit(solution)/shard_map/ppermute | solution.py:31
  6.4 1.5 %collective-permute-start.8 = (bf16[64,768]{1,0:T(8,128)(2,1)}, bf16[64,768]{1,0:T(8,128)(2,1)S(1)}, u32[]{:S(2)}, u32[]{:S(2)}) collective-permute-start(bf16[64,768]{1,0:T(8,128)(2,1)} %refs_2_.1), channel_id=1, source_target_pairs={{0,1},{1,0},{2,6},{3,7},{4,5},{5,4},{6,2},{7,3},{8,9},{9,8},{10,14... | collective-permute-start | bytes 294920 | tf_op jit(solution)/shard_map/ppermute | solution.py:31
  7.9 2.7 %collective-permute-done.refs_5_ = bf16[64,768]{1,0:T(8,128)(2,1)S(1)} collective-permute-done((bf16[64,768]{1,0:T(8,128)(2,1)}, bf16[64,768]{1,0:T(8,128)(2,1)S(1)}, u32[]{:S(2)}, u32[]{:S(2)}) %collective-permute-start) | collective-permute-done | bytes 98336 | tf_op jit(solution)/shard_map/ppermute | solution.py:31
  10.6 0.7 %collective-permute-start.2 = (bf16[64,768]{1,0:T(8,128)(2,1)S(1)}, bf16[64,768]{1,0:T(8,128)(2,1)S(1)}, u32[]{:S(2)}, u32[]{:S(2)}) collective-permute-start(bf16[64,768]{1,0:T(8,128)(2,1)S(1)} %collective-permute-done.refs_5_), channel_id=1, source_target_pairs={{0,8},{1,9},{2,10},{3,11},{4,12},{5,13},{6,14},{7,15},{8,0},{9,1},... | collective-permute-start | bytes 294920 | tf_op jit(solution)/shard_map/ppermute | solution.py:31
  11.4 0.0 collective-permute-done.5.refs_4_
  11.4 1.6 %collective-permute-start.6 = (bf16[128,768]{1,0:T(8,128)(2,1)S(1)}, bf16[128,768]{1,0:T(8,128)(2,1)S(1)}, u32[]{:S(2)}, u32[]{:S(2)}) collective-permute-start(bf16[128,768]{1,0:T(8,128)(2,1)S(1)} %pad_maximum_fusion.2), channel_id=1, source_target_pairs={{0,1},{1,0},{2,6},{3,7},{4,5},{5,4},{6,2},{7,3},{8,9},{9,8},{10,14... | collective-permute-start | bytes 589832 | tf_op jit(solution)/shard_map/ppermute | solution.py:31
  13.0 0.0 collective-permute-done.8.refs_3_
  13.0 0.9 %pad_maximum_fusion = bf16[256,768]{1,0:T(8,128)(2,1)S(1)} fusion(bf16[64,768]{1,0:T(8,128)(2,1)S(1)} %collective-permute-done.refs_5_, bf16[64,768]{1,0:T(8,128)(2,1)S(1)} %collective-permute-done.5.refs_4_, bf16[64,768]{1,0:T(8,128)(2,1)S(1)} %collective-permute-done.8.refs_3_, bf16[64,768]{1,0:T(8,128)(2,1)} %refs_2_.1), kind=kLoop, calls=%fused_computation | loop fusion | flops 1572864 | bytes 786432 | tf_op jit(solution)/shard_map/concatenate | solution.py:291
  13.9 1.6 %collective-permute-start.9 = (bf16[256,768]{1,0:T(8,128)(2,1)S(1)}, bf16[256,768]{1,0:T(8,128)(2,1)S(1)}, u32[]{:S(2)}, u32[]{:S(2)}) collective-permute-start(bf16[256,768]{1,0:T(8,128)(2,1)S(1)} %pad_maximum_fusion), channel_id=1, source_target_pairs={{0,4},{1,5},{2,3},{3,2},{4,0},{5,1},{6,7},{7,6},{8,12},{9,13},{10,... | collective-permute-start | bytes 1179656 | tf_op jit(solution)/shard_map/ppermute | solution.py:31
  15.5 1.3 %collective-permute-start.3 = (bf16[64,768]{1,0:T(8,128)(2,1)S(1)}, bf16[64,768]{1,0:T(8,128)(2,1)S(1)}, u32[]{:S(2)}, u32[]{:S(2)}) collective-permute-start(bf16[64,768]{1,0:T(8,128)(2,1)S(1)} %collective-permute-done.2.refs_3_), channel_id=1, source_target_pairs={{0,1},{1,0},{2,6},{3,7},{4,5},{5,4},{6,2},{7,3},{8,9},{9,8},{10,14... | collective-permute-start | bytes 294920 | tf_op jit(solution)/shard_map/ppermute | solution.py:31
  16.8 1.4 %collective-permute-done.6.refs_6_ = bf16[128,768]{1,0:T(8,128)(2,1)S(1)} collective-permute-done((bf16[128,768]{1,0:T(8,128)(2,1)S(1)}, bf16[128,768]{1,0:T(8,128)(2,1)S(1)}, u32[]{:S(2)}, u32[]{:S(2)}) %collective-permute-start.6) | collective-permute-done | bytes 196640 | tf_op jit(solution)/shard_map/ppermute | solution.py:31
  18.2 2.6 %collective-permute-start.7 = (bf16[192,768]{1,0:T(8,128)(2,1)S(1)}, bf16[192,768]{1,0:T(8,128)(2,1)S(1)}, u32[]{:S(2)}, u32[]{:S(2)}) collective-permute-start(bf16[192,768]{1,0:T(8,128)(2,1)S(1)} %pad_maximum_fusion.1), channel_id=1, source_target_pairs={{0,4},{1,5},{2,3},{3,2},{4,0},{5,1},{6,7},{7,6},{8,12},{9,13},{10,... | collective-permute-start | bytes 884744 | tf_op jit(solution)/shard_map/ppermute | solution.py:31
  21.5 0.1 pack.1.own_ref.refs_0_.lines_ref
  21.6 0.0 copy-start.1
  21.6 0.6 %line_norms.1.refs_4_ = f32[16,64]{1,0:T(8,128)S(1)} custom-call(bf16[1024,768]{1,0:T(8,128)(2,1)S(1)} %pack.1.own_ref.refs_0_.lines_ref), custom_call_target="tpu_custom_call" | custom-call | flops 201326592 | bytes 1572864 | tf_op jit(solution)/shard_map/line_norms/pallas_call | solution.py:46
  22.2 0.0 collective-permute-done.3.refs_2_
  22.2 0.6 %collective-permute-start.4 = (bf16[64,768]{1,0:T(8,128)(2,1)S(1)}, bf16[64,768]{1,0:T(8,128)(2,1)S(1)}, u32[]{:S(2)}, u32[]{:S(2)}) collective-permute-start(bf16[64,768]{1,0:T(8,128)(2,1)S(1)} %collective-permute-done.3.refs_2_), channel_id=1, source_target_pairs={{0,4},{1,5},{2,3},{3,2},{4,0},{5,1},{6,7},{7,6},{8,12},{9,13},{10,... | collective-permute-start | bytes 294920 | tf_op jit(solution)/shard_map/ppermute | solution.py:31
  22.9 1.3 %absorb.3 = (f32[16,1024]{1,0:T(8,128)S(1)}, f32[16,1024]{1,0:T(8,128)S(1)}) custom-call(bf16[1024,768]{1,0:T(8,128)(2,1)S(1)} %pack.1.own_ref.refs_0_.lines_ref, bf16[1024,768]{1,0:T(8,128)(2,1)S(1)} %collective-permute-done.1.partner_ref.refs_1_, bf16[64,768]{1,0:T(8,128)(2,1)S(1)} %copy-done.1, ...), custom_call_target="tpu_custom_call", output_to_operand_aliasing={{0}: (7, {}), {1}: (8, {})} | custom-call | flops 1207959552 | bytes 3866624 | tf_op jit(solution)/shard_map/absorb/pallas_call | solution.py:46
  24.1 1.3 %absorb.4 = (f32[16,1024]{1,0:T(8,128)S(1)}, f32[16,1024]{1,0:T(8,128)S(1)}) custom-call(bf16[1024,768]{1,0:T(8,128)(2,1)S(1)} %pack.1.own_ref.refs_0_.lines_ref, bf16[1024,768]{1,0:T(8,128)(2,1)S(1)} %collective-permute-done.1.partner_ref.refs_1_, bf16[64,768]{1,0:T(8,128)(2,1)S(1)} %collective-permute-done.3.refs_2_, ...), custom_call_target="tpu_custom_call", output_to_operand_aliasing={{0}: (5, {}), {1}: (6, {})} | custom-call | flops 1207959552 | bytes 3866624 | tf_op jit(solution)/shard_map/absorb/pallas_call | solution.py:46
  25.4 0.3 collective-permute-done.7.refs_2_
  25.7 0.9 %absorb.5 = (f32[16,1024]{1,0:T(8,128)S(1)}, f32[16,1024]{1,0:T(8,128)S(1)}) custom-call(bf16[1024,768]{1,0:T(8,128)(2,1)S(1)} %pack.1.own_ref.refs_0_.lines_ref, bf16[1024,768]{1,0:T(8,128)(2,1)S(1)} %collective-permute-done.1.partner_ref.refs_1_, ...), custom_call_target="tpu_custom_call", output_to_operand_aliasing={{0}: (3, {}), {1}: (4, {})} | custom-call | flops 603979776 | bytes 3571712 | tf_op jit(solution)/shard_map/absorb/pallas_call | solution.py:46
  26.7 0.2 collective-permute-done.4.refs_0_
  26.9 0.5 %collective-permute-start.11 = (f32[16,1024]{1,0:T(8,128)S(1)}, f32[16,1024]{1,0:T(8,128)S(1)}, u32[]{:S(2)}, u32[]{:S(2)}) collective-permute-start(f32[16,1024]{1,0:T(8,128)S(1)} %get-tuple-element.34), channel_id=1, source_target_pairs={{0,2},{1,3},{2,0},{3,1},{4,6},{5,7},{6,4},{7,5},{8,10},{9,11},{10,... | collective-permute-start | bytes 196616 | tf_op jit(solution)/shard_map/ppermute | solution.py:31
  27.4 0.9 %collective-permute-done.11.refs_3_ = f32[16,1024]{1,0:T(8,128)S(1)} collective-permute-done((f32[16,1024]{1,0:T(8,128)S(1)}, f32[16,1024]{1,0:T(8,128)S(1)}, u32[]{:S(2)}, u32[]{:S(2)}) %collective-permute-start.11) | collective-permute-done | bytes 65568 | tf_op jit(solution)/shard_map/ppermute | solution.py:31
  28.3 0.0 collective-permute-done.10.refs_1_
  28.3 1.2 %collective-permute-start.12 = (f32[2,8,64]{2,1,0:T(8,128)S(1)}, f32[2,8,64]{2,1,0:T(8,128)S(1)}, u32[]{:S(2)}, u32[]{:S(2)}) collective-permute-start(f32[2,8,64]{2,1,0:T(8,128)S(1)} %get-tuple-element.38), channel_id=1, source_target_pairs={{0,2},{1,3},{2,4},{3,5},{4,6},{5,7},{6,8},{7,9},{8,10},{9,11},{10,... | collective-permute-start | bytes 12296 | tf_op jit(solution)/shard_map/ppermute | solution.py:31
  29.5 0.8 %last.3 = (f32[2,8,64]{2,1,0:T(8,128)S(1)}, f32[2,8,64]{2,1,0:T(8,128)S(1)}) custom-call(s32[1,1]{1,0:T(1,128)} %bitcast.4.count_ref, s32[1,16]{1,0:T(1,128)S(1)} %bitcast.9, bf16[1024,768]{1,0:T(8,128)(2,1)S(1)} %pack.1.own_ref.refs_0_.lines_ref, bf16[64,768]{1,0:T(8,128)(2,1)S(1)} %collective-permute-done.4.refs_0_, ...), custom_call_target="tpu_custom_call", output_to_operand_aliasing={{0}: (8, {})} | custom-call | flops 201326592 | bytes 1908804 | tf_op jit(solution)/shard_map/last/pallas_call | solution.py:46
  30.3 0.1 collective-permute-start.13
  30.4 3.9 %collective-permute-done.12.arrived_ref = f32[2,8,64]{2,1,0:T(8,128)S(1)} collective-permute-done((f32[2,8,64]{2,1,0:T(8,128)S(1)}, f32[2,8,64]{2,1,0:T(8,128)S(1)}, u32[]{:S(2)}, u32[]{:S(2)}) %collective-permute-start.12) | collective-permute-done | bytes 4128 | tf_op jit(solution)/shard_map/ppermute | solution.py:31
  34.2 0.6 %final.1 = (f32[8,64]{1,0:T(8,128)}, f32[8,64]{1,0:T(8,128)}) custom-call(f32[2,8,64]{2,1,0:T(8,128)S(1)} %merged.1.placed_ref, f32[2,8,64]{2,1,0:T(8,128)S(1)} %collective-permute-done.13.arrived_ref), custom_call_target="tpu_custom_call" | custom-call | bytes 8192 | tf_op jit(solution)/shard_map/final/pallas_call | solution.py:46
  (17 shorter events, 0.1 us)
Async XLA Ops:
  0.6 20.8 %copy-start = (bf16[16,64,768]{2,1,0:T(8,128)(2,1)S(1)}, bf16[16,64,768]{2,1,0:T(8,128)(2,1)}, u32[]{:S(2)}) copy-start(bf16[16,64,768]{2,1,0:T(8,128)(2,1)} %param.4) | copy-start | bytes 4718596
  0.6 10.7 %collective-permute-start.1 = (bf16[1024,768]{1,0:T(8,128)(2,1)}, bf16[1024,768]{1,0:T(8,128)(2,1)S(1)}, u32[]{:S(2)}, u32[]{:S(2)}) collective-permute-start(bf16[1024,768]{1,0:T(8,128)(2,1)} %bitcast.6), channel_id=1, source_target_pairs={{0,2},{1,3},{2,0},{3,1},{4,6},{5,7},{6,4},{7,5},{8,10},{9,11},{10,... | collective-permute-start | bytes 4718600 | tf_op jit(solution)/shard_map/ppermute | solution.py:31
  1.2 9.5 %collective-permute-start = (bf16[64,768]{1,0:T(8,128)(2,1)}, bf16[64,768]{1,0:T(8,128)(2,1)S(1)}, u32[]{:S(2)}, u32[]{:S(2)}) collective-permute-start(bf16[64,768]{1,0:T(8,128)(2,1)} %refs_2_.1), channel_id=1, source_target_pairs={{0,16},{1,17},{2,18},{3,19},{4,20},{5,21},{6,22},{7,23},{8,24},{9,... | collective-permute-start | bytes 294920 | tf_op jit(solution)/shard_map/ppermute | solution.py:31
  4.8 6.6 %collective-permute-start.5 = (bf16[64,768]{1,0:T(8,128)(2,1)}, bf16[64,768]{1,0:T(8,128)(2,1)S(1)}, u32[]{:S(2)}, u32[]{:S(2)}) collective-permute-start(bf16[64,768]{1,0:T(8,128)(2,1)} %refs_2_.1), channel_id=1, source_target_pairs={{0,8},{1,9},{2,10},{3,11},{4,12},{5,13},{6,14},{7,15},{8,0},{9,1},... | collective-permute-start | bytes 294920 | tf_op jit(solution)/shard_map/ppermute | solution.py:31
  6.4 6.6 %collective-permute-start.8 = (bf16[64,768]{1,0:T(8,128)(2,1)}, bf16[64,768]{1,0:T(8,128)(2,1)S(1)}, u32[]{:S(2)}, u32[]{:S(2)}) collective-permute-start(bf16[64,768]{1,0:T(8,128)(2,1)} %refs_2_.1), channel_id=1, source_target_pairs={{0,1},{1,0},{2,6},{3,7},{4,5},{5,4},{6,2},{7,3},{8,9},{9,8},{10,14... | collective-permute-start | bytes 294920 | tf_op jit(solution)/shard_map/ppermute | solution.py:31
  10.6 4.8 %collective-permute-start.2 = (bf16[64,768]{1,0:T(8,128)(2,1)S(1)}, bf16[64,768]{1,0:T(8,128)(2,1)S(1)}, u32[]{:S(2)}, u32[]{:S(2)}) collective-permute-start(bf16[64,768]{1,0:T(8,128)(2,1)S(1)} %collective-permute-done.refs_5_), channel_id=1, source_target_pairs={{0,8},{1,9},{2,10},{3,11},{4,12},{5,13},{6,14},{7,15},{8,0},{9,1},... | collective-permute-start | bytes 294920 | tf_op jit(solution)/shard_map/ppermute | solution.py:31
  11.4 6.8 %collective-permute-start.6 = (bf16[128,768]{1,0:T(8,128)(2,1)S(1)}, bf16[128,768]{1,0:T(8,128)(2,1)S(1)}, u32[]{:S(2)}, u32[]{:S(2)}) collective-permute-start(bf16[128,768]{1,0:T(8,128)(2,1)S(1)} %pad_maximum_fusion.2), channel_id=1, source_target_pairs={{0,1},{1,0},{2,6},{3,7},{4,5},{5,4},{6,2},{7,3},{8,9},{9,8},{10,14... | collective-permute-start | bytes 589832 | tf_op jit(solution)/shard_map/ppermute | solution.py:31
  13.9 10.2 %collective-permute-start.9 = (bf16[256,768]{1,0:T(8,128)(2,1)S(1)}, bf16[256,768]{1,0:T(8,128)(2,1)S(1)}, u32[]{:S(2)}, u32[]{:S(2)}) collective-permute-start(bf16[256,768]{1,0:T(8,128)(2,1)S(1)} %pad_maximum_fusion), channel_id=1, source_target_pairs={{0,4},{1,5},{2,3},{3,2},{4,0},{5,1},{6,7},{7,6},{8,12},{9,13},{10,... | collective-permute-start | bytes 1179656 | tf_op jit(solution)/shard_map/ppermute | solution.py:31
  15.5 6.8 %collective-permute-start.3 = (bf16[64,768]{1,0:T(8,128)(2,1)S(1)}, bf16[64,768]{1,0:T(8,128)(2,1)S(1)}, u32[]{:S(2)}, u32[]{:S(2)}) collective-permute-start(bf16[64,768]{1,0:T(8,128)(2,1)S(1)} %collective-permute-done.2.refs_3_), channel_id=1, source_target_pairs={{0,1},{1,0},{2,6},{3,7},{4,5},{5,4},{6,2},{7,3},{8,9},{9,8},{10,14... | collective-permute-start | bytes 294920 | tf_op jit(solution)/shard_map/ppermute | solution.py:31
  18.2 7.5 %collective-permute-start.7 = (bf16[192,768]{1,0:T(8,128)(2,1)S(1)}, bf16[192,768]{1,0:T(8,128)(2,1)S(1)}, u32[]{:S(2)}, u32[]{:S(2)}) collective-permute-start(bf16[192,768]{1,0:T(8,128)(2,1)S(1)} %pad_maximum_fusion.1), channel_id=1, source_target_pairs={{0,4},{1,5},{2,3},{3,2},{4,0},{5,1},{6,7},{7,6},{8,12},{9,13},{10,... | collective-permute-start | bytes 884744 | tf_op jit(solution)/shard_map/ppermute | solution.py:31
  21.6 1.2 %copy-start.1 = (bf16[64,768]{1,0:T(8,128)(2,1)S(1)}, bf16[64,768]{1,0:T(8,128)(2,1)}, u32[]{:S(2)}) copy-start(bf16[64,768]{1,0:T(8,128)(2,1)} %refs_2_.1) | copy-start | bytes 294916
  22.2 4.6 %collective-permute-start.4 = (bf16[64,768]{1,0:T(8,128)(2,1)S(1)}, bf16[64,768]{1,0:T(8,128)(2,1)S(1)}, u32[]{:S(2)}, u32[]{:S(2)}) collective-permute-start(bf16[64,768]{1,0:T(8,128)(2,1)S(1)} %collective-permute-done.3.refs_2_), channel_id=1, source_target_pairs={{0,4},{1,5},{2,3},{3,2},{4,0},{5,1},{6,7},{7,6},{8,12},{9,13},{10,... | collective-permute-start | bytes 294920 | tf_op jit(solution)/shard_map/ppermute | solution.py:31
  25.7 2.6 %copy-start.2 = (s32[16]{0:T(128)S(1)}, s32[16]{0:T(128)}, u32[]{:S(2)}) copy-start(s32[16]{0:T(128)} %param.6) | copy-start | bytes 196
  26.9 1.4 %collective-permute-start.10 = (bf16[64,768]{1,0:T(8,128)(2,1)S(1)}, bf16[64,768]{1,0:T(8,128)(2,1)S(1)}, u32[]{:S(2)}, u32[]{:S(2)}) collective-permute-start(bf16[64,768]{1,0:T(8,128)(2,1)S(1)} %collective-permute-done.4.refs_0_), channel_id=1, source_target_pairs={{0,2},{1,3},{2,0},{3,1},{4,6},{5,7},{6,4},{7,5},{8,10},{9,11},{10,... | collective-permute-start | bytes 294920 | tf_op jit(solution)/shard_map/ppermute | solution.py:31
  26.9 1.4 %collective-permute-start.11 = (f32[16,1024]{1,0:T(8,128)S(1)}, f32[16,1024]{1,0:T(8,128)S(1)}, u32[]{:S(2)}, u32[]{:S(2)}) collective-permute-start(f32[16,1024]{1,0:T(8,128)S(1)} %get-tuple-element.34), channel_id=1, source_target_pairs={{0,2},{1,3},{2,0},{3,1},{4,6},{5,7},{6,4},{7,5},{8,10},{9,11},{10,... | collective-permute-start | bytes 196616 | tf_op jit(solution)/shard_map/ppermute | solution.py:31
  28.3 5.9 %collective-permute-start.12 = (f32[2,8,64]{2,1,0:T(8,128)S(1)}, f32[2,8,64]{2,1,0:T(8,128)S(1)}, u32[]{:S(2)}, u32[]{:S(2)}) collective-permute-start(f32[2,8,64]{2,1,0:T(8,128)S(1)} %get-tuple-element.38), channel_id=1, source_target_pairs={{0,2},{1,3},{2,4},{3,5},{4,6},{5,7},{6,8},{7,9},{8,10},{9,11},{10,... | collective-permute-start | bytes 12296 | tf_op jit(solution)/shard_map/ppermute | solution.py:31
  30.3 4.0 %collective-permute-start.13 = (f32[2,8,64]{2,1,0:T(8,128)S(1)}, f32[2,8,64]{2,1,0:T(8,128)S(1)}, u32[]{:S(2)}, u32[]{:S(2)}) collective-permute-start(f32[2,8,64]{2,1,0:T(8,128)S(1)} %get-tuple-element.39), channel_id=1, source_target_pairs={{0,2},{1,3},{2,0},{3,1},{4,6},{5,7},{6,4},{7,5},{8,10},{9,11},{10,... | collective-permute-start | bytes 12296 | tf_op jit(solution)/shard_map/ppermute | solution.py:31

commit v7 on v6

--- a/solution.py
+++ b/solution.py
@@ -171,9 +171,14 @@
             out_ref[:SUBLANES, at : at + step] = first
             out_ref[SUBLANES:, at : at + step] = second
     if give:
-        mine_ref, theirs_ref = refs[line_count:]
+        mine_ref, theirs_ref, given_ref = refs[line_count:]
         half = mine_ref.shape[1] // 2
-        theirs_ref[:, half:] = mine_ref[:, half:]
+        both = jnp.concatenate([theirs_ref[:, :half], mine_ref[:, half:]], axis=1)
+        first, second = both[:SUBLANES], both[SUBLANES:]
+        rows = SUBLANES // 2
+        first, second = join(first[:rows], second[:rows], first[rows:], second[rows:])
+        given_ref[:rows] = first
+        given_ref[rows:] = second
 
 
 def absorb(states, banks, line_sets, give=False):
@@ -182,9 +187,12 @@
     total = sum(lines.shape[0] for lines in line_sets)
     count = len(line_sets)
     operands = (*line_sets, *banks, *states)
+    outs = tuple(jax.ShapeDtypeStruct(state.shape, state.dtype) for state in states)
+    if give:
+        outs += (jax.ShapeDtypeStruct((SUBLANES, states[0].shape[1]), states[0].dtype),)
     return call(
         functools.partial(absorb_kernel, count, len(banks), give),
-        tuple(jax.ShapeDtypeStruct(state.shape, state.dtype) for state in states),
+        outs,
         operands,
         (VMEM,) * len(operands),
         2 * rows * total * features,
@@ -211,7 +219,8 @@
 
     @pl.when(lax.rem(host, 2) == parity)
     def work():
-        given = folded(returned_ref[:SUBLANES], returned_ref[SUBLANES:])
+        rows = SUBLANES // 2
+        given = folded(returned_ref[:rows], returned_ref[rows:])
         order = [*range(slots // 2), *reversed(range(slots // 2, slots))]
         for index, value in enumerate(given):
             spread(slot_ref.at[2 + index], value, order)
@@ -333,8 +342,8 @@
     corner = moved(near_last, turned)
     states = absorb(states, (centroids, near, *level, distant, near_level), lines)
     states = absorb(states, (near_beyond, *beyond, crossed_level), lines)
-    mine, theirs = absorb(states, (crossed_beyond,), lines, give=True)
-    returned = moved(theirs, partner_of)
+    mine, _, given = absorb(states, (crossed_beyond,), lines, give=True)
+    returned = moved(given, partner_of)
     corner, mine, norms = lax.optimization_barrier((corner, mine, norms))
     banks = (corner, moved(corner, partner_of))
 

time: 35 us -> 35 us (level)
  no operation moved by 1% of the time
where the time goes in v7:
time: 35 us; the launch traced here: 34.8 us
  starting transfers between devices  17.4 us (50%)
  waiting for transfers between devices  9.38 us (27%)
  Pallas kernels  5.62 us (16%)
  between operations  1.4 us (4%)
  other arithmetic  0.95 us (3%)
    ppermute x14, starting transfers between devices, moved(): return lax.ppermute(value, AXES, route)  17.4 us
    ppermute x14, waiting for transfers between devices, moved(): return lax.ppermute(value, AXES, route)  9.38 us
    pallas_call x9, Pallas kernels, call(): pl.pallas_call(body, in_specs=list(spaces), out_specs=(VMEM,) * len(outs)...  5.62 us
    concatenate x3, other arithmetic, stacked(): return jnp.concatenate(pieces, axis=0) if len(pieces) > 1 else pieces[0]  0.95 us
  transfers between devices with their start and end apart: 14, of which 6 were waited for; matrix products, arithmetic and copies ran while one was open for 3% of the time, Pallas kernels for 14%

profile of v7, /device:TPU:0, one launch (start us, length us, event | category | flops | bytes accessed | tf_op | source)
XLA Modules:
  0.0 34.8 jit_solution(10832338652525332768)
XLA Ops:
  0.6 0.5 %collective-permute-start.1 = (bf16[1024,768]{1,0:T(8,128)(2,1)}, bf16[1024,768]{1,0:T(8,128)(2,1)S(1)}, u32[]{:S(2)}, u32[]{:S(2)}) collective-permute-start(bf16[1024,768]{1,0:T(8,128)(2,1)} %bitcast.6), channel_id=1, source_target_pairs={{0,2},{1,3},{2,0},{3,1},{4,6},{5,7},{6,4},{7,5},{8,10},{9,11},{10,... | collective-permute-start | bytes 4718600 | tf_op jit(solution)/shard_map/ppermute | solution.py:31
  1.2 3.7 %collective-permute-start = (bf16[64,768]{1,0:T(8,128)(2,1)}, bf16[64,768]{1,0:T(8,128)(2,1)S(1)}, u32[]{:S(2)}, u32[]{:S(2)}) collective-permute-start(bf16[64,768]{1,0:T(8,128)(2,1)} %refs_2_.1), channel_id=1, source_target_pairs={{0,16},{1,17},{2,18},{3,19},{4,20},{5,21},{6,22},{7,23},{8,24},{9,... | collective-permute-start | bytes 294920 | tf_op jit(solution)/shard_map/ppermute | solution.py:31
  4.8 1.6 %collective-permute-start.5 = (bf16[64,768]{1,0:T(8,128)(2,1)}, bf16[64,768]{1,0:T(8,128)(2,1)S(1)}, u32[]{:S(2)}, u32[]{:S(2)}) collective-permute-start(bf16[64,768]{1,0:T(8,128)(2,1)} %refs_2_.1), channel_id=1, source_target_pairs={{0,8},{1,9},{2,10},{3,11},{4,12},{5,13},{6,14},{7,15},{8,0},{9,1},... | collective-permute-start | bytes 294920 | tf_op jit(solution)/shard_map/ppermute | solution.py:31
  6.4 1.5 %collective-permute-start.8 = (bf16[64,768]{1,0:T(8,128)(2,1)}, bf16[64,768]{1,0:T(8,128)(2,1)S(1)}, u32[]{:S(2)}, u32[]{:S(2)}) collective-permute-start(bf16[64,768]{1,0:T(8,128)(2,1)} %refs_2_.1), channel_id=1, source_target_pairs={{0,1},{1,0},{2,6},{3,7},{4,5},{5,4},{6,2},{7,3},{8,9},{9,8},{10,14... | collective-permute-start | bytes 294920 | tf_op jit(solution)/shard_map/ppermute | solution.py:31
  7.9 2.7 %collective-permute-done.refs_5_ = bf16[64,768]{1,0:T(8,128)(2,1)S(1)} collective-permute-done((bf16[64,768]{1,0:T(8,128)(2,1)}, bf16[64,768]{1,0:T(8,128)(2,1)S(1)}, u32[]{:S(2)}, u32[]{:S(2)}) %collective-permute-start) | collective-permute-done | bytes 98336 | tf_op jit(solution)/shard_map/ppermute | solution.py:31
  10.6 0.7 %collective-permute-start.2 = (bf16[64,768]{1,0:T(8,128)(2,1)S(1)}, bf16[64,768]{1,0:T(8,128)(2,1)S(1)}, u32[]{:S(2)}, u32[]{:S(2)}) collective-permute-start(bf16[64,768]{1,0:T(8,128)(2,1)S(1)} %collective-permute-done.refs_5_), channel_id=1, source_target_pairs={{0,8},{1,9},{2,10},{3,11},{4,12},{5,13},{6,14},{7,15},{8,0},{9,1},... | collective-permute-start | bytes 294920 | tf_op jit(solution)/shard_map/ppermute | solution.py:31
  11.4 1.6 %collective-permute-start.6 = (bf16[128,768]{1,0:T(8,128)(2,1)S(1)}, bf16[128,768]{1,0:T(8,128)(2,1)S(1)}, u32[]{:S(2)}, u32[]{:S(2)}) collective-permute-start(bf16[128,768]{1,0:T(8,128)(2,1)S(1)} %pad_maximum_fusion.2), channel_id=1, source_target_pairs={{0,1},{1,0},{2,6},{3,7},{4,5},{5,4},{6,2},{7,3},{8,9},{9,8},{10,14... | collective-permute-start | bytes 589832 | tf_op jit(solution)/shard_map/ppermute | solution.py:31
  13.0 0.0 collective-permute-done.8.refs_3_
  13.0 0.9 %pad_maximum_fusion = bf16[256,768]{1,0:T(8,128)(2,1)S(1)} fusion(bf16[64,768]{1,0:T(8,128)(2,1)S(1)} %collective-permute-done.refs_5_, bf16[64,768]{1,0:T(8,128)(2,1)S(1)} %collective-permute-done.5.refs_4_, bf16[64,768]{1,0:T(8,128)(2,1)S(1)} %collective-permute-done.8.refs_3_, bf16[64,768]{1,0:T(8,128)(2,1)} %refs_2_.1), kind=kLoop, calls=%fused_computation | loop fusion | flops 1572864 | bytes 786432 | tf_op jit(solution)/shard_map/concatenate | solution.py:300
  13.9 1.6 %collective-permute-start.9 = (bf16[256,768]{1,0:T(8,128)(2,1)S(1)}, bf16[256,768]{1,0:T(8,128)(2,1)S(1)}, u32[]{:S(2)}, u32[]{:S(2)}) collective-permute-start(bf16[256,768]{1,0:T(8,128)(2,1)S(1)} %pad_maximum_fusion), channel_id=1, source_target_pairs={{0,4},{1,5},{2,3},{3,2},{4,0},{5,1},{6,7},{7,6},{8,12},{9,13},{10,... | collective-permute-start | bytes 1179656 | tf_op jit(solution)/shard_map/ppermute | solution.py:31
  15.5 0.0 collective-permute-done.2.refs_3_
  15.5 1.3 %collective-permute-start.3 = (bf16[64,768]{1,0:T(8,128)(2,1)S(1)}, bf16[64,768]{1,0:T(8,128)(2,1)S(1)}, u32[]{:S(2)}, u32[]{:S(2)}) collective-permute-start(bf16[64,768]{1,0:T(8,128)(2,1)S(1)} %collective-permute-done.2.refs_3_), channel_id=1, source_target_pairs={{0,1},{1,0},{2,6},{3,7},{4,5},{5,4},{6,2},{7,3},{8,9},{9,8},{10,14... | collective-permute-start | bytes 294920 | tf_op jit(solution)/shard_map/ppermute | solution.py:31
  16.8 1.4 %collective-permute-done.6.refs_6_ = bf16[128,768]{1,0:T(8,128)(2,1)S(1)} collective-permute-done((bf16[128,768]{1,0:T(8,128)(2,1)S(1)}, bf16[128,768]{1,0:T(8,128)(2,1)S(1)}, u32[]{:S(2)}, u32[]{:S(2)}) %collective-permute-start.6) | collective-permute-done | bytes 196640 | tf_op jit(solution)/shard_map/ppermute | solution.py:31
  18.2 2.6 %collective-permute-start.7 = (bf16[192,768]{1,0:T(8,128)(2,1)S(1)}, bf16[192,768]{1,0:T(8,128)(2,1)S(1)}, u32[]{:S(2)}, u32[]{:S(2)}) collective-permute-start(bf16[192,768]{1,0:T(8,128)(2,1)S(1)} %pad_maximum_fusion.1), channel_id=1, source_target_pairs={{0,4},{1,5},{2,3},{3,2},{4,0},{5,1},{6,7},{7,6},{8,12},{9,13},{10,... | collective-permute-start | bytes 884744 | tf_op jit(solution)/shard_map/ppermute | solution.py:31
  21.5 0.1 pack.1.own_ref.refs_0_.lines_ref
  21.6 0.0 copy-start.1
  21.6 0.6 %line_norms.1.refs_4_ = f32[16,64]{1,0:T(8,128)S(1)} custom-call(bf16[1024,768]{1,0:T(8,128)(2,1)S(1)} %pack.1.own_ref.refs_0_.lines_ref), custom_call_target="tpu_custom_call" | custom-call | flops 201326592 | bytes 1572864 | tf_op jit(solution)/shard_map/line_norms/pallas_call | solution.py:46
  22.2 0.6 %collective-permute-start.4 = (bf16[64,768]{1,0:T(8,128)(2,1)S(1)}, bf16[64,768]{1,0:T(8,128)(2,1)S(1)}, u32[]{:S(2)}, u32[]{:S(2)}) collective-permute-start(bf16[64,768]{1,0:T(8,128)(2,1)S(1)} %collective-permute-done.3.refs_2_), channel_id=1, source_target_pairs={{0,4},{1,5},{2,3},{3,2},{4,0},{5,1},{6,7},{7,6},{8,12},{9,13},{10,... | collective-permute-start | bytes 294920 | tf_op jit(solution)/shard_map/ppermute | solution.py:31
  22.9 1.3 %absorb.3 = (f32[16,1024]{1,0:T(8,128)S(1)}, f32[16,1024]{1,0:T(8,128)S(1)}) custom-call(bf16[1024,768]{1,0:T(8,128)(2,1)S(1)} %pack.1.own_ref.refs_0_.lines_ref, bf16[1024,768]{1,0:T(8,128)(2,1)S(1)} %collective-permute-done.1.partner_ref.refs_1_, bf16[64,768]{1,0:T(8,128)(2,1)S(1)} %copy-done.1, ...), custom_call_target="tpu_custom_call", output_to_operand_aliasing={{0}: (7, {}), {1}: (8, {})} | custom-call | flops 1207959552 | bytes 3866624 | tf_op jit(solution)/shard_map/absorb/pallas_call | solution.py:46
  24.1 1.3 %absorb.4 = (f32[16,1024]{1,0:T(8,128)S(1)}, f32[16,1024]{1,0:T(8,128)S(1)}) custom-call(bf16[1024,768]{1,0:T(8,128)(2,1)S(1)} %pack.1.own_ref.refs_0_.lines_ref, bf16[1024,768]{1,0:T(8,128)(2,1)S(1)} %collective-permute-done.1.partner_ref.refs_1_, bf16[64,768]{1,0:T(8,128)(2,1)S(1)} %collective-permute-done.3.refs_2_, ...), custom_call_target="tpu_custom_call", output_to_operand_aliasing={{0}: (5, {}), {1}: (6, {})} | custom-call | flops 1207959552 | bytes 3866624 | tf_op jit(solution)/shard_map/absorb/pallas_call | solution.py:46
  25.4 0.3 collective-permute-done.7.refs_2_
  25.7 0.9 %absorb.5 = (f32[16,1024]{1,0:T(8,128)S(1)}, f32[16,1024]{1,0:T(8,128)S(1)}, f32[8,1024]{1,0:T(8,128)S(1)}) custom-call(bf16[1024,768]{1,0:T(8,128)(2,1)S(1)} %pack.1.own_ref.refs_0_.lines_ref, bf16[1024,768]{1,0:T(8,128)(2,1)S(1)} %collective-permute-done.1.partner_ref.refs_1_, ...), custom_call_target="tpu_custom_call", output_to_operand_aliasing={{0}: (3, {}), {1}: (4, {})} | custom-call | flops 603979776 | bytes 3571712 | tf_op jit(solution)/shard_map/absorb/pallas_call | solution.py:46
  26.7 0.2 collective-permute-done.4.refs_0_
  26.9 0.0 collective-permute-start.10
  26.9 0.5 %collective-permute-start.11 = (f32[8,1024]{1,0:T(8,128)S(1)}, f32[8,1024]{1,0:T(8,128)S(1)}, u32[]{:S(2)}, u32[]{:S(2)}) collective-permute-start(f32[8,1024]{1,0:T(8,128)S(1)} %get-tuple-element.34), channel_id=1, source_target_pairs={{0,2},{1,3},{2,0},{3,1},{4,6},{5,7},{6,4},{7,5},{8,10},{9,11},{10,... | collective-permute-start | bytes 98312 | tf_op jit(solution)/shard_map/ppermute | solution.py:31
  27.4 0.9 %collective-permute-done.11.refs_3_ = f32[8,1024]{1,0:T(8,128)S(1)} collective-permute-done((f32[8,1024]{1,0:T(8,128)S(1)}, f32[8,1024]{1,0:T(8,128)S(1)}, u32[]{:S(2)}, u32[]{:S(2)}) %collective-permute-start.11) | collective-permute-done | bytes 32800 | tf_op jit(solution)/shard_map/ppermute | solution.py:31
  28.2 0.0 collective-permute-done.10.refs_1_
  28.3 1.2 %collective-permute-start.12 = (f32[2,8,64]{2,1,0:T(8,128)S(1)}, f32[2,8,64]{2,1,0:T(8,128)S(1)}, u32[]{:S(2)}, u32[]{:S(2)}) collective-permute-start(f32[2,8,64]{2,1,0:T(8,128)S(1)} %get-tuple-element.38), channel_id=1, source_target_pairs={{0,2},{1,3},{2,4},{3,5},{4,6},{5,7},{6,8},{7,9},{8,10},{9,11},{10,... | collective-permute-start | bytes 12296 | tf_op jit(solution)/shard_map/ppermute | solution.py:31
  29.4 0.8 %last.3 = (f32[2,8,64]{2,1,0:T(8,128)S(1)}, f32[2,8,64]{2,1,0:T(8,128)S(1)}) custom-call(s32[1,1]{1,0:T(1,128)} %bitcast.4.count_ref, s32[1,16]{1,0:T(1,128)S(1)} %bitcast.9, bf16[1024,768]{1,0:T(8,128)(2,1)S(1)} %pack.1.own_ref.refs_0_.lines_ref, bf16[64,768]{1,0:T(8,128)(2,1)S(1)} %collective-permute-done.4.refs_0_, ...), custom_call_target="tpu_custom_call", output_to_operand_aliasing={{0}: (8, {})} | custom-call | flops 201326592 | bytes 1876036 | tf_op jit(solution)/shard_map/last/pallas_call | solution.py:46
  30.2 0.1 collective-permute-start.13
  30.3 3.9 %collective-permute-done.12.arrived_ref = f32[2,8,64]{2,1,0:T(8,128)S(1)} collective-permute-done((f32[2,8,64]{2,1,0:T(8,128)S(1)}, f32[2,8,64]{2,1,0:T(8,128)S(1)}, u32[]{:S(2)}, u32[]{:S(2)}) %collective-permute-start.12) | collective-permute-done | bytes 4128 | tf_op jit(solution)/shard_map/ppermute | solution.py:31
  34.2 0.6 %final.1 = (f32[8,64]{1,0:T(8,128)}, f32[8,64]{1,0:T(8,128)}) custom-call(f32[2,8,64]{2,1,0:T(8,128)S(1)} %merged.1.placed_ref, f32[2,8,64]{2,1,0:T(8,128)S(1)} %collective-permute-done.13.arrived_ref), custom_call_target="tpu_custom_call" | custom-call | bytes 8192 | tf_op jit(solution)/shard_map/final/pallas_call | solution.py:46
  (17 shorter events, 0.1 us)
Async XLA Ops:
  0.6 20.8 %copy-start = (bf16[16,64,768]{2,1,0:T(8,128)(2,1)S(1)}, bf16[16,64,768]{2,1,0:T(8,128)(2,1)}, u32[]{:S(2)}) copy-start(bf16[16,64,768]{2,1,0:T(8,128)(2,1)} %param.4) | copy-start | bytes 4718596
  0.6 10.7 %collective-permute-start.1 = (bf16[1024,768]{1,0:T(8,128)(2,1)}, bf16[1024,768]{1,0:T(8,128)(2,1)S(1)}, u32[]{:S(2)}, u32[]{:S(2)}) collective-permute-start(bf16[1024,768]{1,0:T(8,128)(2,1)} %bitcast.6), channel_id=1, source_target_pairs={{0,2},{1,3},{2,0},{3,1},{4,6},{5,7},{6,4},{7,5},{8,10},{9,11},{10,... | collective-permute-start | bytes 4718600 | tf_op jit(solution)/shard_map/ppermute | solution.py:31
  1.2 9.5 %collective-permute-start = (bf16[64,768]{1,0:T(8,128)(2,1)}, bf16[64,768]{1,0:T(8,128)(2,1)S(1)}, u32[]{:S(2)}, u32[]{:S(2)}) collective-permute-start(bf16[64,768]{1,0:T(8,128)(2,1)} %refs_2_.1), channel_id=1, source_target_pairs={{0,16},{1,17},{2,18},{3,19},{4,20},{5,21},{6,22},{7,23},{8,24},{9,... | collective-permute-start | bytes 294920 | tf_op jit(solution)/shard_map/ppermute | solution.py:31
  4.8 6.6 %collective-permute-start.5 = (bf16[64,768]{1,0:T(8,128)(2,1)}, bf16[64,768]{1,0:T(8,128)(2,1)S(1)}, u32[]{:S(2)}, u32[]{:S(2)}) collective-permute-start(bf16[64,768]{1,0:T(8,128)(2,1)} %refs_2_.1), channel_id=1, source_target_pairs={{0,8},{1,9},{2,10},{3,11},{4,12},{5,13},{6,14},{7,15},{8,0},{9,1},... | collective-permute-start | bytes 294920 | tf_op jit(solution)/shard_map/ppermute | solution.py:31
  6.4 6.6 %collective-permute-start.8 = (bf16[64,768]{1,0:T(8,128)(2,1)}, bf16[64,768]{1,0:T(8,128)(2,1)S(1)}, u32[]{:S(2)}, u32[]{:S(2)}) collective-permute-start(bf16[64,768]{1,0:T(8,128)(2,1)} %refs_2_.1), channel_id=1, source_target_pairs={{0,1},{1,0},{2,6},{3,7},{4,5},{5,4},{6,2},{7,3},{8,9},{9,8},{10,14... | collective-permute-start | bytes 294920 | tf_op jit(solution)/shard_map/ppermute | solution.py:31
  10.6 4.8 %collective-permute-start.2 = (bf16[64,768]{1,0:T(8,128)(2,1)S(1)}, bf16[64,768]{1,0:T(8,128)(2,1)S(1)}, u32[]{:S(2)}, u32[]{:S(2)}) collective-permute-start(bf16[64,768]{1,0:T(8,128)(2,1)S(1)} %collective-permute-done.refs_5_), channel_id=1, source_target_pairs={{0,8},{1,9},{2,10},{3,11},{4,12},{5,13},{6,14},{7,15},{8,0},{9,1},... | collective-permute-start | bytes 294920 | tf_op jit(solution)/shard_map/ppermute | solution.py:31
  11.4 6.8 %collective-permute-start.6 = (bf16[128,768]{1,0:T(8,128)(2,1)S(1)}, bf16[128,768]{1,0:T(8,128)(2,1)S(1)}, u32[]{:S(2)}, u32[]{:S(2)}) collective-permute-start(bf16[128,768]{1,0:T(8,128)(2,1)S(1)} %pad_maximum_fusion.2), channel_id=1, source_target_pairs={{0,1},{1,0},{2,6},{3,7},{4,5},{5,4},{6,2},{7,3},{8,9},{9,8},{10,14... | collective-permute-start | bytes 589832 | tf_op jit(solution)/shard_map/ppermute | solution.py:31
  13.9 10.2 %collective-permute-start.9 = (bf16[256,768]{1,0:T(8,128)(2,1)S(1)}, bf16[256,768]{1,0:T(8,128)(2,1)S(1)}, u32[]{:S(2)}, u32[]{:S(2)}) collective-permute-start(bf16[256,768]{1,0:T(8,128)(2,1)S(1)} %pad_maximum_fusion), channel_id=1, source_target_pairs={{0,4},{1,5},{2,3},{3,2},{4,0},{5,1},{6,7},{7,6},{8,12},{9,13},{10,... | collective-permute-start | bytes 1179656 | tf_op jit(solution)/shard_map/ppermute | solution.py:31
  15.5 6.8 %collective-permute-start.3 = (bf16[64,768]{1,0:T(8,128)(2,1)S(1)}, bf16[64,768]{1,0:T(8,128)(2,1)S(1)}, u32[]{:S(2)}, u32[]{:S(2)}) collective-permute-start(bf16[64,768]{1,0:T(8,128)(2,1)S(1)} %collective-permute-done.2.refs_3_), channel_id=1, source_target_pairs={{0,1},{1,0},{2,6},{3,7},{4,5},{5,4},{6,2},{7,3},{8,9},{9,8},{10,14... | collective-permute-start | bytes 294920 | tf_op jit(solution)/shard_map/ppermute | solution.py:31
  18.2 7.5 %collective-permute-start.7 = (bf16[192,768]{1,0:T(8,128)(2,1)S(1)}, bf16[192,768]{1,0:T(8,128)(2,1)S(1)}, u32[]{:S(2)}, u32[]{:S(2)}) collective-permute-start(bf16[192,768]{1,0:T(8,128)(2,1)S(1)} %pad_maximum_fusion.1), channel_id=1, source_target_pairs={{0,4},{1,5},{2,3},{3,2},{4,0},{5,1},{6,7},{7,6},{8,12},{9,13},{10,... | collective-permute-start | bytes 884744 | tf_op jit(solution)/shard_map/ppermute | solution.py:31
  21.6 1.2 %copy-start.1 = (bf16[64,768]{1,0:T(8,128)(2,1)S(1)}, bf16[64,768]{1,0:T(8,128)(2,1)}, u32[]{:S(2)}) copy-start(bf16[64,768]{1,0:T(8,128)(2,1)} %refs_2_.1) | copy-start | bytes 294916
  22.2 4.6 %collective-permute-start.4 = (bf16[64,768]{1,0:T(8,128)(2,1)S(1)}, bf16[64,768]{1,0:T(8,128)(2,1)S(1)}, u32[]{:S(2)}, u32[]{:S(2)}) collective-permute-start(bf16[64,768]{1,0:T(8,128)(2,1)S(1)} %collective-permute-done.3.refs_2_), channel_id=1, source_target_pairs={{0,4},{1,5},{2,3},{3,2},{4,0},{5,1},{6,7},{7,6},{8,12},{9,13},{10,... | collective-permute-start | bytes 294920 | tf_op jit(solution)/shard_map/ppermute | solution.py:31
  25.7 2.5 %copy-start.2 = (s32[16]{0:T(128)S(1)}, s32[16]{0:T(128)}, u32[]{:S(2)}) copy-start(s32[16]{0:T(128)} %param.6) | copy-start | bytes 196
  26.9 1.4 %collective-permute-start.10 = (bf16[64,768]{1,0:T(8,128)(2,1)S(1)}, bf16[64,768]{1,0:T(8,128)(2,1)S(1)}, u32[]{:S(2)}, u32[]{:S(2)}) collective-permute-start(bf16[64,768]{1,0:T(8,128)(2,1)S(1)} %collective-permute-done.4.refs_0_), channel_id=1, source_target_pairs={{0,2},{1,3},{2,0},{3,1},{4,6},{5,7},{6,4},{7,5},{8,10},{9,11},{10,... | collective-permute-start | bytes 294920 | tf_op jit(solution)/shard_map/ppermute | solution.py:31
  26.9 1.4 %collective-permute-start.11 = (f32[8,1024]{1,0:T(8,128)S(1)}, f32[8,1024]{1,0:T(8,128)S(1)}, u32[]{:S(2)}, u32[]{:S(2)}) collective-permute-start(f32[8,1024]{1,0:T(8,128)S(1)} %get-tuple-element.34), channel_id=1, source_target_pairs={{0,2},{1,3},{2,0},{3,1},{4,6},{5,7},{6,4},{7,5},{8,10},{9,11},{10,... | collective-permute-start | bytes 98312 | tf_op jit(solution)/shard_map/ppermute | solution.py:31
  28.3 5.9 %collective-permute-start.12 = (f32[2,8,64]{2,1,0:T(8,128)S(1)}, f32[2,8,64]{2,1,0:T(8,128)S(1)}, u32[]{:S(2)}, u32[]{:S(2)}) collective-permute-start(f32[2,8,64]{2,1,0:T(8,128)S(1)} %get-tuple-element.38), channel_id=1, source_target_pairs={{0,2},{1,3},{2,4},{3,5},{4,6},{5,7},{6,8},{7,9},{8,10},{9,11},{10,... | collective-permute-start | bytes 12296 | tf_op jit(solution)/shard_map/ppermute | solution.py:31
  30.2 4.0 %collective-permute-start.13 = (f32[2,8,64]{2,1,0:T(8,128)S(1)}, f32[2,8,64]{2,1,0:T(8,128)S(1)}, u32[]{:S(2)}, u32[]{:S(2)}) collective-permute-start(f32[2,8,64]{2,1,0:T(8,128)S(1)} %get-tuple-element.39), channel_id=1, source_target_pairs={{0,2},{1,3},{2,0},{3,1},{4,6},{5,7},{6,4},{7,5},{8,10},{9,11},{10,... | collective-permute-start | bytes 12296 | tf_op jit(solution)/shard_map/ppermute | solution.py:31

commit v8 on v6

--- a/solution.py
+++ b/solution.py
@@ -335,7 +335,7 @@
     states = absorb(states, (near_beyond, *beyond, crossed_level), lines)
     mine, theirs = absorb(states, (crossed_beyond,), lines, give=True)
     returned = moved(theirs, partner_of)
-    corner, mine, norms = lax.optimization_barrier((corner, mine, norms))
+    corner, mine = lax.optimization_barrier((corner, mine))
     banks = (corner, moved(corner, partner_of))
 
     placed = jnp.zeros((2, places, sub_rows), jnp.float32)

time: 35 us -> 35 us (level)
  no operation moved by 1% of the time
where the time goes in v8:
time: 35 us; the launch traced here: 34.9 us
  starting transfers between devices  17.4 us (50%)
  waiting for transfers between devices  9.43 us (27%)
  Pallas kernels  5.61 us (16%)
  between operations  1.4 us (4%)
  other arithmetic  0.95 us (3%)
    ppermute x14, starting transfers between devices, moved(): return lax.ppermute(value, AXES, route)  17.4 us
    ppermute x14, waiting for transfers between devices, moved(): return lax.ppermute(value, AXES, route)  9.43 us
    pallas_call x9, Pallas kernels, call(): pl.pallas_call(body, in_specs=list(spaces), out_specs=(VMEM,) * len(outs)...  5.61 us
    concatenate x3, other arithmetic, stacked(): return jnp.concatenate(pieces, axis=0) if len(pieces) > 1 else pieces[0]  0.95 us
  transfers between devices with their start and end apart: 14, of which 6 were waited for; matrix products, arithmetic and copies ran while one was open for 3% of the time, Pallas kernels for 14%

profile of v8, /device:TPU:0, one launch (start us, length us, event | category | flops | bytes accessed | tf_op | source)
XLA Modules:
  0.0 34.9 jit_solution(4119406303226346993)
XLA Ops:
  0.6 0.5 %collective-permute-start.1 = (bf16[1024,768]{1,0:T(8,128)(2,1)}, bf16[1024,768]{1,0:T(8,128)(2,1)S(1)}, u32[]{:S(2)}, u32[]{:S(2)}) collective-permute-start(bf16[1024,768]{1,0:T(8,128)(2,1)} %bitcast.6), channel_id=1, source_target_pairs={{0,2},{1,3},{2,0},{3,1},{4,6},{5,7},{6,4},{7,5},{8,10},{9,11},{10,... | collective-permute-start | bytes 4718600 | tf_op jit(solution)/shard_map/ppermute | solution.py:31
  1.2 3.7 %collective-permute-start = (bf16[64,768]{1,0:T(8,128)(2,1)}, bf16[64,768]{1,0:T(8,128)(2,1)S(1)}, u32[]{:S(2)}, u32[]{:S(2)}) collective-permute-start(bf16[64,768]{1,0:T(8,128)(2,1)} %refs_2_.1), channel_id=1, source_target_pairs={{0,16},{1,17},{2,18},{3,19},{4,20},{5,21},{6,22},{7,23},{8,24},{9,... | collective-permute-start | bytes 294920 | tf_op jit(solution)/shard_map/ppermute | solution.py:31
  4.8 1.6 %collective-permute-start.5 = (bf16[64,768]{1,0:T(8,128)(2,1)}, bf16[64,768]{1,0:T(8,128)(2,1)S(1)}, u32[]{:S(2)}, u32[]{:S(2)}) collective-permute-start(bf16[64,768]{1,0:T(8,128)(2,1)} %refs_2_.1), channel_id=1, source_target_pairs={{0,8},{1,9},{2,10},{3,11},{4,12},{5,13},{6,14},{7,15},{8,0},{9,1},... | collective-permute-start | bytes 294920 | tf_op jit(solution)/shard_map/ppermute | solution.py:31
  6.4 1.5 %collective-permute-start.8 = (bf16[64,768]{1,0:T(8,128)(2,1)}, bf16[64,768]{1,0:T(8,128)(2,1)S(1)}, u32[]{:S(2)}, u32[]{:S(2)}) collective-permute-start(bf16[64,768]{1,0:T(8,128)(2,1)} %refs_2_.1), channel_id=1, source_target_pairs={{0,1},{1,0},{2,6},{3,7},{4,5},{5,4},{6,2},{7,3},{8,9},{9,8},{10,14... | collective-permute-start | bytes 294920 | tf_op jit(solution)/shard_map/ppermute | solution.py:31
  7.9 2.7 %collective-permute-done.refs_5_ = bf16[64,768]{1,0:T(8,128)(2,1)S(1)} collective-permute-done((bf16[64,768]{1,0:T(8,128)(2,1)}, bf16[64,768]{1,0:T(8,128)(2,1)S(1)}, u32[]{:S(2)}, u32[]{:S(2)}) %collective-permute-start) | collective-permute-done | bytes 98336 | tf_op jit(solution)/shard_map/ppermute | solution.py:31
  10.6 0.7 %collective-permute-start.2 = (bf16[64,768]{1,0:T(8,128)(2,1)S(1)}, bf16[64,768]{1,0:T(8,128)(2,1)S(1)}, u32[]{:S(2)}, u32[]{:S(2)}) collective-permute-start(bf16[64,768]{1,0:T(8,128)(2,1)S(1)} %collective-permute-done.refs_5_), channel_id=1, source_target_pairs={{0,8},{1,9},{2,10},{3,11},{4,12},{5,13},{6,14},{7,15},{8,0},{9,1},... | collective-permute-start | bytes 294920 | tf_op jit(solution)/shard_map/ppermute | solution.py:31
  11.4 0.0 collective-permute-done.5.refs_4_
  11.4 1.6 %collective-permute-start.6 = (bf16[128,768]{1,0:T(8,128)(2,1)S(1)}, bf16[128,768]{1,0:T(8,128)(2,1)S(1)}, u32[]{:S(2)}, u32[]{:S(2)}) collective-permute-start(bf16[128,768]{1,0:T(8,128)(2,1)S(1)} %pad_maximum_fusion.2), channel_id=1, source_target_pairs={{0,1},{1,0},{2,6},{3,7},{4,5},{5,4},{6,2},{7,3},{8,9},{9,8},{10,14... | collective-permute-start | bytes 589832 | tf_op jit(solution)/shard_map/ppermute | solution.py:31
  13.0 0.0 collective-permute-done.8.refs_3_
  13.0 0.9 %pad_maximum_fusion = bf16[256,768]{1,0:T(8,128)(2,1)S(1)} fusion(bf16[64,768]{1,0:T(8,128)(2,1)S(1)} %collective-permute-done.refs_5_, bf16[64,768]{1,0:T(8,128)(2,1)S(1)} %collective-permute-done.5.refs_4_, bf16[64,768]{1,0:T(8,128)(2,1)S(1)} %collective-permute-done.8.refs_3_, bf16[64,768]{1,0:T(8,128)(2,1)} %refs_2_.1), kind=kLoop, calls=%fused_computation | loop fusion | flops 1572864 | bytes 786432 | tf_op jit(solution)/shard_map/concatenate | solution.py:291
  13.9 1.6 %collective-permute-start.9 = (bf16[256,768]{1,0:T(8,128)(2,1)S(1)}, bf16[256,768]{1,0:T(8,128)(2,1)S(1)}, u32[]{:S(2)}, u32[]{:S(2)}) collective-permute-start(bf16[256,768]{1,0:T(8,128)(2,1)S(1)} %pad_maximum_fusion), channel_id=1, source_target_pairs={{0,4},{1,5},{2,3},{3,2},{4,0},{5,1},{6,7},{7,6},{8,12},{9,13},{10,... | collective-permute-start | bytes 1179656 | tf_op jit(solution)/shard_map/ppermute | solution.py:31
  15.5 1.3 %collective-permute-start.3 = (bf16[64,768]{1,0:T(8,128)(2,1)S(1)}, bf16[64,768]{1,0:T(8,128)(2,1)S(1)}, u32[]{:S(2)}, u32[]{:S(2)}) collective-permute-start(bf16[64,768]{1,0:T(8,128)(2,1)S(1)} %collective-permute-done.2.refs_3_), channel_id=1, source_target_pairs={{0,1},{1,0},{2,6},{3,7},{4,5},{5,4},{6,2},{7,3},{8,9},{9,8},{10,14... | collective-permute-start | bytes 294920 | tf_op jit(solution)/shard_map/ppermute | solution.py:31
  16.8 1.4 %collective-permute-done.6.refs_6_ = bf16[128,768]{1,0:T(8,128)(2,1)S(1)} collective-permute-done((bf16[128,768]{1,0:T(8,128)(2,1)S(1)}, bf16[128,768]{1,0:T(8,128)(2,1)S(1)}, u32[]{:S(2)}, u32[]{:S(2)}) %collective-permute-start.6) | collective-permute-done | bytes 196640 | tf_op jit(solution)/shard_map/ppermute | solution.py:31
  18.2 2.6 %collective-permute-start.7 = (bf16[192,768]{1,0:T(8,128)(2,1)S(1)}, bf16[192,768]{1,0:T(8,128)(2,1)S(1)}, u32[]{:S(2)}, u32[]{:S(2)}) collective-permute-start(bf16[192,768]{1,0:T(8,128)(2,1)S(1)} %pad_maximum_fusion.1), channel_id=1, source_target_pairs={{0,4},{1,5},{2,3},{3,2},{4,0},{5,1},{6,7},{7,6},{8,12},{9,13},{10,... | collective-permute-start | bytes 884744 | tf_op jit(solution)/shard_map/ppermute | solution.py:31
  21.5 0.1 pack.1.own_ref.refs_0_.lines_ref
  21.6 0.0 copy-start.1
  21.6 0.6 %line_norms.1.refs_4_ = f32[16,64]{1,0:T(8,128)S(1)} custom-call(bf16[1024,768]{1,0:T(8,128)(2,1)S(1)} %pack.1.own_ref.refs_0_.lines_ref), custom_call_target="tpu_custom_call" | custom-call | flops 201326592 | bytes 1572864 | tf_op jit(solution)/shard_map/line_norms/pallas_call | solution.py:46
  22.2 0.0 collective-permute-done.3.refs_2_
  22.2 0.6 %collective-permute-start.4 = (bf16[64,768]{1,0:T(8,128)(2,1)S(1)}, bf16[64,768]{1,0:T(8,128)(2,1)S(1)}, u32[]{:S(2)}, u32[]{:S(2)}) collective-permute-start(bf16[64,768]{1,0:T(8,128)(2,1)S(1)} %collective-permute-done.3.refs_2_), channel_id=1, source_target_pairs={{0,4},{1,5},{2,3},{3,2},{4,0},{5,1},{6,7},{7,6},{8,12},{9,13},{10,... | collective-permute-start | bytes 294920 | tf_op jit(solution)/shard_map/ppermute | solution.py:31
  22.9 1.3 %absorb.3 = (f32[16,1024]{1,0:T(8,128)S(1)}, f32[16,1024]{1,0:T(8,128)S(1)}) custom-call(bf16[1024,768]{1,0:T(8,128)(2,1)S(1)} %pack.1.own_ref.refs_0_.lines_ref, bf16[1024,768]{1,0:T(8,128)(2,1)S(1)} %collective-permute-done.1.partner_ref.refs_1_, bf16[64,768]{1,0:T(8,128)(2,1)S(1)} %copy-done.1, ...), custom_call_target="tpu_custom_call", output_to_operand_aliasing={{0}: (7, {}), {1}: (8, {})} | custom-call | flops 1207959552 | bytes 3866624 | tf_op jit(solution)/shard_map/absorb/pallas_call | solution.py:46
  24.1 1.3 %absorb.4 = (f32[16,1024]{1,0:T(8,128)S(1)}, f32[16,1024]{1,0:T(8,128)S(1)}) custom-call(bf16[1024,768]{1,0:T(8,128)(2,1)S(1)} %pack.1.own_ref.refs_0_.lines_ref, bf16[1024,768]{1,0:T(8,128)(2,1)S(1)} %collective-permute-done.1.partner_ref.refs_1_, bf16[64,768]{1,0:T(8,128)(2,1)S(1)} %collective-permute-done.3.refs_2_, ...), custom_call_target="tpu_custom_call", output_to_operand_aliasing={{0}: (5, {}), {1}: (6, {})} | custom-call | flops 1207959552 | bytes 3866624 | tf_op jit(solution)/shard_map/absorb/pallas_call | solution.py:46
  25.4 0.3 collective-permute-done.7.refs_2_
  25.7 0.9 %absorb.5 = (f32[16,1024]{1,0:T(8,128)S(1)}, f32[16,1024]{1,0:T(8,128)S(1)}) custom-call(bf16[1024,768]{1,0:T(8,128)(2,1)S(1)} %pack.1.own_ref.refs_0_.lines_ref, bf16[1024,768]{1,0:T(8,128)(2,1)S(1)} %collective-permute-done.1.partner_ref.refs_1_, ...), custom_call_target="tpu_custom_call", output_to_operand_aliasing={{0}: (3, {}), {1}: (4, {})} | custom-call | flops 603979776 | bytes 3571712 | tf_op jit(solution)/shard_map/absorb/pallas_call | solution.py:46
  26.7 0.2 collective-permute-done.4.refs_0_
  26.9 0.5 %collective-permute-start.11 = (f32[16,1024]{1,0:T(8,128)S(1)}, f32[16,1024]{1,0:T(8,128)S(1)}, u32[]{:S(2)}, u32[]{:S(2)}) collective-permute-start(f32[16,1024]{1,0:T(8,128)S(1)} %get-tuple-element.32), channel_id=1, source_target_pairs={{0,2},{1,3},{2,0},{3,1},{4,6},{5,7},{6,4},{7,5},{8,10},{9,11},{10,... | collective-permute-start | bytes 196616 | tf_op jit(solution)/shard_map/ppermute | solution.py:31
  27.4 0.9 %collective-permute-done.11.refs_3_ = f32[16,1024]{1,0:T(8,128)S(1)} collective-permute-done((f32[16,1024]{1,0:T(8,128)S(1)}, f32[16,1024]{1,0:T(8,128)S(1)}, u32[]{:S(2)}, u32[]{:S(2)}) %collective-permute-start.11) | collective-permute-done | bytes 65568 | tf_op jit(solution)/shard_map/ppermute | solution.py:31
  28.3 0.0 collective-permute-done.10.refs_1_
  28.3 1.2 %collective-permute-start.12 = (f32[2,8,64]{2,1,0:T(8,128)S(1)}, f32[2,8,64]{2,1,0:T(8,128)S(1)}, u32[]{:S(2)}, u32[]{:S(2)}) collective-permute-start(f32[2,8,64]{2,1,0:T(8,128)S(1)} %get-tuple-element.36), channel_id=1, source_target_pairs={{0,2},{1,3},{2,4},{3,5},{4,6},{5,7},{6,8},{7,9},{8,10},{9,11},{10,... | collective-permute-start | bytes 12296 | tf_op jit(solution)/shard_map/ppermute | solution.py:31
  29.5 0.8 %last.3 = (f32[2,8,64]{2,1,0:T(8,128)S(1)}, f32[2,8,64]{2,1,0:T(8,128)S(1)}) custom-call(s32[1,1]{1,0:T(1,128)} %bitcast.4.count_ref, s32[1,16]{1,0:T(1,128)S(1)} %bitcast.9, bf16[1024,768]{1,0:T(8,128)(2,1)S(1)} %pack.1.own_ref.refs_0_.lines_ref, bf16[64,768]{1,0:T(8,128)(2,1)S(1)} %collective-permute-done.4.refs_0_, ...), custom_call_target="tpu_custom_call", output_to_operand_aliasing={{0}: (8, {})} | custom-call | flops 201326592 | bytes 1908804 | tf_op jit(solution)/shard_map/last/pallas_call | solution.py:46
  30.3 0.1 collective-permute-start.13
  30.4 3.9 %collective-permute-done.12.arrived_ref = f32[2,8,64]{2,1,0:T(8,128)S(1)} collective-permute-done((f32[2,8,64]{2,1,0:T(8,128)S(1)}, f32[2,8,64]{2,1,0:T(8,128)S(1)}, u32[]{:S(2)}, u32[]{:S(2)}) %collective-permute-start.12) | collective-permute-done | bytes 4128 | tf_op jit(solution)/shard_map/ppermute | solution.py:31
  34.2 0.6 %final.1 = (f32[8,64]{1,0:T(8,128)}, f32[8,64]{1,0:T(8,128)}) custom-call(f32[2,8,64]{2,1,0:T(8,128)S(1)} %merged.1.placed_ref, f32[2,8,64]{2,1,0:T(8,128)S(1)} %collective-permute-done.13.arrived_ref), custom_call_target="tpu_custom_call" | custom-call | bytes 8192 | tf_op jit(solution)/shard_map/final/pallas_call | solution.py:46
  (17 shorter events, 0.1 us)
Async XLA Ops:
  0.6 20.8 %copy-start = (bf16[16,64,768]{2,1,0:T(8,128)(2,1)S(1)}, bf16[16,64,768]{2,1,0:T(8,128)(2,1)}, u32[]{:S(2)}) copy-start(bf16[16,64,768]{2,1,0:T(8,128)(2,1)} %param.4) | copy-start | bytes 4718596
  0.6 10.7 %collective-permute-start.1 = (bf16[1024,768]{1,0:T(8,128)(2,1)}, bf16[1024,768]{1,0:T(8,128)(2,1)S(1)}, u32[]{:S(2)}, u32[]{:S(2)}) collective-permute-start(bf16[1024,768]{1,0:T(8,128)(2,1)} %bitcast.6), channel_id=1, source_target_pairs={{0,2},{1,3},{2,0},{3,1},{4,6},{5,7},{6,4},{7,5},{8,10},{9,11},{10,... | collective-permute-start | bytes 4718600 | tf_op jit(solution)/shard_map/ppermute | solution.py:31
  1.2 9.5 %collective-permute-start = (bf16[64,768]{1,0:T(8,128)(2,1)}, bf16[64,768]{1,0:T(8,128)(2,1)S(1)}, u32[]{:S(2)}, u32[]{:S(2)}) collective-permute-start(bf16[64,768]{1,0:T(8,128)(2,1)} %refs_2_.1), channel_id=1, source_target_pairs={{0,16},{1,17},{2,18},{3,19},{4,20},{5,21},{6,22},{7,23},{8,24},{9,... | collective-permute-start | bytes 294920 | tf_op jit(solution)/shard_map/ppermute | solution.py:31
  4.8 6.6 %collective-permute-start.5 = (bf16[64,768]{1,0:T(8,128)(2,1)}, bf16[64,768]{1,0:T(8,128)(2,1)S(1)}, u32[]{:S(2)}, u32[]{:S(2)}) collective-permute-start(bf16[64,768]{1,0:T(8,128)(2,1)} %refs_2_.1), channel_id=1, source_target_pairs={{0,8},{1,9},{2,10},{3,11},{4,12},{5,13},{6,14},{7,15},{8,0},{9,1},... | collective-permute-start | bytes 294920 | tf_op jit(solution)/shard_map/ppermute | solution.py:31
  6.4 6.6 %collective-permute-start.8 = (bf16[64,768]{1,0:T(8,128)(2,1)}, bf16[64,768]{1,0:T(8,128)(2,1)S(1)}, u32[]{:S(2)}, u32[]{:S(2)}) collective-permute-start(bf16[64,768]{1,0:T(8,128)(2,1)} %refs_2_.1), channel_id=1, source_target_pairs={{0,1},{1,0},{2,6},{3,7},{4,5},{5,4},{6,2},{7,3},{8,9},{9,8},{10,14... | collective-permute-start | bytes 294920 | tf_op jit(solution)/shard_map/ppermute | solution.py:31
  10.6 4.8 %collective-permute-start.2 = (bf16[64,768]{1,0:T(8,128)(2,1)S(1)}, bf16[64,768]{1,0:T(8,128)(2,1)S(1)}, u32[]{:S(2)}, u32[]{:S(2)}) collective-permute-start(bf16[64,768]{1,0:T(8,128)(2,1)S(1)} %collective-permute-done.refs_5_), channel_id=1, source_target_pairs={{0,8},{1,9},{2,10},{3,11},{4,12},{5,13},{6,14},{7,15},{8,0},{9,1},... | collective-permute-start | bytes 294920 | tf_op jit(solution)/shard_map/ppermute | solution.py:31
  11.4 6.8 %collective-permute-start.6 = (bf16[128,768]{1,0:T(8,128)(2,1)S(1)}, bf16[128,768]{1,0:T(8,128)(2,1)S(1)}, u32[]{:S(2)}, u32[]{:S(2)}) collective-permute-start(bf16[128,768]{1,0:T(8,128)(2,1)S(1)} %pad_maximum_fusion.2), channel_id=1, source_target_pairs={{0,1},{1,0},{2,6},{3,7},{4,5},{5,4},{6,2},{7,3},{8,9},{9,8},{10,14... | collective-permute-start | bytes 589832 | tf_op jit(solution)/shard_map/ppermute | solution.py:31
  13.9 10.2 %collective-permute-start.9 = (bf16[256,768]{1,0:T(8,128)(2,1)S(1)}, bf16[256,768]{1,0:T(8,128)(2,1)S(1)}, u32[]{:S(2)}, u32[]{:S(2)}) collective-permute-start(bf16[256,768]{1,0:T(8,128)(2,1)S(1)} %pad_maximum_fusion), channel_id=1, source_target_pairs={{0,4},{1,5},{2,3},{3,2},{4,0},{5,1},{6,7},{7,6},{8,12},{9,13},{10,... | collective-permute-start | bytes 1179656 | tf_op jit(solution)/shard_map/ppermute | solution.py:31
  15.5 6.8 %collective-permute-start.3 = (bf16[64,768]{1,0:T(8,128)(2,1)S(1)}, bf16[64,768]{1,0:T(8,128)(2,1)S(1)}, u32[]{:S(2)}, u32[]{:S(2)}) collective-permute-start(bf16[64,768]{1,0:T(8,128)(2,1)S(1)} %collective-permute-done.2.refs_3_), channel_id=1, source_target_pairs={{0,1},{1,0},{2,6},{3,7},{4,5},{5,4},{6,2},{7,3},{8,9},{9,8},{10,14... | collective-permute-start | bytes 294920 | tf_op jit(solution)/shard_map/ppermute | solution.py:31
  18.2 7.5 %collective-permute-start.7 = (bf16[192,768]{1,0:T(8,128)(2,1)S(1)}, bf16[192,768]{1,0:T(8,128)(2,1)S(1)}, u32[]{:S(2)}, u32[]{:S(2)}) collective-permute-start(bf16[192,768]{1,0:T(8,128)(2,1)S(1)} %pad_maximum_fusion.1), channel_id=1, source_target_pairs={{0,4},{1,5},{2,3},{3,2},{4,0},{5,1},{6,7},{7,6},{8,12},{9,13},{10,... | collective-permute-start | bytes 884744 | tf_op jit(solution)/shard_map/ppermute | solution.py:31
  21.6 1.2 %copy-start.1 = (bf16[64,768]{1,0:T(8,128)(2,1)S(1)}, bf16[64,768]{1,0:T(8,128)(2,1)}, u32[]{:S(2)}) copy-start(bf16[64,768]{1,0:T(8,128)(2,1)} %refs_2_.1) | copy-start | bytes 294916
  22.2 4.6 %collective-permute-start.4 = (bf16[64,768]{1,0:T(8,128)(2,1)S(1)}, bf16[64,768]{1,0:T(8,128)(2,1)S(1)}, u32[]{:S(2)}, u32[]{:S(2)}) collective-permute-start(bf16[64,768]{1,0:T(8,128)(2,1)S(1)} %collective-permute-done.3.refs_2_), channel_id=1, source_target_pairs={{0,4},{1,5},{2,3},{3,2},{4,0},{5,1},{6,7},{7,6},{8,12},{9,13},{10,... | collective-permute-start | bytes 294920 | tf_op jit(solution)/shard_map/ppermute | solution.py:31
  25.7 2.6 %copy-start.2 = (s32[16]{0:T(128)S(1)}, s32[16]{0:T(128)}, u32[]{:S(2)}) copy-start(s32[16]{0:T(128)} %param.6) | copy-start | bytes 196
  26.9 1.4 %collective-permute-start.10 = (bf16[64,768]{1,0:T(8,128)(2,1)S(1)}, bf16[64,768]{1,0:T(8,128)(2,1)S(1)}, u32[]{:S(2)}, u32[]{:S(2)}) collective-permute-start(bf16[64,768]{1,0:T(8,128)(2,1)S(1)} %collective-permute-done.4.refs_0_), channel_id=1, source_target_pairs={{0,2},{1,3},{2,0},{3,1},{4,6},{5,7},{6,4},{7,5},{8,10},{9,11},{10,... | collective-permute-start | bytes 294920 | tf_op jit(solution)/shard_map/ppermute | solution.py:31
  26.9 1.4 %collective-permute-start.11 = (f32[16,1024]{1,0:T(8,128)S(1)}, f32[16,1024]{1,0:T(8,128)S(1)}, u32[]{:S(2)}, u32[]{:S(2)}) collective-permute-start(f32[16,1024]{1,0:T(8,128)S(1)} %get-tuple-element.32), channel_id=1, source_target_pairs={{0,2},{1,3},{2,0},{3,1},{4,6},{5,7},{6,4},{7,5},{8,10},{9,11},{10,... | collective-permute-start | bytes 196616 | tf_op jit(solution)/shard_map/ppermute | solution.py:31
  28.3 5.9 %collective-permute-start.12 = (f32[2,8,64]{2,1,0:T(8,128)S(1)}, f32[2,8,64]{2,1,0:T(8,128)S(1)}, u32[]{:S(2)}, u32[]{:S(2)}) collective-permute-start(f32[2,8,64]{2,1,0:T(8,128)S(1)} %get-tuple-element.36), channel_id=1, source_target_pairs={{0,2},{1,3},{2,4},{3,5},{4,6},{5,7},{6,8},{7,9},{8,10},{9,11},{10,... | collective-permute-start | bytes 12296 | tf_op jit(solution)/shard_map/ppermute | solution.py:31
  30.3 4.0 %collective-permute-start.13 = (f32[2,8,64]{2,1,0:T(8,128)S(1)}, f32[2,8,64]{2,1,0:T(8,128)S(1)}, u32[]{:S(2)}, u32[]{:S(2)}) collective-permute-start(f32[2,8,64]{2,1,0:T(8,128)S(1)} %get-tuple-element.37), channel_id=1, source_target_pairs={{0,2},{1,3},{2,0},{3,1},{4,6},{5,7},{6,4},{7,5},{8,10},{9,11},{10,... | collective-permute-start | bytes 12296 | tf_op jit(solution)/shard_map/ppermute | solution.py:31
